TPU v7x, 32 devices: a whole 2x2x4 slice. The times are simulated.
32 devices in a mesh: slot: 2 (over core), ctx: 4 (over y, x), uly: 4 (over z).
Axes of the slice: x: 2, y: 2, z: 4, core: 2. Of those that a mesh axis runs over, the one named last changes fastest.
Arguments:
- tokens: bfloat16 [2, 2048, 2048], P('slot', ('ctx', 'uly')), may hold values from -6 to 6
- segment_ids: int32 [2, 2048], P('slot', ('ctx', 'uly')), may hold values from 0 to 1, as said below
- qkv_weight: bfloat16 [3, 2048, 2048], P(None, ('slot', 'ctx'), 'uly'), may hold values from -0.125 to 0.125
- out_weight: bfloat16 [2048, 2048], P('uly', ('slot', 'ctx')), may hold values from -0.125 to 0.125
- gate_up: bfloat16 [2, 2048, 8192], P(None, ('slot', 'ctx'), 'uly'), may hold values from -0.125 to 0.125
- down_weight: bfloat16 [8192, 2048], P('uly', ('slot', 'ctx')), may hold values from -0.0625 to 0.0625
- qk_gain: float32 [2, 2048], P(None, 'uly'), may hold values from 0.1 to 1.9
- post_gain: float32 [2, 2048], replicated, may hold values from 0.1 to 1.9
- cotangent: bfloat16 [2, 2048, 2048], P('slot', ('ctx', 'uly')), may hold values from -6 to 6
Outputs:
- block_out: bfloat16 [2, 2048, 2048], P('slot', ('ctx', 'uly'))
- input_grad: bfloat16 [2, 2048, 2048], P('slot', ('ctx', 'uly'))
- qkv_grad: float32 [3, 2048, 2048], P(None, ('slot', 'ctx'), 'uly')
- out_grad: float32 [2048, 2048], P('uly', ('slot', 'ctx'))
- gate_up_grad: float32 [2, 2048, 8192], P(None, ('slot', 'ctx'), 'uly')
- down_grad: float32 [8192, 2048], P('uly', ('slot', 'ctx'))
- gain_grad: float32 [4, 2048], P(None, ('slot', 'ctx'))
Inputs may be any that keep to these rules, and one draw needn't show every extreme that they name: `segment_ids`: in each slot the ids never fall: all 0 (one sequence), or 0 up to a boundary of the slot's own and 1 from there on (two sequences), the boundary lying between 512 and 1536. One slot, drawn from the seed, holds one sequence; every other slot holds two.
All inputs are finite; a program needn't handle non-finite values.
Results may differ from a plain program's by a relative error of at most 0.025.
Values may be sent and summed in bfloat16 or wider, within the bound.
A program may use at most 192 MiB of HBM per device.

v0:
```python
import jax
import jax.numpy as jnp
from jax import lax
from jax.sharding import PartitionSpec as P

HEAD_DIM = 128


epsilon = 1e-06
rope_base = 500000.0
floor_value = -1e30


def rotate(values, positions, direction):
    half = values.shape[-1] // 2
    freqs = rope_base ** (-(jnp.arange(half, dtype=jnp.float32) * 2.0 / values.shape[-1]))
    angles = positions.astype(jnp.float32)[:, None] * freqs[None, :]
    cosine = jnp.cos(angles)[:, None, :]
    sine = jnp.sin(angles)[:, None, :]
    first = values[..., :half]
    second = values[..., half:]
    return jnp.concatenate(
        [first * cosine - direction * second * sine, second * cosine + direction * first * sine],
        axis=-1,
    )


def inverse_rms(values):
    return lax.rsqrt(jnp.mean(values * values, axis=-1, keepdims=True) + epsilon)


def norm_back(values, inverse, grad_scaled, width):
    return inverse * grad_scaled - values * inverse**3 * (
        jnp.sum(values * grad_scaled, axis=-1, keepdims=True) / width
    )


def allowed(query_pos, key_pos, query_seg, key_seg):
    return (key_pos[None, :] <= query_pos[:, None]) & (key_seg[None, :] == query_seg[:, None])


def share_keys(key_low, value_low, seg_low):
    return (
        lax.all_gather(key_low, "ctx", axis=0, tiled=True),
        lax.all_gather(value_low, "ctx", axis=0, tiled=True),
        lax.all_gather(seg_low, "ctx", axis=0, tiled=True),
    )


def on_device(
    tokens, segment_ids, qkv_weight, out_weight, gate_up, down_weight, qk_gain, post_gain, cotangent
):
    x_rows = tokens[0]
    width = x_rows.shape[1]
    qkv_cols, out_rows, gate_cols, down_rows = (
        lax.all_gather(qkv_weight, ("slot", "ctx"), axis=1, tiled=True),
        lax.all_gather(out_weight, ("slot", "ctx"), axis=1, tiled=True),
        lax.all_gather(gate_up, ("slot", "ctx"), axis=1, tiled=True),
        lax.all_gather(down_weight, ("slot", "ctx"), axis=1, tiled=True),
    )
    group_x, group_seg = (
        lax.all_gather(x_rows, "uly", axis=0, tiled=True),
        lax.all_gather(segment_ids[0].astype(jnp.bfloat16), "uly", axis=0, tiled=True),
    )
    span = group_x.shape[0]
    local_cols = qkv_cols.shape[2]
    heads_here = local_cols // HEAD_DIM
    scale = HEAD_DIM ** (-0.5)
    projected = jnp.einsum("td,cde->cte", group_x, qkv_cols, preferred_element_type=jnp.float32)
    square_sums = jnp.sum(projected[:2] * projected[:2], axis=-1)
    totals = lax.psum(square_sums, "uly")
    inverse_qk = lax.rsqrt(totals / width + epsilon)[:, :, None]
    scaled_in = projected[:2] * inverse_qk
    normed = scaled_in * qk_gain[:, None, :]
    positions = lax.axis_index("ctx") * span + jnp.arange(span, dtype=jnp.int32)
    rotated = rotate(normed.reshape(2, span, heads_here, HEAD_DIM), positions, 1.0)
    query_low = rotated[0].astype(jnp.bfloat16)
    key_low = rotated[1].astype(jnp.bfloat16)
    value_low = projected[2].reshape(span, heads_here, HEAD_DIM).astype(jnp.bfloat16)
    keys_all, values_all, segs_all = share_keys(key_low, value_low, group_seg)
    blocks = keys_all.shape[0] // span
    local_pos = jnp.arange(span, dtype=jnp.int32)
    block_ids = jnp.arange(blocks, dtype=jnp.int32)

    def forward_block(carry, block):
        run_max, run_sum, accum = carry
        key_block, value_block, seg_block, number = block
        mask = allowed(positions, number * span + local_pos, group_seg, seg_block)
        scores = (
            jnp.einsum("qhd,khd->hqk", query_low, key_block, preferred_element_type=jnp.float32)
            * scale
        )
        scores = jnp.where(mask[None], scores, floor_value)
        new_max = jnp.maximum(run_max, jnp.max(scores, axis=-1))
        factor = jnp.exp(run_max - new_max)
        weights = jnp.where(mask[None], jnp.exp(scores - new_max[:, :, None]), 0.0)
        run_sum = run_sum * factor + jnp.sum(weights, axis=-1)
        accum = accum * factor.T[:, :, None] + jnp.einsum(
            "hqk,khd->qhd",
            weights.astype(jnp.bfloat16),
            value_block,
            preferred_element_type=jnp.float32,
        )
        return ((new_max, run_sum, accum), None)

    start_state = (
        jnp.full((heads_here, span), floor_value, jnp.float32),
        jnp.zeros((heads_here, span), jnp.float32),
        jnp.zeros((span, heads_here, HEAD_DIM), jnp.float32),
    )
    (run_max, run_sum, accum), unused = lax.scan(
        forward_block,
        start_state,
        (
            keys_all.reshape(blocks, span, heads_here, HEAD_DIM),
            values_all.reshape(blocks, span, heads_here, HEAD_DIM),
            segs_all.reshape(blocks, span),
            block_ids,
        ),
    )
    log_total = run_max + jnp.log(run_sum)
    attention = accum / run_sum.T[:, :, None]
    attn_low = attention.reshape(span, local_cols).astype(jnp.bfloat16)
    rows = attn_low
    branch = lax.psum_scatter(
        jnp.dot(rows, out_rows, preferred_element_type=jnp.float32).astype(jnp.bfloat16),
        "uly",
        scatter_dimension=0,
        tiled=True,
    ).astype(jnp.float32)
    inverse_branch = inverse_rms(branch)
    resid = x_rows.astype(jnp.float32) + branch * inverse_branch * post_gain[0]
    group_resid = lax.all_gather(resid.astype(jnp.bfloat16), "uly", axis=0, tiled=True)
    gate_lin = jnp.einsum("td,cdf->ctf", group_resid, gate_cols, preferred_element_type=jnp.float32)
    activated = jax.nn.silu(gate_lin[0])
    hidden_low = (activated * gate_lin[1]).astype(jnp.bfloat16)
    rows = hidden_low
    mlp_out = lax.psum_scatter(
        jnp.dot(rows, down_rows, preferred_element_type=jnp.float32).astype(jnp.bfloat16),
        "uly",
        scatter_dimension=0,
        tiled=True,
    ).astype(jnp.float32)
    inverse_mlp = inverse_rms(mlp_out)
    block_out = (resid + mlp_out * inverse_mlp * post_gain[1]).astype(jnp.bfloat16)[None]
    grad_out = cotangent[0].astype(jnp.float32)
    gain_mlp = jnp.sum(grad_out * mlp_out * inverse_mlp, axis=0)
    d_mlp = norm_back(mlp_out, inverse_mlp, grad_out * post_gain[1], width).astype(jnp.bfloat16)
    group_dmlp = lax.all_gather(d_mlp, "uly", axis=0, tiled=True)
    d_hidden = jnp.einsum("td,fd->tf", group_dmlp, down_rows, preferred_element_type=jnp.float32)
    down_grad = jnp.einsum("tf,td->fd", hidden_low, group_dmlp, preferred_element_type=jnp.float32)
    sigmoid_gate = jax.nn.sigmoid(gate_lin[0])
    silu_slope = sigmoid_gate * (1.0 + gate_lin[0] * (1.0 - sigmoid_gate))
    d_gate_up = jnp.stack([d_hidden * gate_lin[1] * silu_slope, d_hidden * activated]).astype(
        jnp.bfloat16
    )
    gate_grad = jnp.einsum(
        "td,ctf->cdf", group_resid, d_gate_up, preferred_element_type=jnp.float32
    )
    rows = d_gate_up
    d_resid = grad_out + lax.psum_scatter(
        jnp.einsum("ctf,cdf->td", rows, gate_cols, preferred_element_type=jnp.float32).astype(
            jnp.bfloat16
        ),
        "uly",
        scatter_dimension=0,
        tiled=True,
    ).astype(jnp.float32)
    d_branch = norm_back(branch, inverse_branch, d_resid * post_gain[0], width).astype(jnp.bfloat16)
    group_dbranch = lax.all_gather(d_branch, "uly", axis=0, tiled=True)
    gain_attn = jnp.sum(d_resid * branch * inverse_branch, axis=0)
    d_attn = jnp.einsum("td,ed->te", group_dbranch, out_rows, preferred_element_type=jnp.float32)
    out_grad = jnp.einsum("te,td->ed", attn_low, group_dbranch, preferred_element_type=jnp.float32)
    d_attn_low = d_attn.astype(jnp.bfloat16).reshape(span, heads_here, HEAD_DIM)
    delta = jnp.sum(d_attn_low.astype(jnp.float32) * attention, axis=-1).T
    keys_back, values_back, segs_back = (keys_all, values_all, segs_all)

    def backward_block(d_query, block):
        key_block, value_block, seg_block, number = block
        mask = allowed(positions, number * span + local_pos, group_seg, seg_block)
        scores = (
            jnp.einsum("qhd,khd->hqk", query_low, key_block, preferred_element_type=jnp.float32)
            * scale
        )
        probs = jnp.where(mask[None], jnp.exp(scores - log_total[:, :, None]), 0.0)
        d_value = jnp.einsum(
            "hqk,qhd->khd",
            probs.astype(jnp.bfloat16),
            d_attn_low,
            preferred_element_type=jnp.float32,
        )
        d_probs = jnp.einsum(
            "qhd,khd->hqk", d_attn_low, value_block, preferred_element_type=jnp.float32
        )
        d_scores = (probs * (d_probs - delta[:, :, None])).astype(jnp.bfloat16)
        d_query = (
            d_query
            + jnp.einsum("hqk,khd->qhd", d_scores, key_block, preferred_element_type=jnp.float32)
            * scale
        )
        d_key = (
            jnp.einsum("hqk,qhd->khd", d_scores, query_low, preferred_element_type=jnp.float32)
            * scale
        )
        return (d_query, (d_key, d_value))

    d_query, (d_keys, d_values) = lax.scan(
        backward_block,
        jnp.zeros((span, heads_here, HEAD_DIM), jnp.float32),
        (
            keys_back.reshape(blocks, span, heads_here, HEAD_DIM),
            values_back.reshape(blocks, span, heads_here, HEAD_DIM),
            segs_back.reshape(blocks, span),
            block_ids,
        ),
    )
    key_grad, value_grad = (
        lax.psum_scatter(
            d_keys.reshape(blocks * span, local_cols).astype(jnp.bfloat16),
            "ctx",
            scatter_dimension=0,
            tiled=True,
        ).astype(jnp.float32),
        lax.psum_scatter(
            d_values.reshape(blocks * span, local_cols).astype(jnp.bfloat16),
            "ctx",
            scatter_dimension=0,
            tiled=True,
        ).astype(jnp.float32),
    )
    d_rot = rotate(
        jnp.stack([d_query, key_grad.reshape(span, heads_here, HEAD_DIM)]), positions, -1.0
    ).reshape(2, span, local_cols)
    gain_cols = jnp.sum(d_rot * scaled_in, axis=1)
    scaled_grad = d_rot * qk_gain[:, None, :]
    row_dots = jnp.sum(projected[:2] * scaled_grad, axis=-1)
    gain_block = lax.dynamic_update_slice(
        jnp.zeros((2, width), jnp.float32), gain_cols, (0, lax.axis_index("uly") * local_cols)
    )
    gain_terms = jnp.concatenate([gain_block, jnp.stack([gain_attn, gain_mlp])], axis=0)
    dot_totals, gain_totals = (
        lax.psum(row_dots.astype(jnp.bfloat16), "uly").astype(jnp.float32),
        lax.psum(gain_terms.astype(jnp.bfloat16), "uly").astype(jnp.float32),
    )
    d_qk = (
        inverse_qk * scaled_grad - projected[:2] * inverse_qk**3 * (dot_totals / width)[:, :, None]
    )
    d_proj = jnp.concatenate([d_qk, value_grad[None]], axis=0).astype(jnp.bfloat16)
    qkv_grad = jnp.einsum("td,cte->cde", group_x, d_proj, preferred_element_type=jnp.float32)
    rows = d_proj
    input_grad = (
        d_resid
        + lax.psum_scatter(
            jnp.einsum("cte,cde->td", rows, qkv_cols, preferred_element_type=jnp.float32).astype(
                jnp.bfloat16
            ),
            "uly",
            scatter_dimension=0,
            tiled=True,
        ).astype(jnp.float32)
    ).astype(jnp.bfloat16)[None]
    qkv_part, out_part, gate_part, down_part, gain_part = (
        lax.psum_scatter(
            qkv_grad.astype(jnp.bfloat16), ("slot", "ctx"), scatter_dimension=1, tiled=True
        ).astype(jnp.float32),
        lax.psum_scatter(
            out_grad.astype(jnp.bfloat16), ("slot", "ctx"), scatter_dimension=1, tiled=True
        ).astype(jnp.float32),
        lax.psum_scatter(
            gate_grad.astype(jnp.bfloat16), ("slot", "ctx"), scatter_dimension=1, tiled=True
        ).astype(jnp.float32),
        lax.psum_scatter(
            down_grad.astype(jnp.bfloat16), ("slot", "ctx"), scatter_dimension=1, tiled=True
        ).astype(jnp.float32),
        lax.psum_scatter(
            gain_totals.astype(jnp.bfloat16), ("slot", "ctx"), scatter_dimension=1, tiled=True
        ).astype(jnp.float32),
    )
    return (block_out, input_grad, qkv_part, out_part, gate_part, down_part, gain_part)


def solution(mesh):
    in_specs = (
        P("slot", ("ctx", "uly"), None),
        P("slot", ("ctx", "uly")),
        P(None, ("slot", "ctx"), "uly"),
        P("uly", ("slot", "ctx")),
        P(None, ("slot", "ctx"), "uly"),
        P("uly", ("slot", "ctx")),
        P(None, "uly"),
        P(),
        P("slot", ("ctx", "uly"), None),
    )
    out_specs = (
        P("slot", ("ctx", "uly"), None),
        P("slot", ("ctx", "uly"), None),
        P(None, ("slot", "ctx"), "uly"),
        P("uly", ("slot", "ctx")),
        P(None, ("slot", "ctx"), "uly"),
        P("uly", ("slot", "ctx")),
        P(None, ("slot", "ctx")),
    )
    return jax.shard_map(
        on_device, mesh=mesh, in_specs=in_specs, out_specs=out_specs, check_vma=False
    )
```

profile of v0, /device:TPU:0, one launch (start us, length us, event | category | flops | bytes accessed | tf_op | source)
XLA Modules:
  0.0 1250.2 jit_solution(13457118054681160565)
XLA Ops:
  11.5 46.7 %all-gather.31.cloned.1.call-done = bf16[1,512,2048]{2,1,0:T(8,128)(2,1)} async-done(((bf16[1,128,2048]{2,1,0:T(8,128)(2,1)}), bf16[1,512,2048]{2,1,0:T(8,128)(2,1)}) %all-gather.31.cloned.1.call-update) | async-done | bytes 2097168 | tf_op jit(solution)/shard_map/all_gather | solution.py:62
  58.2 47.9 %all-gather.15.cloned.1.call-done = bf16[3,2048,512]{1,2,0:T(8,128)(2,1)} async-done(((bf16[3,256,512]{1,2,0:T(8,128)(2,1)}), bf16[3,2048,512]{1,2,0:T(8,128)(2,1)}) %all-gather.15.cloned.1.call-update) | async-done | bytes 6291472 | tf_op jit(solution)/shard_map/all_gather | solution.py:56
  146.6 13.0 %all-gather.33.cloned.1.call-done = bf16[1,2048,4,128]{1,3,2,0:T(8,128)(2,1)} async-done(((bf16[1,512,4,128]{1,3,2,0:T(8,128)(2,1)}), bf16[1,2048,4,128]{1,3,2,0:T(8,128)(2,1)}) %all-gather.33.cloned.1.call-update) | async-done | bytes 2097168 | tf_op jit(solution)/shard_map/all_gather | solution.py:44
  167.5 29.7 %all-gather.17.cloned.1.call-done = bf16[2048,4,128]{2,0,1:T(8,128)(2,1)} async-done(((bf16[512,4,128]{2,0,1:T(8,128)(2,1)}), bf16[2048,4,128]{2,0,1:T(8,128)(2,1)}) %all-gather.17.cloned.1.call-update) | async-done | bytes 2097168 | tf_op jit(solution)/shard_map/all_gather | solution.py:45
  197.2 46.3 %while.30 = (s32[]{:T(128)}, f32[4,512]{1,0:T(4,128)S(1)}, f32[4,512]{1,0:T(4,128)S(1)}, f32[512,4,128]{0,2,1:T(8,128)}, s32[4]{0:T(128)S(1)}, /*index=5*/bf16[4...) while((s32[]{:T(128)}, f32[4,512]{1,0:T(4,128)S(1)}, ...), condition=%wide.region_5.6_spmd.clone, body=%wide.region_2.5_spmd.clone.sunk | while | flops 552612864 | bytes 34222304 | solution.py:111
  250.6 43.2 %reduce-scatter.14.cloned.1.call-done = bf16[128,2048]{1,0:T(8,128)(2,1)} async-done(((bf16[512,2048]{1,0:T(8,128)(2,1)}), bf16[128,2048]{1,0:T(8,128)(2,1)}) %reduce-scatter.14.cloned.1.call-update) | async-done | bytes 524304 | tf_op jit(solution)/shard_map/reduce_scatter | solution.py:125
  298.8 43.7 %all-gather.21.cloned.1.call-done = bf16[512,2048]{1,0:T(8,128)(2,1)} async-done(((bf16[128,2048]{1,0:T(8,128)(2,1)}), bf16[512,2048]{1,0:T(8,128)(2,1)}) %all-gather.21.cloned.1.call-update) | async-done | bytes 2097168 | tf_op jit(solution)/shard_map/all_gather | solution.py:133
  342.5 90.7 %all-gather.23.cloned.1.call-done = bf16[2,2048,2048]{2,1,0:T(8,128)(2,1)} async-done(((bf16[2,256,2048]{2,1,0:T(8,128)(2,1)}), bf16[2,2048,2048]{2,1,0:T(8,128)(2,1)}) %all-gather.23.cloned.1.call-update) | async-done | bytes 16777232 | tf_op jit(solution)/shard_map/all_gather | solution.py:58
  433.2 12.6 %convolution_bitcast_fusion = f32[2,512,2048]{2,1,0:T(8,128)S(1)} fusion(bf16[2,2048,2048]{2,1,0:T(8,128)(2,1)} %all-gather.23.cloned.1.call-done, bf16[512,2048]{1,0:T(8,128)(2,1)} %all-gather.21.cloned.1.call-done), kind=kOutput, calls=%fused_computation.69 | convolution fusion | flops 8589934592 | bytes 27262976 | tf_op jit(solution)/shard_map/td,cdf->ctf/dot_general | solution.py:134
  451.6 39.6 %all-gather.25.cloned.1.call-done = bf16[2048,2048]{1,0:T(8,128)(2,1)} async-done(((bf16[2048,256]{1,0:T(8,128)(2,1)}), bf16[2048,2048]{1,0:T(8,128)(2,1)}) %all-gather.25.cloned.1.call-update) | async-done | bytes 8388624 | tf_op jit(solution)/shard_map/all_gather | solution.py:59
  501.1 44.0 %reduce-scatter.16.cloned.1.call-done = bf16[128,2048]{1,0:T(8,128)(2,1)} async-done(((bf16[512,2048]{1,0:T(8,128)(2,1)}), bf16[128,2048]{1,0:T(8,128)(2,1)}) %reduce-scatter.16.cloned.1.call-update) | async-done | bytes 524304 | tf_op jit(solution)/shard_map/reduce_scatter | solution.py:138
  550.5 45.0 %all-gather.27.cloned.1.call-done = bf16[512,2048]{1,0:T(8,128)(2,1)} async-done(((bf16[128,2048]{1,0:T(8,128)(2,1)}), bf16[512,2048]{1,0:T(8,128)(2,1)}) %all-gather.27.cloned.1.call-update) | async-done | bytes 2097168 | tf_op jit(solution)/shard_map/all_gather | solution.py:149
  609.5 13.4 %bitcast_convert_fusion.1 = bf16[512,2048]{1,0:T(8,128)(2,1)} fusion(bf16[2,2048,2048]{2,1,0:T(8,128)(2,1)} %all-gather.23.cloned.1.call-done, bf16[1,512,2048]{2,1,0:T(8,128)(2,1)S(1)} %get-tuple-element.410, bf16[1,512,2048]{2,1,0:T(8,128)(2,1)S(1)} %get-tuple-element.409), kind=kOutput, calls=%fused_computation.74 | convolution fusion | flops 8593080320 | bytes 23068672 | tf_op jit(solution)/shard_map/ctf,cdf->td/dot_general | solution.py:162
  623.0 42.7 %reduce-scatter.18.cloned.1.call-done = bf16[128,2048]{1,0:T(8,128)(2,1)} async-done(((bf16[512,2048]{1,0:T(8,128)(2,1)}), bf16[128,2048]{1,0:T(8,128)(2,1)}) %reduce-scatter.18.cloned.1.call-update) | async-done | bytes 524304 | tf_op jit(solution)/shard_map/reduce_scatter | solution.py:161
  670.6 45.2 %all-gather.29.cloned.1.call-done = bf16[512,2048]{1,0:T(8,128)(2,1)} async-done(((bf16[128,2048]{1,0:T(8,128)(2,1)}), bf16[512,2048]{1,0:T(8,128)(2,1)}) %all-gather.29.cloned.1.call-update) | async-done | bytes 2097168 | tf_op jit(solution)/shard_map/all_gather | solution.py:170
  720.6 50.2 %while.31 = (s32[]{:T(128)}, f32[512,4,128]{0,2,1:T(8,128)}, bf16[4,512,4,128]{3,1,2,0:T(8,128)(2,1)}, bf16[4,512,4,128]{3,1,2,0:T(8,128)(2,1)}, bf16[4,512,4,12...) while((s32[]{:T(128)}, f32[512,4,128]{0,2,1:T(8,128)}, ...), condition=%wide.region_15.16_spmd.clone, body=%wide.region_14.15_spmd.clone.sunk | while | flops 1355023360 | bytes 96768424 | solution.py:207
  775.8 34.0 %reduce-scatter.20.cloned.1.call-done = bf16[512,512]{1,0:T(8,128)(2,1)} async-done(((bf16[2048,512]{1,0:T(8,128)(2,1)}), bf16[512,512]{1,0:T(8,128)(2,1)}) %reduce-scatter.20.cloned.1.call-update) | async-done | bytes 524304 | tf_op jit(solution)/shard_map/reduce_scatter | solution.py:218
  865.6 22.7 %reduce-scatter.22.cloned.1.call-done = bf16[512,512]{0,1:T(8,128)(2,1)} async-done(((bf16[2048,512]{0,1:T(8,128)(2,1)}), bf16[512,512]{0,1:T(8,128)(2,1)}) %reduce-scatter.22.cloned.1.call-update) | async-done | bytes 524304 | tf_op jit(solution)/shard_map/reduce_scatter | solution.py:224
  905.8 14.7 %convert_bitcast_fusion = bf16[2,2048,2048]{1,2,0:T(8,128)(2,1)} fusion(bf16[1,512,2048]{2,1,0:T(8,128)(2,1)} %copy-done.33, bf16[1,512,2048]{2,1,0:T(8,128)(2,1)} %copy-done.32, bf16[512,2048]{1,0:T(8,128)(2,1)S(1)} %copy-done.30), kind=kOutput, calls=%fused_computation.66 | convolution fusion | flops 8600420352 | bytes 23068672 | tf_op jit(solution)/shard_map/td,ctf->cdf/dot_general | solution.py:157
  920.5 12.2 reduce-scatter.28.cloned.1.call-done
  935.1 72.7 %reduce-scatter.32.cloned.1.call-done = bf16[2048,256]{1,0:T(8,128)(2,1)} async-done(((bf16[2048,2048]{1,0:T(8,128)(2,1)}), bf16[2048,256]{1,0:T(8,128)(2,1)}) %reduce-scatter.32.cloned.1.call-update) | async-done | bytes 1048592 | tf_op jit(solution)/shard_map/reduce_scatter | solution.py:272
  1010.5 44.0 %reduce-scatter.24.cloned.1.call-done = bf16[128,2048]{1,0:T(8,128)(2,1)} async-done(((bf16[512,2048]{1,0:T(8,128)(2,1)}), bf16[128,2048]{1,0:T(8,128)(2,1)}) %reduce-scatter.24.cloned.1.call-update) | async-done | bytes 524304 | tf_op jit(solution)/shard_map/reduce_scatter | solution.py:253
  1056.6 62.6 %reduce-scatter.26.cloned.1.call-done = bf16[3,256,512]{1,2,0:T(8,128)(2,1)} async-done(((bf16[3,2048,512]{1,2,0:T(8,128)(2,1)}), bf16[3,256,512]{1,2,0:T(8,128)(2,1)}) %reduce-scatter.26.cloned.1.call-update) | async-done | bytes 786448 | tf_op jit(solution)/shard_map/reduce_scatter | solution.py:263
  1121.8 117.0 %reduce-scatter.30.cloned.1.call-done = bf16[2,256,2048]{1,2,0:T(8,128)(2,1)} async-done(((bf16[2,2048,2048]{1,2,0:T(8,128)(2,1)}), bf16[2,256,2048]{1,2,0:T(8,128)(2,1)}) %reduce-scatter.30.cloned.1.call-update) | async-done | bytes 2097168 | tf_op jit(solution)/shard_map/reduce_scatter | solution.py:269
  (315 shorter events, 292.1 us)
Async XLA Ops:
  7.2 51.1 %all-gather.31.cloned.1.call-start = ((), (), s32[]{:S(2)}) async-start(), calls=%async_computation.29 | async-start | bytes 2621440 | tf_op jit(solution)/shard_map/all_gather | solution.py:62
  7.9 98.2 %all-gather.15.cloned.1.call-start = ((), (), s32[]{:S(2)}) async-start(), calls=%async_computation.11 | async-start | bytes 7077888 | tf_op jit(solution)/shard_map/all_gather | solution.py:56
  10.3 149.3 %all-gather.33.cloned.1.call-start = ((), (), s32[]{:S(2)}) async-start(), calls=%async_computation.30 | async-start | bytes 2621440 | tf_op jit(solution)/shard_map/all_gather | solution.py:44
  11.5 113.9 %copy-start.17 = (f32[512,64]{0,1:T(8,128)}, f32[512,64]{0,1:T(8,128)S(1)}, u32[]{:S(2)}) copy-start(f32[512,64]{0,1:T(8,128)S(1)} %get-tuple-element.425) | copy-start | bytes 393220
  127.0 70.2 %all-gather.17.cloned.1.call-start = ((), (), s32[]{:S(2)}) async-start(), calls=%async_computation.12 | async-start | bytes 2621440 | tf_op jit(solution)/shard_map/all_gather | solution.py:45
  130.1 114.8 %all-gather.19.cloned.1.call-start = ((), (), s32[]{:S(2)}) async-start(), calls=%async_computation.13 | async-start | bytes 2359296 | tf_op jit(solution)/shard_map/all_gather | solution.py:57
  130.6 163.1 %reduce-scatter.14.cloned.1.call-start = ((), (), s32[]{:S(2)}) async-start(), calls=%async_computation.14 | async-start | bytes 2621440 | tf_op jit(solution)/shard_map/reduce_scatter | solution.py:125
  249.9 92.7 %all-gather.21.cloned.1.call-start = ((), (), s32[]{:S(2)}) async-start(), calls=%async_computation.15 | async-start | bytes 2621440 | tf_op jit(solution)/shard_map/all_gather | solution.py:133
  297.1 136.1 %all-gather.23.cloned.1.call-start = ((), (), s32[]{:S(2)}) async-start(), calls=%async_computation.16 | async-start | bytes 18874368 | tf_op jit(solution)/shard_map/all_gather | solution.py:58
  297.8 193.4 %all-gather.25.cloned.1.call-start = ((), (), s32[]{:S(2)}) async-start(), calls=%async_computation.17 | async-start | bytes 9437184 | tf_op jit(solution)/shard_map/all_gather | solution.py:59
  298.6 246.5 %reduce-scatter.16.cloned.1.call-start = ((), (), s32[]{:S(2)}) async-start(), calls=%async_computation.18 | async-start | bytes 2621440 | tf_op jit(solution)/shard_map/reduce_scatter | solution.py:138
  501.1 94.4 %all-gather.27.cloned.1.call-start = ((), (), s32[]{:S(2)}) async-start(), calls=%async_computation.19 | async-start | bytes 2621440 | tf_op jit(solution)/shard_map/all_gather | solution.py:149
  550.0 115.6 %reduce-scatter.18.cloned.1.call-start = ((), (), s32[]{:S(2)}) async-start(), calls=%async_computation.20 | async-start | bytes 2621440 | tf_op jit(solution)/shard_map/reduce_scatter | solution.py:161
  622.9 92.9 %all-gather.29.cloned.1.call-start = ((), (), s32[]{:S(2)}) async-start(), calls=%async_computation.21 | async-start | bytes 2621440 | tf_op jit(solution)/shard_map/all_gather | solution.py:170
  670.4 139.4 %reduce-scatter.20.cloned.1.call-start = ((), (), s32[]{:S(2)}) async-start(), calls=%async_computation.22 | async-start | bytes 2621440 | tf_op jit(solution)/shard_map/reduce_scatter | solution.py:218
  775.7 74.3 %reduce-scatter.34.cloned.1.call-start = ((), (), s32[]{:S(2)}) async-start(), calls=%async_computation.31 | async-start | bytes 589824
  815.8 72.6 %reduce-scatter.22.cloned.1.call-start = ((), (), s32[]{:S(2)}) async-start(), calls=%async_computation.23 | async-start | bytes 2621440 | tf_op jit(solution)/shard_map/reduce_scatter | solution.py:224
  824.0 108.8 %reduce-scatter.28.cloned.1.call-start = ((), (), s32[]{:S(2)}) async-start(), calls=%async_computation.26 | async-start | bytes 2359296 | tf_op jit(solution)/shard_map/reduce_scatter | solution.py:266
  828.5 179.3 %reduce-scatter.32.cloned.1.call-start = ((), (), s32[]{:S(2)}) async-start(), calls=%async_computation.28 | async-start | bytes 9437184 | tf_op jit(solution)/shard_map/reduce_scatter | solution.py:272
  838.8 215.7 %reduce-scatter.24.cloned.1.call-start = ((), (), s32[]{:S(2)}) async-start(), calls=%async_computation.24 | async-start | bytes 2621440 | tf_op jit(solution)/shard_map/reduce_scatter | solution.py:253
  896.6 222.7 %reduce-scatter.26.cloned.1.call-start = ((), (), s32[]{:S(2)}) async-start(), calls=%async_computation.25 | async-start | bytes 7077888 | tf_op jit(solution)/shard_map/reduce_scatter | solution.py:263
  904.2 334.6 %reduce-scatter.30.cloned.1.call-start = ((), (), s32[]{:S(2)}) async-start(), calls=%async_computation.27 | async-start | bytes 18874368 | tf_op jit(solution)/shard_map/reduce_scatter | solution.py:269
  920.5 134.0 %copy-start.10 = (bf16[1,128,2048]{2,1,0:T(8,128)(2,1)S(1)}, bf16[1,128,2048]{2,1,0:T(8,128)(2,1)}, u32[]{:S(2)}) copy-start(bf16[1,128,2048]{2,1,0:T(8,128)(2,1)} %param.21) | copy-start | bytes 1572868
  920.5 134.0 %copy-start.13 = (bf16[128,2048]{1,0:T(8,128)(2,1)S(1)}, bf16[128,2048]{1,0:T(8,128)(2,1)}, u32[]{:S(2)}) copy-start(bf16[128,2048]{1,0:T(8,128)(2,1)} %reduce-scatter.18.cloned.1.call-done) | copy-start | bytes 1572868
  (55 other events, 384.1 us)
Sparse Core Ops, SparseCore 0:
  9.6 48.6 all-gather.30
  60.7 45.3 all-gather.14
  127.1 32.4 all-gather.32
  161.9 35.3 all-gather.16
  199.0 28.1 all-gather.18
  250.0 43.7 reduce-scatter.13
  297.2 45.2 all-gather.20
  344.6 88.5 all-gather.22
  435.2 55.9 all-gather.24
  501.2 43.8 reduce-scatter.15
  550.1 45.2 all-gather.26
  623.0 42.5 reduce-scatter.17
  670.5 45.2 all-gather.28
  775.8 33.8 reduce-scatter.19
  815.9 34.1 reduce-scatter.33
  853.1 35.1 reduce-scatter.21
  891.5 41.2 reduce-scatter.27
  936.4 71.2 reduce-scatter.31
  1010.6 43.8 reduce-scatter.23
  1058.1 61.0 reduce-scatter.25
  1122.8 115.9 reduce-scatter.29
where the time goes:
time: 1260 us; the launch traced here: 1250 us
  waiting for transfers between devices  910 us (72%)
  matrix products  167 us (13%)
  local copies, waits for them, and re-layouts  63.6 us (5%)
  other arithmetic  47 us (4%)
  blocking collectives  38.9 us (3%)
  between operations  15.2 us (1%)
    reduce_scatter x1, waiting for transfers between devices, on_device(): lax.psum_scatter(gate_grad.astype(jnp.bfloat16), ('slot', 'ctx'), scatter...  117 us
    all_gather x1, waiting for transfers between devices, on_device(): lax.all_gather(gate_up, ('slot', 'ctx'), axis=1, tiled=True)  90.7 us
    reduce_scatter x1, waiting for transfers between devices, on_device(): lax.psum_scatter(down_grad.astype(jnp.bfloat16), ('slot', 'ctx'), scatter...  72.7 us
    reduce_scatter x1, waiting for transfers between devices, on_device(): lax.psum_scatter(qkv_grad.astype(jnp.bfloat16), ('slot', 'ctx'), scatter_...  62.6 us
    all_gather x1, waiting for transfers between devices, on_device(): lax.all_gather(qkv_weight, ('slot', 'ctx'), axis=1, tiled=True)  47.9 us
    all_gather x1, waiting for transfers between devices, on_device(): lax.all_gather(x_rows, 'uly', axis=0, tiled=True)  46.7 us
    all_gather x1, waiting for transfers between devices, on_device(): group_dbranch = lax.all_gather(d_branch, 'uly', axis=0, tiled=True)  45.2 us
    all_gather x1, waiting for transfers between devices, on_device(): group_dmlp = lax.all_gather(d_mlp, 'uly', axis=0, tiled=True)  45 us
  transfers between devices with their start and end apart: 21, of which 20 were waited for; matrix products, arithmetic and copies ran while one was open for 11% of the time, Pallas kernels for 0%

commit v1 on v0

v1 whole, which is shorter than its diff:
```python
import functools

import jax
import jax.numpy as jnp
import numpy as np
from jax import lax
from jax.experimental import pallas as pl
from jax.experimental.pallas import tpu as pltpu
from jax.sharding import PartitionSpec as P

HEAD_DIM = 128
HALF = HEAD_DIM // 2
EPS = 1e-06
ROPE_BASE = 500000.0
FLOOR = -1e30
LOG2E = 1.4426950408889634
SCALE2 = HEAD_DIM ** (-0.5) * LOG2E
MESH_ID = pl.DeviceIdType.MESH
BF16 = jnp.bfloat16
F32 = jnp.float32
VMEM_LIMIT = 60 * 1024 * 1024
CHUNKS = 4

VM = pl.BlockSpec(memory_space=pltpu.VMEM)
HB = pl.BlockSpec(memory_space=pl.ANY)


def shape(dims, dtype):
    return jax.ShapeDtypeStruct(dims, dtype)


def where_am_i():
    return lax.axis_index("slot"), lax.axis_index("ctx"), lax.axis_index("uly")


def rows_of(index, rows):
    return pl.ds(pl.multiple_of(index * rows, rows), rows)


def greet(peers):
    barrier = pltpu.get_barrier_semaphore()
    total = 0
    for condition, peer in peers:
        if condition is None:
            pl.semaphore_signal(barrier, inc=1, device_id=peer, device_id_type=MESH_ID)
            total = total + 1
        else:

            @pl.when(condition)
            def _():
                pl.semaphore_signal(barrier, inc=1, device_id=peer, device_id_type=MESH_ID)

            total = total + condition.astype(jnp.int32)
    pl.semaphore_wait(barrier, total)


def line_peers(n):
    s, c, u = where_am_i()
    return [(u > 0, (s, c, u - 1)), (u < n - 1, (s, c, u + 1))]


def plane_peers():
    s, c, u = where_am_i()
    return [(None, (s, c ^ 1, u)), (None, (s, c ^ 2, u))]


def remote(src, dst, send, recv, peer):
    return pltpu.make_async_remote_copy(
        src_ref=src,
        dst_ref=dst,
        send_sem=send,
        recv_sem=recv,
        device_id=peer,
        device_id_type=MESH_ID,
    )


def line_sems(n, chunks=None):
    dims = (n - 1,) if chunks is None else (n - 1, chunks)
    return [pltpu.SemaphoreType.DMA(dims)] * 4


class LineGather:
    def __init__(self, n, rows, buf, sems):
        self.n, self.rows, self.buf, self.sems = n, rows, buf, sems

    def copy(self, right, slot, shard):
        s, c, u = where_am_i()
        send_r, recv_r, send_l, recv_l = self.sems
        view = self.buf.at[rows_of(shard, self.rows)]
        if right:
            return remote(view, view, send_r.at[slot], recv_r.at[slot], (s, c, u + 1))
        return remote(view, view, send_l.at[slot], recv_l.at[slot], (s, c, u - 1))

    def send(self, slot):
        u, n = lax.axis_index("uly"), self.n

        @pl.when((u < n - 1) & (u - slot >= 0))
        def _():
            self.copy(True, slot, u - slot).start()

        @pl.when((u > 0) & (u + slot <= n - 1))
        def _():
            self.copy(False, slot, u + slot).start()

    def wait(self, slot):
        u, n = lax.axis_index("uly"), self.n

        @pl.when(u - 1 - slot >= 0)
        def _():
            self.copy(True, slot, u - 1 - slot).wait_recv()

        @pl.when(u + 1 + slot <= n - 1)
        def _():
            self.copy(False, slot, u + 1 + slot).wait_recv()

        if slot + 1 < n - 1:
            self.send(slot + 1)

    def finish(self):
        u, n = lax.axis_index("uly"), self.n
        for slot in range(n - 1):

            @pl.when((u < n - 1) & (u - slot >= 0))
            def _():
                self.copy(True, slot, u - slot).wait_send()

            @pl.when((u > 0) & (u + slot <= n - 1))
            def _():
                self.copy(False, slot, u + slot).wait_send()

    def run(self):
        self.send(0)
        for slot in range(self.n - 1):
            self.wait(slot)
        self.finish()


class LineReduce:
    def __init__(self, n, rows, part, from_l, from_r, sems):
        self.n, self.rows, self.sems = n, rows, sems
        self.part, self.from_l, self.from_r = part, from_l, from_r
        self.chunks = part.shape[0]

    def copy(self, right, slot, chunk, block):
        s, c, u = where_am_i()
        send_r, recv_r, send_l, recv_l = self.sems
        where = rows_of(block, self.rows)
        src = self.part.at[chunk, where]
        if right:
            return remote(
                src,
                self.from_l.at[chunk, where],
                send_r.at[slot, chunk],
                recv_r.at[slot, chunk],
                (s, c, u + 1),
            )
        return remote(
            src,
            self.from_r.at[chunk, where],
            send_l.at[slot, chunk],
            recv_l.at[slot, chunk],
            (s, c, u - 1),
        )

    def add(self, chunk, block, source):
        where = rows_of(block, self.rows)
        self.part[chunk, where, :] = (
            self.part[chunk, where, :].astype(F32) + source[chunk, where, :].astype(F32)
        ).astype(BF16)

    def step(self, slot, chunk):
        u, n = lax.axis_index("uly"), self.n
        block_r = n - 1 - slot + u
        block_l = slot - (n - 1) + u

        @pl.when(u <= slot)
        def _():
            if slot > 0:

                @pl.when(u > 0)
                def _():
                    self.copy(True, slot - 1, chunk, block_r).wait_recv()
                    self.add(chunk, block_r, self.from_l)

            self.copy(True, slot, chunk, block_r).start()

        @pl.when(u >= n - 1 - slot)
        def _():
            if slot > 0:

                @pl.when(u < n - 1)
                def _():
                    self.copy(False, slot - 1, chunk, block_l).wait_recv()
                    self.add(chunk, block_l, self.from_r)

            self.copy(False, slot, chunk, block_l).start()

    def last(self, out):
        u, n = lax.axis_index("uly"), self.n
        where = rows_of(u, self.rows)
        width = self.part.shape[2]
        for chunk in range(self.chunks):
            cols = slice(chunk * width, (chunk + 1) * width)
            out[:, cols] = self.part[chunk, where, :].astype(F32)

            @pl.when(u > 0)
            def _():
                self.copy(True, n - 2, chunk, u).wait_recv()
                out[:, cols] += self.from_l[chunk, where, :].astype(F32)

            @pl.when(u < n - 1)
            def _():
                self.copy(False, n - 2, chunk, u).wait_recv()
                out[:, cols] += self.from_r[chunk, where, :].astype(F32)

    def finish(self):
        u, n = lax.axis_index("uly"), self.n
        for slot in range(n - 1):
            for chunk in range(self.chunks):

                @pl.when(u <= slot)
                def _():
                    self.copy(True, slot, chunk, n - 1 - slot + u).wait_send()

                @pl.when(u >= n - 1 - slot)
                def _():
                    self.copy(False, slot, chunk, slot - (n - 1) + u).wait_send()

    def run(self, compute, out):
        for slot in range(self.n - 1):
            for chunk in range(self.chunks):
                if slot == 0:
                    compute(chunk)
                self.step(slot, chunk)
        self.last(out)
        self.finish()


def dot(a, b, dims):
    return lax.dot_general(a, b, ((dims[:1], dims[1:]), ((), ())), preferred_element_type=F32)


NN, NT, TN = (1, 0), (1, 1), (0, 0)


def tiles(total, size):
    size = min(total, size)
    return total // size, size


def inverse_rms(values):
    return lax.rsqrt(jnp.mean(values * values, axis=-1, keepdims=True) + EPS)


def norm_back(values, inverse, grad_scaled, width):
    return inverse * grad_scaled - values * inverse**3 * (
        jnp.sum(values * grad_scaled, axis=-1, keepdims=True) / width
    )


def rope_factors(table):
    lane = lax.broadcasted_iota(jnp.int32, table.shape, 1)
    turned = pltpu.roll(table, HALF, 1)
    cosine = jnp.where(lane < HALF, table, turned)
    sine = jnp.where(lane < HALF, -turned, table)
    return cosine, sine


def exchange_rows(n, mine, msg, send, recv):
    s, c, u = where_am_i()
    msg[pl.ds(u, 1)] = mine[None]
    copies = []
    for step in range(1, n):
        peer = lax.rem(u + step, n)
        copy = remote(msg.at[u], msg.at[u], send.at[step - 1], recv.at[step - 1], (s, c, peer))
        copy.start()
        copies.append(copy)
    for step in range(1, n):
        source = lax.rem(u + n - step, n)
        remote(
            msg.at[source], msg.at[source], send.at[step - 1], recv.at[step - 1], (s, c, source)
        ).wait_recv()
    total = msg[0]
    for j in range(1, n):
        total = total + msg[j]
    for copy in copies:
        copy.wait_send()
    return total


def to_rows(col0, col1):
    span = col0.shape[0]
    lane = lax.broadcasted_iota(jnp.int32, (span, 128), 1)
    both = jnp.where(lane == 0, col0, jnp.where(lane == 1, col1, 0.0))
    return jnp.transpose(both)[:8]


def to_columns(rows8):
    return jnp.transpose(jnp.concatenate([rows8] * 16, axis=0))


def all_uly_peers(n):
    s, c, u = where_am_i()
    return [(None, (s, c, lax.rem(u + k, n))) for k in range(1, n)]


def proj_kernel(
    n,
    x_ref,
    w_ref,
    tab_ref,
    gain_ref,
    seg_ref,
    xg_out,
    wq_out,
    proj_ref,
    q_ref,
    kv_ref,
    inv_ref,
    zero_ref,
    xg,
    wq,
    tab,
    msg,
    local_sem,
    w_send,
    w_recv,
    m_send,
    m_recv,
    *line,
):
    s, c, u = where_am_i()
    rows, width = x_ref.shape
    span = n * rows
    kb = w_ref.shape[1]
    sib, xn, yn = (1 - s, c, u), (s, c ^ 1, u), (s, c ^ 2, u)
    tab_copy = pltpu.make_async_copy(tab_ref.at[rows_of(c, span)], tab, local_sem.at[0])
    tab_copy.start()
    own_block = s * 4 + c
    own_copy = pltpu.make_async_copy(w_ref, wq.at[:, rows_of(own_block, kb)], local_sem.at[1])
    own_copy.start()
    xg[rows_of(u, rows), :] = x_ref[...]
    greet(all_uly_peers(n) + plane_peers() + [(None, sib)])

    def block(b):
        return wq.at[:, rows_of(b, kb)]

    def half(b, part):
        return wq.at[:, pl.ds(pl.multiple_of(b * kb + part * (kb // 2), kb // 2), kb // 2)]

    def sent(k, src, dst, peer):
        return remote(src, dst, w_send.at[k], w_recv.at[k], peer)

    bx, by, bd = s * 4 + (c ^ 1), s * 4 + (c ^ 2), s * 4 + (c ^ 3)
    gather = LineGather(n, rows, xg, line)
    gather.send(0)
    copies = [
        sent(0, w_ref, block(own_block), xn),
        sent(1, w_ref, block(own_block), yn),
        sent(2, w_ref, block(own_block), sib),
    ]
    for copy in copies:
        copy.start()
    gather.wait(0)
    sent(0, block(bx), block(bx), xn).wait_recv()
    more = [sent(3, half(bx, 0), half(bx, 0), yn), sent(4, block(bx), block(bx), sib)]
    for copy in more:
        copy.start()
    copies += more
    sent(1, block(by), block(by), yn).wait_recv()
    more = [sent(5, half(by, 1), half(by, 1), xn), sent(6, block(by), block(by), sib)]
    for copy in more:
        copy.start()
    copies += more
    if n > 2:
        gather.wait(1)
    sent(3, half(bd, 0), half(bd, 0), yn).wait_recv()
    more = [sent(7, half(bd, 0), half(bd, 0), sib)]
    more[0].start()
    copies += more
    sent(5, half(bd, 1), half(bd, 1), xn).wait_recv()
    more = [sent(8, half(bd, 1), half(bd, 1), sib)]
    more[0].start()
    copies += more
    for slot in range(2 if n > 2 else 1, n - 1):
        gather.wait(slot)
    far = (1 - s) * 4
    sent(2, block(far + c), block(far + c), sib).wait_recv()
    sent(4, block(far + (c ^ 1)), block(far + (c ^ 1)), sib).wait_recv()
    sent(6, block(far + (c ^ 2)), block(far + (c ^ 2)), sib).wait_recv()
    sent(7, half(far + (c ^ 3), 0), half(far + (c ^ 3), 0), sib).wait_recv()
    sent(8, half(far + (c ^ 3), 1), half(far + (c ^ 3), 1), sib).wait_recv()
    own_copy.wait()
    tab_copy.wait()
    keep = [
        pltpu.make_async_copy(xg, xg_out, local_sem.at[2]),
        pltpu.make_async_copy(wq, wq_out, local_sem.at[3]),
    ]
    for copy in keep:
        copy.start()

    count, size = tiles(span, 512)

    def project(i, carry):
        where = pl.ds(pl.multiple_of(i * size, size), size)
        xs = xg[where, :]
        proj_ref[0, where, :] = dot(xs, wq[0], NN)
        proj_ref[1, where, :] = dot(xs, wq[1], NN)
        kv_ref[1, where, :] = dot(xs, wq[2], NN).astype(BF16)
        return carry

    lax.fori_loop(0, count, project, 0)
    squares = [jnp.sum(proj_ref[i] * proj_ref[i], axis=-1, keepdims=True) for i in range(2)]
    mine = to_rows(*squares)
    zeros = jnp.sum((1 - seg_ref[...]).astype(F32))
    row = lax.broadcasted_iota(jnp.int32, mine.shape, 0)
    mine = jnp.where(row == 2, zeros, mine)
    total = exchange_rows(n, mine, msg, m_send, m_recv)
    zero_ref[...] = jnp.broadcast_to(total[2:3, :128], (8, 128))
    inv = lax.rsqrt(to_columns(total) / width + EPS)
    inv_ref[...] = inv
    cosine, sine = rope_factors(tab[...])
    heads = proj_ref.shape[2] // HEAD_DIM
    for i in range(2):
        inverse = inv_ref[:, i : i + 1]
        for h in range(heads):
            cols = slice(h * HEAD_DIM, (h + 1) * HEAD_DIM)
            v = proj_ref[i, :, cols] * inverse * gain_ref[i : i + 1, cols]
            v = (v * cosine + pltpu.roll(v, HALF, 1) * sine).astype(BF16)
            if i == 0:
                q_ref[:, cols] = v
            else:
                kv_ref[0, :, cols] = v
    for copy in copies:
        copy.wait_send()
    gather.finish()
    for copy in keep:
        copy.wait()


def project(n, x, w, table, gain, seg):
    rows, width = x.shape
    span, cols = n * rows, w.shape[2]
    return pl.pallas_call(
        functools.partial(proj_kernel, n),
        out_shape=(
            shape((span, width), BF16),
            shape((3, width, cols), BF16),
            shape((2, span, cols), F32),
            shape((span, cols), BF16),
            shape((2, span, cols), BF16),
            shape((span, 128), F32),
            shape((8, 128), F32),
        ),
        in_specs=[VM, HB, HB, VM, VM],
        out_specs=(HB, HB, VM, VM, VM, VM, VM),
        scratch_shapes=[
            pltpu.VMEM((span, width), BF16),
            pltpu.VMEM((3, width, cols), BF16),
            pltpu.VMEM((span, 128), F32),
            pltpu.VMEM((n, 8, span), F32),
            pltpu.SemaphoreType.DMA((4,)),
            pltpu.SemaphoreType.DMA((9,)),
            pltpu.SemaphoreType.DMA((9,)),
            pltpu.SemaphoreType.DMA((n - 1,)),
            pltpu.SemaphoreType.DMA((n - 1,)),
        ]
        + line_sems(n),
        compiler_params=pltpu.CompilerParams(
            collective_id=1, has_side_effects=True, vmem_limit_bytes=VMEM_LIMIT
        ),
        cost_estimate=pl.CostEstimate(
            flops=40 * 10**9, bytes_accessed=10**7, transcendentals=0
        ),
        name="project",
    )(x, w, table, gain, seg)


def score_mask(scores, key_first, query_first, starts, diagonal):
    key_pos = key_first + lax.broadcasted_iota(jnp.int32, scores.shape, 0)
    keep = key_pos >= starts
    if diagonal:
        query_pos = query_first + lax.broadcasted_iota(jnp.int32, scores.shape, 1)
        keep = keep & (key_pos <= query_pos)
    return jnp.where(keep, scores, FLOOR)


def segment_starts(first, size, bound):
    pos = first + lax.broadcasted_iota(jnp.int32, (1, size), 1)
    return jnp.where(pos >= bound, bound, 0)


def attend_kernel(
    q_ref,
    kv_ref,
    zero_ref,
    kvall_out,
    attn_ref,
    attn32_ref,
    lse_ref,
    bound_ref,
    kvall,
    peaks,
    sums,
    acct,
    zmsg,
    send,
    recv,
    z_send,
    z_recv,
    keep_sem,
):
    s, c, u = where_am_i()
    span, cols = q_ref.shape
    heads = cols // HEAD_DIM
    xn, yn, dn = (s, c ^ 1, u), (s, c ^ 2, u), (s, c ^ 3, u)
    kvall[pl.ds(c, 1)] = kv_ref[...][None]
    zmsg[pl.ds(c, 1)] = zero_ref[...][None]
    greet(plane_peers() + [(None, dn)])

    def sent(k, view, peer):
        return remote(view, view, send.at[k], recv.at[k], peer)

    bx, by, bd = c ^ 1, c ^ 2, c ^ 3
    zs = [
        remote(zmsg.at[c], zmsg.at[c], z_send.at[k], z_recv.at[k], peer)
        for k, peer in enumerate((xn, yn, dn))
    ]
    for copy in zs:
        copy.start()
    copies = [sent(0, kvall.at[c], xn), sent(1, kvall.at[c], yn)]
    for copy in copies:
        copy.start()
    for k, (b, peer) in enumerate(((bx, xn), (by, yn), (bd, dn))):
        remote(zmsg.at[b], zmsg.at[b], z_send.at[k], z_recv.at[k], peer).wait_recv()
    ahead = jnp.zeros((8, 128), F32)
    for j in range(4):
        ahead = ahead + jnp.where(j <= c, zmsg[j], 0.0)
    bounds = ahead.astype(jnp.int32)
    bound_ref[...] = bounds
    bound = bounds[:1, :1]

    peaks[...] = jnp.full_like(peaks, FLOOR)
    sums[...] = jnp.zeros_like(sums)
    acct[...] = jnp.zeros_like(acct)
    nq, tq = tiles(span, 512)
    nk, tk = tiles(span, 512)

    def update(number, diagonal):
        def over_queries(i, carry):
            first_q = c * span + i * tq
            starts = segment_starts(first_q, tq, bound)
            where_q = pl.ds(pl.multiple_of(i * tq, tq), tq)

            def over_keys(j, carry):
                first_k = number * span + j * tk
                where_k = pl.ds(pl.multiple_of(j * tk, tk), tk)
                for h in range(heads):
                    lanes = slice(h * HEAD_DIM, (h + 1) * HEAD_DIM)
                    scores = dot(kvall[number, 0, where_k, lanes], q_ref[where_q, lanes], NT)
                    scores = score_mask(scores * SCALE2, first_k, first_q, starts, diagonal)
                    old = peaks[h, :1, where_q]
                    new = jnp.maximum(old, jnp.max(scores, axis=0, keepdims=True))
                    factor = jnp.exp2(old - new)
                    weights = jnp.exp2(scores - new)
                    peaks[h, :1, where_q] = new
                    sums[h, :1, where_q] = sums[h, :1, where_q] * factor + jnp.sum(
                        weights, axis=0, keepdims=True
                    )
                    acct[h, :, where_q] = acct[h, :, where_q] * factor + dot(
                        kvall[number, 1, where_k, lanes], weights.astype(BF16), TN
                    )
                return carry

            return lax.fori_loop(0, nk, over_keys, carry)

        lax.fori_loop(0, nq, over_queries, 0)

    update(c, True)
    half = span // 2
    sent(0, kvall.at[bx], xn).wait_recv()
    more = [sent(2, kvall.at[bx, :, pl.ds(0, half)], yn)]
    more[0].start()
    copies += more
    sent(1, kvall.at[by], yn).wait_recv()
    more = [sent(3, kvall.at[by, :, pl.ds(half, half)], xn)]
    more[0].start()
    copies += more
    for b in (bx, by):

        @pl.when(b < c)
        def _():
            update(b, False)

    sent(2, kvall.at[bd, :, pl.ds(0, half)], yn).wait_recv()
    sent(3, kvall.at[bd, :, pl.ds(half, half)], xn).wait_recv()
    keep = pltpu.make_async_copy(kvall, kvall_out, keep_sem)
    keep.start()

    @pl.when(bd < c)
    def _():
        update(bd, False)

    for h in range(heads):
        lanes = slice(h * HEAD_DIM, (h + 1) * HEAD_DIM)
        total = sums[h, :1, :]
        attention = jnp.transpose(acct[h] / total)
        attn32_ref[:, lanes] = attention
        attn_ref[:, lanes] = attention.astype(BF16)
        lse_ref[h, :1, :] = peaks[h, :1, :] + jnp.log2(total)
    for copy in copies + zs:
        copy.wait_send()
    keep.wait()


def attend(q, kv, zero):
    span, cols = q.shape
    heads = cols // HEAD_DIM
    return pl.pallas_call(
        attend_kernel,
        out_shape=(
            shape((4, 2, span, cols), BF16),
            shape((span, cols), BF16),
            shape((span, cols), F32),
            shape((heads, 8, span), F32),
            shape((8, 128), jnp.int32),
        ),
        in_specs=[VM] * 3,
        out_specs=(HB, VM, VM, VM, VM),
        scratch_shapes=[
            pltpu.VMEM((4, 2, span, cols), BF16),
            pltpu.VMEM((heads, 8, span), F32),
            pltpu.VMEM((heads, 8, span), F32),
            pltpu.VMEM((heads, HEAD_DIM, span), F32),
            pltpu.VMEM((4, 8, 128), F32),
            pltpu.SemaphoreType.DMA((4,)),
            pltpu.SemaphoreType.DMA((4,)),
            pltpu.SemaphoreType.DMA((3,)),
            pltpu.SemaphoreType.DMA((3,)),
            pltpu.SemaphoreType.DMA,
        ],
        compiler_params=pltpu.CompilerParams(
            collective_id=2, has_side_effects=True, vmem_limit_bytes=VMEM_LIMIT
        ),
        cost_estimate=pl.CostEstimate(
            flops=40 * 10**9, bytes_accessed=10**7, transcendentals=0
        ),
        name="attend",
    )(q, kv, zero)


def attend_back_kernel(
    q_ref,
    kvall_ref,
    do_ref,
    attn32_ref,
    lse_ref,
    bound_ref,
    dq_ref,
    dkv_ref,
    part,
    got,
    acc,
    delta,
    send,
    recv,
):
    s, c, u = where_am_i()
    span, cols = q_ref.shape
    heads = cols // HEAD_DIM
    xn, yn = (s, c ^ 1, u), (s, c ^ 2, u)
    bx, by, bd = c ^ 1, c ^ 2, c ^ 3
    greet(plane_peers())
    bound = bound_ref[:1, :1]
    nq, tq = tiles(span, 512)
    nk, tk = tiles(span, 512)
    scale = HEAD_DIM ** (-0.5)
    dq_ref[...] = jnp.zeros_like(dq_ref)
    for h in range(heads):
        lanes = slice(h * HEAD_DIM, (h + 1) * HEAD_DIM)
        both = jnp.transpose(do_ref[:, lanes].astype(F32) * attn32_ref[:, lanes])
        delta[h, :1, :] = jnp.sum(both, axis=0, keepdims=True)

    def update(number, diagonal):
        acc[...] = jnp.zeros_like(acc)

        def over_queries(i, carry):
            first_q = c * span + i * tq
            starts = segment_starts(first_q, tq, bound)
            where_q = pl.ds(pl.multiple_of(i * tq, tq), tq)

            def over_keys(j, carry):
                first_k = number * span + j * tk
                where_k = pl.ds(pl.multiple_of(j * tk, tk), tk)
                for h in range(heads):
                    lanes = slice(h * HEAD_DIM, (h + 1) * HEAD_DIM)
                    keys = kvall_ref[number, 0, where_k, lanes]
                    values = kvall_ref[number, 1, where_k, lanes]
                    query, d_out = q_ref[where_q, lanes], do_ref[where_q, lanes]
                    scores = dot(keys, query, NT) * SCALE2
                    scores = score_mask(scores, first_k, first_q, starts, diagonal)
                    probs = jnp.exp2(scores - lse_ref[h, :1, where_q])
                    acc[1, where_k, lanes] += dot(probs.astype(BF16), d_out, NN)
                    d_probs = dot(values, d_out, NT)
                    d_scores = (probs * (d_probs - delta[h, :1, where_q])).astype(BF16)
                    acc[0, where_k, lanes] += dot(d_scores, query, NN) * scale
                    dq_ref[where_q, lanes] += dot(d_scores, keys, TN) * scale
                return carry

            return lax.fori_loop(0, nk, over_keys, carry)

        lax.fori_loop(0, nq, over_queries, 0)

    def work(number):
        @pl.when(number < c)
        def _():
            update(number, False)
            part[pl.ds(number, 1)] = acc[...].astype(BF16)[None]

        @pl.when(number > c)
        def _():
            part[pl.ds(number, 1)] = jnp.zeros_like(part[pl.ds(number, 1)])

    half = span // 2
    lo, hi = pl.ds(0, half), pl.ds(half, half)

    def sent(k, src, dst, peer):
        return remote(src, dst, send.at[k], recv.at[k], peer)

    work(bd)
    copies = [
        sent(0, part.at[bd, :, lo], got.at[0, :, lo], xn),
        sent(1, part.at[bd, :, hi], got.at[0, :, hi], yn),
    ]
    for copy in copies:
        copy.start()
    work(bx)
    sent(1, part.at[bx, :, hi], got.at[0, :, hi], yn).wait_recv()
    part[bx, :, half:, :] = (
        part[bx, :, half:, :].astype(F32) + got[0, :, half:, :].astype(F32)
    ).astype(BF16)
    more = [sent(2, part.at[bx], got.at[1], xn)]
    more[0].start()
    copies += more
    work(by)
    sent(0, part.at[by, :, lo], got.at[0, :, lo], xn).wait_recv()
    part[by, :, :half, :] = (
        part[by, :, :half, :].astype(F32) + got[0, :, :half, :].astype(F32)
    ).astype(BF16)
    more = [sent(3, part.at[by], got.at[2], yn)]
    more[0].start()
    copies += more
    update(c, True)
    sent(2, part.at[bx], got.at[1], xn).wait_recv()
    sent(3, part.at[by], got.at[2], yn).wait_recv()
    dkv_ref[...] = acc[...] + got[1].astype(F32) + got[2].astype(F32)
    for copy in copies:
        copy.wait_send()


def attend_back(q, kvall, d_out, attn32, lse, bound):
    span, cols = q.shape
    heads = cols // HEAD_DIM
    return pl.pallas_call(
        attend_back_kernel,
        out_shape=(shape((span, cols), F32), shape((2, span, cols), F32)),
        in_specs=[VM] * 6,
        out_specs=(VM, VM),
        scratch_shapes=[
            pltpu.VMEM((4, 2, span, cols), BF16),
            pltpu.VMEM((3, 2, span, cols), BF16),
            pltpu.VMEM((2, span, cols), F32),
            pltpu.VMEM((heads, 8, span), F32),
            pltpu.SemaphoreType.DMA((4,)),
            pltpu.SemaphoreType.DMA((4,)),
        ],
        compiler_params=pltpu.CompilerParams(
            collective_id=3, has_side_effects=True, vmem_limit_bytes=VMEM_LIMIT
        ),
        cost_estimate=pl.CostEstimate(
            flops=50 * 10**9, bytes_accessed=10**7, transcendentals=0
        ),
        name="attend_back",
    )(q, kvall, d_out, attn32, lse, bound)


def load_blocks(src, dst, sem, axis):
    blocks = src.shape[0]
    size = dst.shape[axis] // blocks
    copies = []
    for b in range(blocks):
        where = [slice(None)] * len(dst.shape)
        where[axis] = pl.ds(b * size, size)
        copies.append(pltpu.make_async_copy(src.at[b], dst.at[tuple(where)], sem.at[b]))
    for copy in copies:
        copy.start()
    return copies


def wait_all(copies):
    for copy in copies:
        copy.wait()


def mlp_in_kernel(
    n,
    attn_ref,
    wo_ref,
    x_ref,
    gain_ref,
    wg_ref,
    branch_ref,
    resid_ref,
    group_out,
    gate_ref,
    up_ref,
    hidden_ref,
    wo,
    wg,
    group,
    part,
    from_l,
    from_r,
    sem_o,
    sem_g,
    keep_sem,
    *sems,
):
    s, c, u = where_am_i()
    rows, width = x_ref.shape
    load_o = load_blocks(wo_ref, wo, sem_o, 1)
    load_g = load_blocks(wg_ref, wg, sem_g, 1)
    greet(line_peers(n))
    wait_all(load_o)
    chunk_cols = width // part.shape[0]
    span = n * rows
    count, size = tiles(span, 512)

    def compute(chunk):
        def tile(i, carry):
            where = pl.ds(pl.multiple_of(i * size, size), size)
            part[chunk, where, :] = dot(
                attn_ref[where, :], wo[:, chunk * chunk_cols : (chunk + 1) * chunk_cols], NN
            ).astype(BF16)
            return carry

        lax.fori_loop(0, count, tile, 0)

    LineReduce(n, rows, part, from_l, from_r, sems[:4]).run(compute, branch_ref)
    branch = branch_ref[...]
    resid = x_ref[...].astype(F32) + branch * inverse_rms(branch) * gain_ref[0:1, :]
    resid_ref[...] = resid
    group[rows_of(u, rows), :] = resid.astype(BF16)
    LineGather(n, rows, group, sems[4:]).run()
    keep = pltpu.make_async_copy(group, group_out, keep_sem)
    keep.start()
    wait_all(load_g)
    ntile, tsize = tiles(gate_ref.shape[1], 512)

    def body(i, carry):
        lanes = pl.ds(pl.multiple_of(i * tsize, tsize), tsize)

        def tile(j, carry):
            where = pl.ds(pl.multiple_of(j * size, size), size)
            gate = dot(group[where, :], wg[0, :, lanes], NN)
            up = dot(group[where, :], wg[1, :, lanes], NN)
            gate_ref[where, lanes] = gate.astype(BF16)
            up_ref[where, lanes] = up.astype(BF16)
            hidden_ref[where, lanes] = (gate * jax.nn.sigmoid(gate) * up).astype(BF16)
            return carry

        return lax.fori_loop(0, count, tile, carry)

    lax.fori_loop(0, ntile, body, 0)
    keep.wait()


def reduce_scratch(n, rows, width):
    dims = (CHUNKS, n * rows, width // CHUNKS)
    return [pltpu.VMEM(dims, BF16)] * 3


def mlp_in(n, attn, wo, x, gain, wg):
    rows, width = x.shape
    span, cols = attn.shape
    ff = wg.shape[3]
    return pl.pallas_call(
        functools.partial(mlp_in_kernel, n),
        out_shape=(
            shape((rows, width), F32),
            shape((rows, width), F32),
            shape((span, width), BF16),
            shape((span, ff), BF16),
            shape((span, ff), BF16),
            shape((span, ff), BF16),
        ),
        in_specs=[VM, HB, VM, VM, HB],
        out_specs=(VM, VM, HB, VM, VM, VM),
        scratch_shapes=[
            pltpu.VMEM((cols, width), BF16),
            pltpu.VMEM((2, width, ff), BF16),
            pltpu.VMEM((span, width), BF16),
        ]
        + reduce_scratch(n, rows, width)
        + [
            pltpu.SemaphoreType.DMA((8,)),
            pltpu.SemaphoreType.DMA((8,)),
            pltpu.SemaphoreType.DMA,
        ]
        + line_sems(n, CHUNKS)
        + line_sems(n),
        compiler_params=pltpu.CompilerParams(
            collective_id=4, has_side_effects=True, vmem_limit_bytes=VMEM_LIMIT
        ),
        cost_estimate=pl.CostEstimate(
            flops=80 * 10**9, bytes_accessed=10**7, transcendentals=0
        ),
        name="mlp_in",
    )(attn, wo, x, gain, wg)


def mlp_out_kernel(
    n,
    hidden_ref,
    wd_ref,
    resid_ref,
    gain_ref,
    cot_ref,
    gate_ref,
    up_ref,
    out_ref,
    group_out,
    dgu_ref,
    dgain_ref,
    wd,
    mlp,
    group,
    part,
    from_l,
    from_r,
    sem_d,
    keep_sem,
    *sems,
):
    s, c, u = where_am_i()
    rows, width = resid_ref.shape
    load_d = load_blocks(wd_ref, wd, sem_d, 1)
    greet(line_peers(n))
    wait_all(load_d)
    chunk_cols = width // part.shape[0]
    span = n * rows
    count, size = tiles(span, 512)

    def compute(chunk):
        def tile(i, carry):
            where = pl.ds(pl.multiple_of(i * size, size), size)
            part[chunk, where, :] = dot(
                hidden_ref[where, :], wd[:, chunk * chunk_cols : (chunk + 1) * chunk_cols], NN
            ).astype(BF16)
            return carry

        lax.fori_loop(0, count, tile, 0)

    LineReduce(n, rows, part, from_l, from_r, sems[:4]).run(compute, mlp)
    values = mlp[...]
    inverse = inverse_rms(values)
    grad = cot_ref[...].astype(F32)
    d_mlp = norm_back(values, inverse, grad * gain_ref[1:2, :], width)
    group[rows_of(u, rows), :] = d_mlp.astype(BF16)
    gather = LineGather(n, rows, group, sems[4:])
    gather.send(0)
    scaled = values * inverse
    out_ref[...] = (resid_ref[...] + scaled * gain_ref[1:2, :]).astype(BF16)
    dgain_ref[...] = jnp.sum(grad * scaled, axis=0, keepdims=True)
    for slot in range(n - 1):
        gather.wait(slot)
    gather.finish()
    keep = pltpu.make_async_copy(group, group_out, keep_sem)
    keep.start()
    ntile, tsize = tiles(gate_ref.shape[1], 512)

    def body(i, carry):
        lanes = pl.ds(pl.multiple_of(i * tsize, tsize), tsize)

        def tile(j, carry):
            where = pl.ds(pl.multiple_of(j * size, size), size)
            d_hidden = dot(group[where, :], wd[lanes, :], NT)
            gate = gate_ref[where, lanes].astype(F32)
            up = up_ref[where, lanes].astype(F32)
            sig = jax.nn.sigmoid(gate)
            slope = sig * (1.0 + gate * (1.0 - sig))
            dgu_ref[0, where, lanes] = (d_hidden * up * slope).astype(BF16)
            dgu_ref[1, where, lanes] = (d_hidden * (gate * sig)).astype(BF16)
            return carry

        return lax.fori_loop(0, count, tile, carry)

    lax.fori_loop(0, ntile, body, 0)
    keep.wait()


def mlp_out(n, hidden, wd, resid, gain, cot, gate, up):
    rows, width = resid.shape
    span, ff = hidden.shape
    return pl.pallas_call(
        functools.partial(mlp_out_kernel, n),
        out_shape=(
            shape((rows, width), BF16),
            shape((span, width), BF16),
            shape((2, span, ff), BF16),
            shape((1, width), F32),
        ),
        in_specs=[VM, HB, VM, VM, VM, VM, VM],
        out_specs=(VM, HB, VM, VM),
        scratch_shapes=[
            pltpu.VMEM((ff, width), BF16),
            pltpu.VMEM((rows, width), F32),
            pltpu.VMEM((span, width), BF16),
        ]
        + reduce_scratch(n, rows, width)
        + [pltpu.SemaphoreType.DMA((8,)), pltpu.SemaphoreType.DMA]
        + line_sems(n, CHUNKS)
        + line_sems(n),
        compiler_params=pltpu.CompilerParams(
            collective_id=5, has_side_effects=True, vmem_limit_bytes=VMEM_LIMIT
        ),
        cost_estimate=pl.CostEstimate(
            flops=80 * 10**9, bytes_accessed=10**7, transcendentals=0
        ),
        name="mlp_out",
    )(hidden, wd, resid, gain, cot, gate, up)


def mlp_back_kernel(
    n,
    dgu_ref,
    wg_ref,
    cot_ref,
    branch_ref,
    gain_ref,
    wo_ref,
    dresid_ref,
    group_out,
    dattn_ref,
    dgain_ref,
    wo,
    wg,
    group,
    part,
    from_l,
    from_r,
    sem_o,
    sem_g,
    keep_sem,
    *sems,
):
    s, c, u = where_am_i()
    rows, width = cot_ref.shape
    load_g = load_blocks(wg_ref, wg, sem_g, 1)
    load_o = load_blocks(wo_ref, wo, sem_o, 1)
    greet(line_peers(n))
    wait_all(load_g)
    chunk_cols = width // part.shape[0]
    span = n * rows
    count, size = tiles(span, 512)

    def compute(chunk):
        cols = slice(chunk * chunk_cols, (chunk + 1) * chunk_cols)

        def tile(i, carry):
            where = pl.ds(pl.multiple_of(i * size, size), size)
            part[chunk, where, :] = (
                dot(dgu_ref[0, where, :], wg[0, cols, :], NT)
                + dot(dgu_ref[1, where, :], wg[1, cols, :], NT)
            ).astype(BF16)
            return carry

        lax.fori_loop(0, count, tile, 0)

    LineReduce(n, rows, part, from_l, from_r, sems[:4]).run(compute, dresid_ref)
    d_resid = dresid_ref[...] + cot_ref[...].astype(F32)
    dresid_ref[...] = d_resid
    branch = branch_ref[...]
    inverse = inverse_rms(branch)
    d_branch = norm_back(branch, inverse, d_resid * gain_ref[0:1, :], width)
    group[rows_of(u, rows), :] = d_branch.astype(BF16)
    gather = LineGather(n, rows, group, sems[4:])
    gather.send(0)
    dgain_ref[...] = jnp.sum(d_resid * branch * inverse, axis=0, keepdims=True)
    wait_all(load_o)
    for slot in range(n - 1):
        gather.wait(slot)
    gather.finish()
    keep = pltpu.make_async_copy(group, group_out, keep_sem)
    keep.start()

    def tile(j, carry):
        where = pl.ds(pl.multiple_of(j * size, size), size)
        dattn_ref[where, :] = dot(group[where, :], wo[...], NT).astype(BF16)
        return carry

    lax.fori_loop(0, count, tile, 0)
    keep.wait()


def mlp_back(n, dgu, wg, cot, branch, gain, wo):
    rows, width = branch.shape
    span, ff = dgu.shape[1:]
    cols = wo.shape[1]
    return pl.pallas_call(
        functools.partial(mlp_back_kernel, n),
        out_shape=(
            shape((rows, width), F32),
            shape((span, width), BF16),
            shape((span, cols), BF16),
            shape((1, width), F32),
        ),
        in_specs=[VM, HB, VM, VM, VM, HB],
        out_specs=(VM, HB, VM, VM),
        scratch_shapes=[
            pltpu.VMEM((cols, width), BF16),
            pltpu.VMEM((2, width, ff), BF16),
            pltpu.VMEM((span, width), BF16),
        ]
        + reduce_scratch(n, rows, width)
        + [
            pltpu.SemaphoreType.DMA((8,)),
            pltpu.SemaphoreType.DMA((8,)),
            pltpu.SemaphoreType.DMA,
        ]
        + line_sems(n, CHUNKS)
        + line_sems(n),
        compiler_params=pltpu.CompilerParams(
            collective_id=6, has_side_effects=True, vmem_limit_bytes=VMEM_LIMIT
        ),
        cost_estimate=pl.CostEstimate(
            flops=80 * 10**9, bytes_accessed=10**7, transcendentals=0
        ),
        name="mlp_back",
    )(dgu, wg, cot, branch, gain, wo)


def proj_back_kernel(
    n,
    dq_ref,
    dkv_ref,
    proj_ref,
    inv_ref,
    gain_ref,
    tab_ref,
    wq_ref,
    dresid_ref,
    out_ref,
    dproj_ref,
    dgain_ref,
    wq,
    tab,
    scaled_ref,
    total_ref,
    msg,
    part,
    from_l,
    from_r,
    local_sem,
    m_send,
    m_recv,
    *sems,
):
    s, c, u = where_am_i()
    rows, width = dresid_ref.shape
    span = n * rows
    load = [
        pltpu.make_async_copy(tab_ref.at[rows_of(c, span)], tab, local_sem.at[0]),
        pltpu.make_async_copy(wq_ref, wq, local_sem.at[1]),
    ]
    for copy in load:
        copy.start()
    greet(all_uly_peers(n))
    load[0].wait()
    cosine, sine = rope_factors(tab[...])
    heads = dq_ref.shape[1] // HEAD_DIM
    dots = []
    for i in range(2):
        inverse = inv_ref[:, i : i + 1]
        row_dot = jnp.zeros((span, 1), F32)
        for h in range(heads):
            cols = slice(h * HEAD_DIM, (h + 1) * HEAD_DIM)
            v = dq_ref[:, cols] if i == 0 else dkv_ref[0, :, cols]
            v = v * cosine - pltpu.roll(v, HALF, 1) * sine
            values = proj_ref[i, :, cols]
            dgain_ref[i : i + 1, cols] = jnp.sum(v * values * inverse, axis=0, keepdims=True)
            v = v * gain_ref[i : i + 1, cols]
            scaled_ref[i, :, cols] = v
            row_dot = row_dot + jnp.sum(values * v, axis=-1, keepdims=True)
        dots.append(row_dot)
    total = exchange_rows(n, to_rows(*dots), msg, m_send, m_recv)
    means = to_columns(total) / width
    total_ref[...] = means
    for i in range(2):
        inverse = inv_ref[:, i : i + 1]
        factor = inverse**3 * total_ref[:, i : i + 1]
        dproj_ref[i] = (inverse * scaled_ref[i] - proj_ref[i] * factor).astype(BF16)
    dproj_ref[2] = dkv_ref[1].astype(BF16)
    load[1].wait()
    chunk_cols = width // part.shape[0]
    count, size = tiles(span, 512)

    def compute(chunk):
        cols = slice(chunk * chunk_cols, (chunk + 1) * chunk_cols)

        def tile(i, carry):
            where = pl.ds(pl.multiple_of(i * size, size), size)
            part[chunk, where, :] = (
                dot(dproj_ref[0, where, :], wq[0, cols, :], NT)
                + dot(dproj_ref[1, where, :], wq[1, cols, :], NT)
                + dot(dproj_ref[2, where, :], wq[2, cols, :], NT)
            ).astype(BF16)
            return carry

        lax.fori_loop(0, count, tile, 0)

    LineReduce(n, rows, part, from_l, from_r, sems[:4]).run(compute, total_wide := sems[4])
    out_ref[...] = (dresid_ref[...] + total_wide[...]).astype(BF16)


def proj_back(n, dq, dkv, proj, inv, gain, table, wq, dresid):
    rows, width = dresid.shape
    span, cols = dq.shape
    return pl.pallas_call(
        functools.partial(proj_back_kernel, n),
        out_shape=(
            shape((rows, width), BF16),
            shape((3, span, cols), BF16),
            shape((2, cols), F32),
        ),
        in_specs=[VM, VM, VM, VM, VM, HB, HB, VM],
        out_specs=(VM, VM, VM),
        scratch_shapes=[
            pltpu.VMEM((3, width, cols), BF16),
            pltpu.VMEM((span, 128), F32),
            pltpu.VMEM((2, span, cols), F32),
            pltpu.VMEM((span, 128), F32),
            pltpu.VMEM((n, 8, span), F32),
        ]
        + reduce_scratch(n, rows, width)
        + [
            pltpu.SemaphoreType.DMA((2,)),
            pltpu.SemaphoreType.DMA((n - 1,)),
            pltpu.SemaphoreType.DMA((n - 1,)),
        ]
        + line_sems(n, CHUNKS)
        + [pltpu.VMEM((rows, width), F32)],
        compiler_params=pltpu.CompilerParams(
            collective_id=7, has_side_effects=True, vmem_limit_bytes=VMEM_LIMIT
        ),
        cost_estimate=pl.CostEstimate(
            flops=50 * 10**9, bytes_accessed=10**7, transcendentals=0
        ),
        name="proj_back",
    )(dq, dkv, proj, inv, gain, table, wq, dresid)


def rope_table(length):
    freqs = np.power(
        np.float32(ROPE_BASE), -(np.arange(HALF, dtype=np.float32) * 2.0 / HEAD_DIM)
    ).astype(np.float32)
    angles = (np.arange(length, dtype=np.float32)[:, None] * freqs[None, :]).astype(np.float64)
    return np.concatenate([np.cos(angles), np.sin(angles)], axis=1).astype(np.float32)


def on_device(
    n,
    table,
    tokens,
    segment_ids,
    qkv_weight,
    out_weight,
    gate_up,
    down_weight,
    qk_gain,
    post_gain,
    cotangent,
):
    x = tokens[0]
    width = x.shape[1]
    cot = cotangent[0]
    spread = ("slot", "ctx")
    wo = lax.all_gather(out_weight, spread, axis=0)
    wg = lax.all_gather(gate_up, spread, axis=0)
    wd = lax.all_gather(down_weight, spread, axis=0)
    table = jnp.asarray(table)
    group_x, wq, proj, q, kv, inv, zero = project(n, x, qkv_weight, table, qk_gain, segment_ids)
    kvall, attn, attn32, lse, bound = attend(q, kv, zero)
    branch, resid, group_resid, gate, up, hidden = mlp_in(n, attn, wo, x, post_gain, wg)
    block_out, group_dmlp, dgu, gain_mlp = mlp_out(n, hidden, wd, resid, post_gain, cot, gate, up)
    down_grad = dot(hidden, group_dmlp, TN).astype(BF16)
    d_resid, group_dbranch, d_attn, gain_attn = mlp_back(n, dgu, wg, cot, branch, post_gain, wo)
    gate_grad = jnp.einsum(
        "td,ctf->cdf", group_resid, dgu, preferred_element_type=F32
    ).astype(BF16)
    out_grad = dot(attn, group_dbranch, TN).astype(BF16)
    dq, dkv = attend_back(q, kvall, d_attn, attn32, lse, bound)
    input_grad, d_proj, gain_cols = proj_back(n, dq, dkv, proj, inv, qk_gain, table, wq, d_resid)
    qkv_grad = jnp.einsum(
        "td,cte->cde", group_x, d_proj, preferred_element_type=F32
    ).astype(BF16)
    local_cols = q.shape[1]
    gain_block = lax.dynamic_update_slice(
        jnp.zeros((2, width), F32), gain_cols, (0, lax.axis_index("uly") * local_cols)
    )
    gain_terms = jnp.concatenate([gain_block, gain_attn, gain_mlp], axis=0)
    gain_totals = lax.psum(gain_terms, "uly")

    def scatter(value, dim):
        return lax.psum_scatter(value, spread, scatter_dimension=dim, tiled=True).astype(F32)

    return (
        block_out[None],
        input_grad[None],
        scatter(qkv_grad, 1),
        scatter(out_grad, 1),
        scatter(gate_grad, 1),
        scatter(down_grad, 1),
        scatter(gain_totals, 1),
    )


def solution(mesh):
    n = mesh.shape["uly"]
    in_specs = (
        P("slot", ("ctx", "uly"), None),
        P("slot", ("ctx", "uly")),
        P(None, ("slot", "ctx"), "uly"),
        P("uly", ("slot", "ctx")),
        P(None, ("slot", "ctx"), "uly"),
        P("uly", ("slot", "ctx")),
        P(None, "uly"),
        P(),
        P("slot", ("ctx", "uly"), None),
    )
    out_specs = (
        P("slot", ("ctx", "uly"), None),
        P("slot", ("ctx", "uly"), None),
        P(None, ("slot", "ctx"), "uly"),
        P("uly", ("slot", "ctx")),
        P(None, ("slot", "ctx"), "uly"),
        P("uly", ("slot", "ctx")),
        P(None, ("slot", "ctx")),
    )

    def whole(tokens, *rest):
        table = rope_table(tokens.shape[1])
        return jax.shard_map(
            functools.partial(on_device, n, table),
            mesh=mesh,
            in_specs=in_specs,
            out_specs=out_specs,
            check_vma=False,
        )(tokens, *rest)

    return whole
```

time: 1260 us -> 885 us (0.70)
  waiting for transfers between devices: 910 us -> 321 us
  Pallas kernels: 0 us -> 475 us
  matrix products: 167 us -> 32.4 us
  local copies, waits for them, and re-layouts: 63.6 us -> 15.8 us
  other arithmetic: 47 us -> 4.51 us
  blocking collectives: 38.9 us -> 11.8 us
    pallas_call x0 -> x7, Pallas kernels: none -> 475 us  [the longest x1 95.2 us: mlp_in(): pl.pallas_call(functools.partial(mlp_in_kernel, n), out_shape=(shape((row...]
    all_gather x10 -> x3, waiting for transfers between devices: 401 us -> 33.6 us  [the longest x1 33.6 us: on_device(): wg = lax.all_gather(gate_up, spread, axis=0)]
    reduce_scatter x10 -> x4, waiting for transfers between devices: 495 us -> 285 us  [scatter(): lax.psum_scatter(value, spread, scatter_dimension=dim, tiled=True)]
    dot_general x40 -> x4, matrix products: 167 us -> 32.4 us  [the longest x1 14.6 us: on_device(): jnp.einsum('td,ctf->cdf', group_resid, dgu, preferred_element_type=F32)]
    reduce_sum x10 -> x0, other arithmetic: 20 us -> none  [the longest x4 13.7 us: forward_block(): run_sum = run_sum * factor + jnp.sum(weights, axis=-1)]
    unnamed x62 -> x24, local copies, waits for them, and re-layouts: 32.7 us -> 15 us
    all_gather x2 -> x0, blocking collectives: 15.5 us -> none  [the longest x1 8.01 us: share_keys(): lax.all_gather(seg_low, 'ctx', axis=0, tiled=True)]
  transfers between devices with their start and end apart: 21 -> 8, of which waited for: 20 -> 5; matrix products, arithmetic and copies ran while one was open for 11% -> 5% of each run, Pallas kernels for 0% -> 25%
where the time goes in v1:
time: 885 us; the launch traced here: 876 us
  Pallas kernels  475 us (54%)
  waiting for transfers between devices  321 us (36%)
  matrix products  32.4 us (4%)
  local copies, waits for them, and re-layouts  15.8 us (2%)
  between operations  14.7 us (2%)
  blocking collectives  11.8 us (1%)
    reduce_scatter x4, waiting for transfers between devices, scatter(): lax.psum_scatter(value, spread, scatter_dimension=dim, tiled=True)  285 us
    pallas_call x1, Pallas kernels, mlp_in(): pl.pallas_call(functools.partial(mlp_in_kernel, n), out_shape=(shape((row...  95.2 us
    pallas_call x1, Pallas kernels, mlp_out(): pl.pallas_call(functools.partial(mlp_out_kernel, n), out_shape=(shape((ro...  85.4 us
    pallas_call x1, Pallas kernels, mlp_back(): pl.pallas_call(functools.partial(mlp_back_kernel, n), out_shape=(shape((r...  84 us
    pallas_call x1, Pallas kernels, attend(): pl.pallas_call(attend_kernel, out_shape=(shape((4, 2, span, cols), BF16),...  71.4 us
    pallas_call x1, Pallas kernels, project(): pl.pallas_call(functools.partial(proj_kernel, n), out_shape=(shape((span,...  53.9 us
    pallas_call x1, Pallas kernels, attend_back(): pl.pallas_call(attend_back_kernel, out_shape=(shape((span, cols), F32), s...  43 us
    pallas_call x1, Pallas kernels, proj_back(): pl.pallas_call(functools.partial(proj_back_kernel, n), out_shape=(shape((...  42.6 us
  transfers between devices with their start and end apart: 8, of which 5 were waited for; matrix products, arithmetic and copies ran while one was open for 5% of the time, Pallas kernels for 25%

profile of v1, /device:TPU:0, one launch (start us, length us, event | category | flops | bytes accessed | tf_op | source)
XLA Modules:
  0.0 875.8 jit_solution(12327602045838621446)
XLA Ops:
  9.4 53.9 %project.1 = (bf16[512,2048]{1,0:T(8,128)(2,1)}, bf16[3,2048,512]{2,1,0:T(8,128)(2,1)}, f32[2,512,512]{2,1,0:T(8,128)}, bf16[512,512]{1,0:T(8,128)(2,1)}, bf16[2...) custom-call(bf16[128,2048]{1,0:T(8,128)(2,1)} %bitcast.34, bf16[3,256,512]{2,1,0:T(8,128)(2,1)} %w_ref.1, ...), custom_call_target="tpu_custom_call" | custom-call | flops 40000000000 | bytes 10000000 | tf_op jit(solution)/shard_map/project/pallas_call | solution.py:445
  63.3 71.4 %attend.1 = (bf16[4,2,512,512]{3,2,1,0:T(8,128)(2,1)}, bf16[512,512]{1,0:T(8,128)(2,1)}, f32[512,512]{1,0:T(8,128)}, f32[4,8,512]{2,1,0:T(8,128)}, s32[8,128]{1,0:T(8,128)}) custom-call(bf16[512,512]{1,0:T(8,128)(2,1)} %get-tuple-element.38.q_ref, bf16[2,512,512]{2,1,0:T(8,128)(2,1)} %get-tuple-element.39.kv_ref, f32[8,128]{1,0:T(8,128)} %get-tuple-element.40.zero_ref), custom_call_target="tpu_custom_call" | custom-call | flops 40000000000 | bytes 10000000 | tf_op jit(solution)/shard_map/attend/pallas_call | solution.py:620
  134.8 33.6 %all-gather.9.cloned.1.call-done = bf16[16,256,2048]{2,1,0:T(8,128)(2,1)} async-done(((bf16[2,256,2048]{2,1,0:T(8,128)(2,1)}), bf16[16,256,2048]{2,1,0:T(8,128)(2,1)}) %all-gather.9.cloned.1.call-update) | async-done | bytes 16777232 | tf_op jit(solution)/shard_map/all_gather | solution.py:1290
  168.4 95.2 %mlp_in.1 = (f32[128,2048]{1,0:T(8,128)}, f32[128,2048]{1,0:T(8,128)}, bf16[512,2048]{1,0:T(8,128)(2,1)}, bf16[512,2048]{1,0:T(8,128)(2,1)}, bf16[512,2048]{1,0:T(8,128)(2,1)}, /*index=5*/bf16[512,2048]{1,0:T(8,128)(2,1)}) custom-call(bf16[512,512]{1,0:T(8,128)(2,1)} %get-tuple-element.41.attn_ref, bf16[8,512,256]{2,1,0:T(8,128)(2,1)} %bitcast.32, ...), custom_call_target="tpu_custom_call" | custom-call | flops 80000000000 | bytes 10000000 | tf_op jit(solution)/shard_map/mlp_in/pallas_call | solution.py:888
  263.6 85.4 %mlp_out.1 = (bf16[128,2048]{1,0:T(8,128)(2,1)}, bf16[512,2048]{1,0:T(8,128)(2,1)}, bf16[2,512,2048]{2,1,0:T(8,128)(2,1)}, f32[1,2048]{1,0:T(1,128)}) custom-call(bf16[512,2048]{1,0:T(8,128)(2,1)} %get-tuple-element.42.hidden_ref, bf16[8,2048,256]{2,1,0:T(8,128)(2,1)} %bitcast.31, f32[128,2048]{1,0:T(8,128)} %get-tuple-element.43.resid_ref, ...), custom_call_target="tpu_custom_call" | custom-call | flops 80000000000 | bytes 10000000 | tf_op jit(solution)/shard_map/mlp_out/pallas_call | solution.py:1006
  349.0 84.0 %mlp_back.1 = (f32[128,2048]{1,0:T(8,128)}, bf16[512,2048]{1,0:T(8,128)(2,1)}, bf16[512,512]{1,0:T(8,128)(2,1)}, f32[1,2048]{1,0:T(1,128)}) custom-call(bf16[2,512,2048]{2,1,0:T(8,128)(2,1)} %get-tuple-element.48.dgu_ref, bf16[8,2,256,2048]{3,2,1,0:T(8,128)(2,1)} %bitcast.30, bf16[128,2048]{1,0:T(8,128)(2,1)} %bitcast.37, ...), custom_call_target="tpu_custom_call" | custom-call | flops 80000000000 | bytes 10000000 | tf_op jit(solution)/shard_map/mlp_back/pallas_call | solution.py:1111
  433.0 43.0 %attend_back.1 = (f32[512,512]{1,0:T(8,128)}, f32[2,512,512]{2,1,0:T(8,128)}) custom-call(bf16[512,512]{1,0:T(8,128)(2,1)} %get-tuple-element.38.q_ref, bf16[4,2,512,512]{3,2,1,0:T(8,128)(2,1)} %get-tuple-element.47.kvall_ref, bf16[512,512]{1,0:T(8,128)(2,1)} %get-tuple-element.50.do_ref, f32[512,512]{1,0:T(8,128)} %get-tuple-element.51.attn32_ref, ...), custom_call_target="tpu_custom_call" | custom-call | flops 49999998976 | bytes 10000000 | tf_op jit(solution)/shard_map/attend_back/pallas_call | solution.py:765
  476.0 42.6 %proj_back.1 = (bf16[128,2048]{1,0:T(8,128)(2,1)}, bf16[3,512,512]{2,1,0:T(8,128)(2,1)}, f32[2,512]{1,0:T(2,128)}) custom-call(f32[512,512]{1,0:T(8,128)} %get-tuple-element.54.dq_ref, f32[2,512,512]{2,1,0:T(8,128)} %get-tuple-element.55.dkv_ref, f32[2,512,512]{2,1,0:T(8,128)} %get-tuple-element.56.proj_ref, f32[512,128]{1,0:T(8,128)} %get-tuple-element.57.inv_ref, ...), custom_call_target="tpu_custom_call" | custom-call | flops 49999998976 | bytes 10000000 | tf_op jit(solution)/shard_map/proj_back/pallas_call | solution.py:1230
  519.5 1.3 copy.27
  520.9 2.6 convolution_convert_fusion.1
  525.1 6.8 convert_bitcast_fusion.1
  532.0 1.6 copy-done.7
  533.6 8.4 convolution_convert_fusion
  542.0 1.5 copy-done.8
  543.6 14.6 %convert_bitcast_fusion = bf16[2,2048,2048]{1,2,0:T(8,128)(2,1)} fusion(bf16[2,512,2048]{2,1,0:T(8,128)(2,1)} %get-tuple-element.48.dgu_ref, bf16[512,2048]{1,0:T(8,128)(2,1)S(1)} %copy-done.8), kind=kOutput, calls=%fused_computation | convolution fusion | flops 8598323200 | bytes 23068672 | tf_op jit(solution)/shard_map/td,ctf->cdf/dot_general | solution.py:1299
  559.2 11.8 %psum.8 = f32[4,256]{1,0:T(4,128)} all-reduce(f32[4,256]{1,0:T(4,128)S(1)} %copy.28), channel_id=1, replica_groups=mesh['slot'=2,'ctx'=4,'uly'=4] {'uly'}, use_global_device_ids=true, to_apply=%region_4.0 | all-reduce | flops 1024 | bytes 8192 | tf_op jit(solution)/shard_map/psum | solution.py:1313
  571.1 31.7 %reduce-scatter.10.cloned.1.call-done = bf16[512,256]{1,0:T(8,128)(2,1)} async-done(((bf16[512,2048]{1,0:T(8,128)(2,1)}), bf16[512,256]{1,0:T(8,128)(2,1)}) %reduce-scatter.10.cloned.1.call-update) | async-done | bytes 262160 | tf_op jit(solution)/shard_map/reduce_scatter | solution.py:1316
  602.7 1.8 convert_element_type.34
  604.5 63.6 %reduce-scatter.8.cloned.1.call-done = bf16[3,256,512]{1,2,0:T(8,128)(2,1)} async-done(((bf16[3,2048,512]{1,2,0:T(8,128)(2,1)}), bf16[3,256,512]{1,2,0:T(8,128)(2,1)}) %reduce-scatter.8.cloned.1.call-update) | async-done | bytes 786448 | tf_op jit(solution)/shard_map/reduce_scatter | solution.py:1316
  668.1 2.6 copy.23
  670.7 72.2 %reduce-scatter.14.cloned.1.call-done = bf16[2048,256]{1,0:T(8,128)(2,1)} async-done(((bf16[2048,2048]{1,0:T(8,128)(2,1)}), bf16[2048,256]{1,0:T(8,128)(2,1)}) %reduce-scatter.14.cloned.1.call-update) | async-done | bytes 1048592 | tf_op jit(solution)/shard_map/reduce_scatter | solution.py:1316
  742.9 2.7 convert_element_type.39
  745.6 117.3 %reduce-scatter.12.cloned.1.call-done = bf16[2,256,2048]{1,2,0:T(8,128)(2,1)} async-done(((bf16[2,2048,2048]{1,2,0:T(8,128)(2,1)}), bf16[2,256,2048]{1,2,0:T(8,128)(2,1)}) %reduce-scatter.12.cloned.1.call-update) | async-done | bytes 2097168 | tf_op jit(solution)/shard_map/reduce_scatter | solution.py:1316
  862.8 4.1 copy.24
  (41 shorter events, 7.5 us)
Async XLA Ops:
  7.2 127.6 %all-gather.7.cloned.1.call-start = ((), (), s32[]{:S(2)}) async-start(), calls=%async_computation.9 | async-start | bytes 2359296 | tf_op jit(solution)/shard_map/all_gather | solution.py:1289
  7.9 160.5 %all-gather.9.cloned.1.call-start = ((), (), s32[]{:S(2)}) async-start(), calls=%async_computation.10 | async-start | bytes 18874368 | tf_op jit(solution)/shard_map/all_gather | solution.py:1290
  8.7 254.9 %all-gather.11.cloned.1.call-start = ((), (), s32[]{:S(2)}) async-start(), calls=%async_computation.11 | async-start | bytes 9437184 | tf_op jit(solution)/shard_map/all_gather | solution.py:1291
  9.4 548.8 %reduce-scatter.16.cloned.1.call-start = ((), (), s32[]{:S(2)}) async-start(), calls=%async_computation.12 | async-start | bytes 1179648
  476.0 43.5 %copy-start.2 = (f32[1,2048]{1,0:T(1,128)S(1)}, f32[1,2048]{1,0:T(1,128)}, u32[]{:S(2)}) copy-start(f32[1,2048]{1,0:T(1,128)} %get-tuple-element.68) | copy-start | bytes 24580
  476.0 43.5 %copy-start.3 = (f32[1,2048]{1,0:T(1,128)S(1)}, f32[1,2048]{1,0:T(1,128)}, u32[]{:S(2)}) copy-start(f32[1,2048]{1,0:T(1,128)} %get-tuple-element.67) | copy-start | bytes 24580
  476.0 44.9 %copy-start.5 = (bf16[512,512]{1,0:T(8,128)(2,1)S(1)}, bf16[512,512]{1,0:T(8,128)(2,1)}, u32[]{:S(2)}) copy-start(bf16[512,512]{1,0:T(8,128)(2,1)} %get-tuple-element.41.attn_ref) | copy-start | bytes 1572868
  518.6 2.3 copy-start.4
  520.9 81.9 %reduce-scatter.10.cloned.1.call-start = ((), (), s32[]{:S(2)}) async-start(), calls=%async_computation.6 | async-start | bytes 2359296 | tf_op jit(solution)/shard_map/reduce_scatter | solution.py:1316
  523.5 1.6 copy-start.6
  523.5 144.6 %reduce-scatter.8.cloned.1.call-start = ((), (), s32[]{:S(2)}) async-start(), calls=%async_computation.5 | async-start | bytes 7077888 | tf_op jit(solution)/shard_map/reduce_scatter | solution.py:1316
  531.9 1.7 copy-start.7
  531.9 210.9 %reduce-scatter.14.cloned.1.call-start = ((), (), s32[]{:S(2)}) async-start(), calls=%async_computation.8 | async-start | bytes 9437184 | tf_op jit(solution)/shard_map/reduce_scatter | solution.py:1316
  542.0 1.6 copy-start.8
  542.0 320.8 %reduce-scatter.12.cloned.1.call-start = ((), (), s32[]{:S(2)}) async-start(), calls=%async_computation.7 | async-start | bytes 18874368 | tf_op jit(solution)/shard_map/reduce_scatter | solution.py:1316
  745.6 121.4 %copy-start = (bf16[128,2048]{1,0:T(8,128)(2,1)S(1)}, bf16[128,2048]{1,0:T(8,128)(2,1)}, u32[]{:S(2)}) copy-start(bf16[128,2048]{1,0:T(8,128)(2,1)} %get-tuple-element.46) | copy-start | bytes 1572868
  745.6 122.2 %copy-start.1 = (bf16[128,2048]{1,0:T(8,128)(2,1)S(1)}, bf16[128,2048]{1,0:T(8,128)(2,1)}, u32[]{:S(2)}) copy-start(bf16[128,2048]{1,0:T(8,128)(2,1)} %get-tuple-element.60) | copy-start | bytes 1572868
Sparse Core Ops, SparseCore 0:
  9.9 37.3 all-gather.6
  49.1 119.2 all-gather.8
  170.3 53.7 all-gather.10
  521.0 36.7 reduce-scatter.15
  561.5 41.1 reduce-scatter.9
  606.3 61.7 reduce-scatter.7
  671.6 71.2 reduce-scatter.13
  746.8 115.9 reduce-scatter.11

commit v2 on v1

--- a/solution.py
+++ b/solution.py
@@ -18,7 +18,7 @@
 MESH_ID = pl.DeviceIdType.MESH
 BF16 = jnp.bfloat16
 F32 = jnp.float32
-VMEM_LIMIT = 60 * 1024 * 1024
+VMEM_LIMIT = 62 * 1024 * 1024
 CHUNKS = 4
 
 VM = pl.BlockSpec(memory_space=pltpu.VMEM)
@@ -129,17 +129,18 @@
             def _():
                 self.copy(False, slot, u + slot).wait_send()
 
-    def run(self):
-        self.send(0)
+    def run(self, hook=None):
         for slot in range(self.n - 1):
             self.wait(slot)
+            if hook is not None:
+                hook(slot)
         self.finish()
 
 
 class LineReduce:
-    def __init__(self, n, rows, part, from_l, from_r, sems):
+    def __init__(self, n, rows, part, got, sems):
         self.n, self.rows, self.sems = n, rows, sems
-        self.part, self.from_l, self.from_r = part, from_l, from_r
+        self.part, self.got = part, got
         self.chunks = part.shape[0]
 
     def copy(self, right, slot, chunk, block):
@@ -150,23 +151,24 @@
         if right:
             return remote(
                 src,
-                self.from_l.at[chunk, where],
+                self.got.at[chunk, rows_of(block + 1, self.rows)],
                 send_r.at[slot, chunk],
                 recv_r.at[slot, chunk],
                 (s, c, u + 1),
             )
         return remote(
             src,
-            self.from_r.at[chunk, where],
+            self.got.at[chunk, where],
             send_l.at[slot, chunk],
             recv_l.at[slot, chunk],
             (s, c, u - 1),
         )
 
-    def add(self, chunk, block, source):
+    def add(self, chunk, block, place):
         where = rows_of(block, self.rows)
         self.part[chunk, where, :] = (
-            self.part[chunk, where, :].astype(F32) + source[chunk, where, :].astype(F32)
+            self.part[chunk, where, :].astype(F32)
+            + self.got[chunk, rows_of(place, self.rows), :].astype(F32)
         ).astype(BF16)
 
     def step(self, slot, chunk):
@@ -181,7 +183,7 @@
                 @pl.when(u > 0)
                 def _():
                     self.copy(True, slot - 1, chunk, block_r).wait_recv()
-                    self.add(chunk, block_r, self.from_l)
+                    self.add(chunk, block_r, block_r + 1)
 
             self.copy(True, slot, chunk, block_r).start()
 
@@ -192,7 +194,7 @@
                 @pl.when(u < n - 1)
                 def _():
                     self.copy(False, slot - 1, chunk, block_l).wait_recv()
-                    self.add(chunk, block_l, self.from_r)
+                    self.add(chunk, block_l, block_l)
 
             self.copy(False, slot, chunk, block_l).start()
 
@@ -207,12 +209,12 @@
             @pl.when(u > 0)
             def _():
                 self.copy(True, n - 2, chunk, u).wait_recv()
-                out[:, cols] += self.from_l[chunk, where, :].astype(F32)
+                out[:, cols] += self.got[chunk, rows_of(u + 1, self.rows), :].astype(F32)
 
             @pl.when(u < n - 1)
             def _():
                 self.copy(False, n - 2, chunk, u).wait_recv()
-                out[:, cols] += self.from_r[chunk, where, :].astype(F32)
+                out[:, cols] += self.got[chunk, where, :].astype(F32)
 
     def finish(self):
         u, n = lax.axis_index("uly"), self.n
@@ -227,14 +229,261 @@
                 def _():
                     self.copy(False, slot, chunk, slot - (n - 1) + u).wait_send()
 
-    def run(self, compute, out):
+    def run(self, compute, out, hook=None):
         for slot in range(self.n - 1):
             for chunk in range(self.chunks):
                 if slot == 0:
                     compute(chunk)
                 self.step(slot, chunk)
+            if hook is not None:
+                hook(slot)
         self.last(out)
         self.finish()
+
+
+class PlaneGather:
+    SEMS = 9
+
+    def __init__(self, src, block, half_rows, send, recv, local):
+        self.s, self.c, self.u = where_am_i()
+        self.src, self.block, self.half_rows = src, block, half_rows
+        self.send_sem, self.recv_sem = send, recv
+        s, c, u = self.s, self.c, self.u
+        self.xn, self.yn, self.sib = (s, c ^ 1, u), (s, c ^ 2, u), (1 - s, c, u)
+        self.started = []
+        self.own = pltpu.make_async_copy(src, block(s * 4 + c), local)
+
+    def half(self, b, part):
+        rows = self.half_rows
+        view = self.block(b)
+        where = [slice(None)] * len(view.shape)
+        where[-2] = pl.ds(part * rows, rows)
+        return view.at[tuple(where)]
+
+    def copy(self, k, view, peer, src=None):
+        return remote(
+            view if src is None else src, view, self.send_sem.at[k], self.recv_sem.at[k], peer
+        )
+
+    def go(self, *copies):
+        for copy in copies:
+            copy.start()
+            self.started.append(copy)
+
+    def start(self):
+        own = self.block(self.s * 4 + self.c)
+        self.go(
+            self.copy(0, own, self.xn, self.src),
+            self.copy(1, own, self.yn, self.src),
+            self.copy(2, own, self.sib, self.src),
+        )
+        self.own.start()
+
+    def middle(self):
+        bx, by = self.s * 4 + (self.c ^ 1), self.s * 4 + (self.c ^ 2)
+        self.copy(0, self.block(bx), self.xn).wait_recv()
+        self.go(
+            self.copy(3, self.half(bx, 0), self.yn), self.copy(4, self.block(bx), self.sib)
+        )
+        self.copy(1, self.block(by), self.yn).wait_recv()
+        self.go(
+            self.copy(5, self.half(by, 1), self.xn), self.copy(6, self.block(by), self.sib)
+        )
+
+    def corner(self):
+        bd = self.s * 4 + (self.c ^ 3)
+        self.copy(3, self.half(bd, 0), self.yn).wait_recv()
+        self.go(self.copy(7, self.half(bd, 0), self.sib))
+        self.copy(5, self.half(bd, 1), self.xn).wait_recv()
+        self.go(self.copy(8, self.half(bd, 1), self.sib))
+
+    def arrive(self):
+        far, c = (1 - self.s) * 4, self.c
+        self.copy(2, self.block(far + c), self.sib).wait_recv()
+        self.copy(4, self.block(far + (c ^ 1)), self.sib).wait_recv()
+        self.copy(6, self.block(far + (c ^ 2)), self.sib).wait_recv()
+        self.copy(7, self.half(far + (c ^ 3), 0), self.sib).wait_recv()
+        self.copy(8, self.half(far + (c ^ 3), 1), self.sib).wait_recv()
+        self.own.wait()
+
+    def finish(self):
+        for copy in self.started:
+            copy.wait_send()
+
+
+class PlaneReduce:
+    SEMS = 6
+
+    def __init__(self, ring, got, outs, place, send, recv, local):
+        self.s, self.c, self.u = where_am_i()
+        s, c, u = self.s, self.c, self.u
+        self.xn, self.yn = (s, c ^ 1, u), (s, c ^ 2, u)
+        self.ring, self.got, self.outs, self.place = ring, got, outs, place
+        self.send_sem, self.recv_sem, self.local = send, recv, local
+        self.slots, self.rows = ring.shape[0], ring.shape[2]
+        self.open = {}
+
+    def halves(self):
+        h = self.rows // 2
+        return pl.ds(0, h), pl.ds(h, h)
+
+    def copy(self, piece, k, src, dst, peer):
+        return remote(src, dst, self.send_sem.at[piece, k], self.recv_sem.at[piece, k], peer)
+
+    def slot(self, piece):
+        if piece >= self.slots:
+            self.close(piece - self.slots)
+        return self.ring.at[piece % self.slots]
+
+    def close(self, piece):
+        if piece in self.open:
+            remotes, own = self.open.pop(piece)
+            for copy in remotes:
+                copy.wait_send()
+            own.wait()
+
+    def first(self, piece):
+        c = self.c
+        lo, hi = self.halves()
+        blocks = self.ring.at[piece % self.slots]
+        own_out, out_x, out_y = self.outs
+        bx, by, bd = c ^ 1, c ^ 2, c ^ 3
+        copies = [
+            self.copy(piece, 0, blocks.at[bd, lo], self.got.at[piece, lo], self.xn),
+            self.copy(piece, 1, blocks.at[bd, hi], self.got.at[piece, hi], self.yn),
+            self.copy(piece, 2, blocks.at[bx, lo], self.place(out_x, piece, 0), self.xn),
+            self.copy(piece, 3, blocks.at[by, hi], self.place(out_y, piece, 1), self.yn),
+        ]
+        for copy in copies:
+            copy.start()
+        own = pltpu.make_async_copy(
+            blocks.at[c], self.place(own_out, piece, None), self.local.at[piece]
+        )
+        own.start()
+        self.open[piece] = (copies, own)
+
+    def second(self, piece):
+        c, h = self.c, self.rows // 2
+        lo, hi = self.halves()
+        slot = piece % self.slots
+        blocks = self.ring.at[slot]
+        own_out, out_x, out_y = self.outs
+        bx, by, bd = c ^ 1, c ^ 2, c ^ 3
+        self.copy(piece, 0, blocks.at[bd, lo], self.got.at[piece, lo], self.xn).wait_recv()
+        self.ring[slot, by, :h, :] = (
+            self.ring[slot, by, :h, :].astype(F32) + self.got[piece, :h, :].astype(F32)
+        ).astype(BF16)
+        first = self.copy(piece, 4, blocks.at[by, lo], self.place(out_y, piece, 0), self.yn)
+        first.start()
+        self.copy(piece, 1, blocks.at[bd, hi], self.got.at[piece, hi], self.yn).wait_recv()
+        self.ring[slot, bx, h:, :] = (
+            self.ring[slot, bx, h:, :].astype(F32) + self.got[piece, h:, :].astype(F32)
+        ).astype(BF16)
+        second = self.copy(piece, 5, blocks.at[bx, hi], self.place(out_x, piece, 1), self.xn)
+        second.start()
+        self.open[piece][0].extend([first, second])
+
+    def finish(self, pieces):
+        own_out, out_x, out_y = self.outs
+        slot = self.ring.at[0]
+        lo, hi = self.halves()
+        for piece in range(pieces):
+            self.close(piece)
+            for k, out, half, peer in (
+                (2, out_x, 0, self.xn),
+                (3, out_y, 1, self.yn),
+                (4, out_y, 0, self.yn),
+                (5, out_x, 1, self.xn),
+            ):
+                where = self.place(out, piece, half)
+                self.copy(piece, k, where, where, peer).wait_recv()
+
+
+class Pieces:
+    def __init__(self, work):
+        self.work, self.done, self.behind = work, 0, []
+
+    def step(self, count=1):
+        for _ in range(count):
+            if self.done < len(self.work):
+                plane, piece, compute = self.work[self.done]
+                compute(plane.slot(piece), piece)
+                plane.first(piece)
+                self.behind.append((plane, piece))
+                self.done += 1
+                if len(self.behind) > 2:
+                    self.catch_up()
+
+    def catch_up(self):
+        plane, piece = self.behind.pop(0)
+        plane.second(piece)
+
+    def finish(self):
+        self.step(len(self.work))
+        while self.behind:
+            self.catch_up()
+
+
+def wide_piece(own, other, lanes):
+    def compute(out, piece):
+        take = lanes(piece)
+        cols = out.shape[2]
+
+        def pair(i, carry):
+            where = pl.ds(pl.multiple_of(i * 2 * cols, 2 * cols), 2 * cols)
+            total = dot(own[0][:, take], own[1][:, where], TN) + dot(
+                other[0][:, take], other[1][:, where], TN
+            )
+            total = total.astype(BF16)
+            out[pl.ds(2 * i, 1)] = total[:, :cols][None]
+            out[pl.ds(2 * i + 1, 1)] = total[:, cols:][None]
+            return carry
+
+        lax.fori_loop(0, 2, pair, 0)
+
+    return compute
+
+
+def tall_piece(own, other, right):
+    def compute(out, piece):
+        rows, cols = out.shape[1:]
+
+        def pair(i, carry):
+            where = pl.ds(pl.multiple_of(i * 2 * rows, 2 * rows), 2 * rows)
+            total = dot(own[0][:, where], right(own[1], piece), TN) + dot(
+                other[0][:, where], right(other[1], piece), TN
+            )
+            out[pl.ds(2 * i, 2)] = total.astype(BF16).reshape(2, rows, cols)
+            return carry
+
+        lax.fori_loop(0, 2, pair, 0)
+
+    return compute
+
+
+def half_columns(ref, s):
+    half = ref.shape[1] // 2
+    return ref.at[:, pl.ds(pl.multiple_of(s * half, half), half)]
+
+
+class Sibling:
+    def __init__(self, send, recv):
+        s, c, u = where_am_i()
+        self.peer, self.send, self.recv = (1 - s, c, u), send, recv
+        self.copies = []
+
+    def start(self, src, dst):
+        k = len(self.copies)
+        copy = remote(src, dst, self.send.at[k], self.recv.at[k], self.peer)
+        copy.start()
+        self.copies.append(copy)
+
+    def wait(self, k):
+        self.copies[k].wait_recv()
+
+    def finish(self):
+        for copy in self.copies:
+            copy.wait_send()
 
 
 def dot(a, b, dims):
@@ -312,8 +561,12 @@
     tab_ref,
     gain_ref,
     seg_ref,
+    wo_ref,
+    gu_ref,
     xg_out,
     wq_out,
+    wo_out,
+    wga_out,
     proj_ref,
     q_ref,
     kv_ref,
@@ -334,68 +587,39 @@
     rows, width = x_ref.shape
     span = n * rows
     kb = w_ref.shape[1]
-    sib, xn, yn = (1 - s, c, u), (s, c ^ 1, u), (s, c ^ 2, u)
+    sib = (1 - s, c, u)
     tab_copy = pltpu.make_async_copy(tab_ref.at[rows_of(c, span)], tab, local_sem.at[0])
     tab_copy.start()
-    own_block = s * 4 + c
-    own_copy = pltpu.make_async_copy(w_ref, wq.at[:, rows_of(own_block, kb)], local_sem.at[1])
-    own_copy.start()
     xg[rows_of(u, rows), :] = x_ref[...]
     greet(all_uly_peers(n) + plane_peers() + [(None, sib)])
 
-    def block(b):
-        return wq.at[:, rows_of(b, kb)]
-
-    def half(b, part):
-        return wq.at[:, pl.ds(pl.multiple_of(b * kb + part * (kb // 2), kb // 2), kb // 2)]
-
-    def sent(k, src, dst, peer):
-        return remote(src, dst, w_send.at[k], w_recv.at[k], peer)
-
-    bx, by, bd = s * 4 + (c ^ 1), s * 4 + (c ^ 2), s * 4 + (c ^ 3)
+    def plane(k, src, block, half_rows):
+        return PlaneGather(
+            src, block, half_rows, w_send.at[k], w_recv.at[k], local_sem.at[3 + k]
+        )
+
+    half = kb // 2
     gather = LineGather(n, rows, xg, line)
+    first = plane(0, w_ref, lambda b: wq.at[:, rows_of(b, kb)], half)
+    second = plane(1, wo_ref, lambda b: wo_out.at[b], wo_ref.shape[0] // 2)
+    third = plane(2, gu_ref.at[0, pl.ds(0, half)], lambda b: wga_out.at[b], half // 2)
     gather.send(0)
-    copies = [
-        sent(0, w_ref, block(own_block), xn),
-        sent(1, w_ref, block(own_block), yn),
-        sent(2, w_ref, block(own_block), sib),
-    ]
-    for copy in copies:
-        copy.start()
+    first.start()
     gather.wait(0)
-    sent(0, block(bx), block(bx), xn).wait_recv()
-    more = [sent(3, half(bx, 0), half(bx, 0), yn), sent(4, block(bx), block(bx), sib)]
-    for copy in more:
-        copy.start()
-    copies += more
-    sent(1, block(by), block(by), yn).wait_recv()
-    more = [sent(5, half(by, 1), half(by, 1), xn), sent(6, block(by), block(by), sib)]
-    for copy in more:
-        copy.start()
-    copies += more
+    first.middle()
+    second.start()
     if n > 2:
         gather.wait(1)
-    sent(3, half(bd, 0), half(bd, 0), yn).wait_recv()
-    more = [sent(7, half(bd, 0), half(bd, 0), sib)]
-    more[0].start()
-    copies += more
-    sent(5, half(bd, 1), half(bd, 1), xn).wait_recv()
-    more = [sent(8, half(bd, 1), half(bd, 1), sib)]
-    more[0].start()
-    copies += more
+    first.corner()
+    second.middle()
+    third.start()
     for slot in range(2 if n > 2 else 1, n - 1):
         gather.wait(slot)
-    far = (1 - s) * 4
-    sent(2, block(far + c), block(far + c), sib).wait_recv()
-    sent(4, block(far + (c ^ 1)), block(far + (c ^ 1)), sib).wait_recv()
-    sent(6, block(far + (c ^ 2)), block(far + (c ^ 2)), sib).wait_recv()
-    sent(7, half(far + (c ^ 3), 0), half(far + (c ^ 3), 0), sib).wait_recv()
-    sent(8, half(far + (c ^ 3), 1), half(far + (c ^ 3), 1), sib).wait_recv()
-    own_copy.wait()
+    first.arrive()
     tab_copy.wait()
     keep = [
-        pltpu.make_async_copy(xg, xg_out, local_sem.at[2]),
-        pltpu.make_async_copy(wq, wq_out, local_sem.at[3]),
+        pltpu.make_async_copy(xg, xg_out, local_sem.at[1]),
+        pltpu.make_async_copy(wq, wq_out, local_sem.at[2]),
     ]
     for copy in keep:
         copy.start()
@@ -416,6 +640,8 @@
     zeros = jnp.sum((1 - seg_ref[...]).astype(F32))
     row = lax.broadcasted_iota(jnp.int32, mine.shape, 0)
     mine = jnp.where(row == 2, zeros, mine)
+    second.corner()
+    third.middle()
     total = exchange_rows(n, mine, msg, m_send, m_recv)
     zero_ref[...] = jnp.broadcast_to(total[2:3, :128], (8, 128))
     inv = lax.rsqrt(to_columns(total) / width + EPS)
@@ -432,14 +658,16 @@
                 q_ref[:, cols] = v
             else:
                 kv_ref[0, :, cols] = v
-    for copy in copies:
-        copy.wait_send()
-    gather.finish()
+    second.arrive()
+    third.corner()
+    third.arrive()
+    for work in (first, second, third, gather):
+        work.finish()
     for copy in keep:
         copy.wait()
 
 
-def project(n, x, w, table, gain, seg):
+def project(n, x, w, table, gain, seg, wo, gu):
     rows, width = x.shape
     span, cols = n * rows, w.shape[2]
     return pl.pallas_call(
@@ -447,22 +675,24 @@
         out_shape=(
             shape((span, width), BF16),
             shape((3, width, cols), BF16),
+            shape((8,) + wo.shape, BF16),
+            shape((8, gu.shape[1] // 2, gu.shape[2]), BF16),
             shape((2, span, cols), F32),
             shape((span, cols), BF16),
             shape((2, span, cols), BF16),
             shape((span, 128), F32),
             shape((8, 128), F32),
         ),
-        in_specs=[VM, HB, HB, VM, VM],
-        out_specs=(HB, HB, VM, VM, VM, VM, VM),
+        in_specs=[VM, HB, HB, VM, VM, HB, HB],
+        out_specs=(HB, HB, HB, HB, VM, VM, VM, VM, VM),
         scratch_shapes=[
             pltpu.VMEM((span, width), BF16),
             pltpu.VMEM((3, width, cols), BF16),
             pltpu.VMEM((span, 128), F32),
             pltpu.VMEM((n, 8, span), F32),
-            pltpu.SemaphoreType.DMA((4,)),
-            pltpu.SemaphoreType.DMA((9,)),
-            pltpu.SemaphoreType.DMA((9,)),
+            pltpu.SemaphoreType.DMA((6,)),
+            pltpu.SemaphoreType.DMA((3, 9)),
+            pltpu.SemaphoreType.DMA((3, 9)),
             pltpu.SemaphoreType.DMA((n - 1,)),
             pltpu.SemaphoreType.DMA((n - 1,)),
         ]
@@ -470,11 +700,8 @@
         compiler_params=pltpu.CompilerParams(
             collective_id=1, has_side_effects=True, vmem_limit_bytes=VMEM_LIMIT
         ),
-        cost_estimate=pl.CostEstimate(
-            flops=40 * 10**9, bytes_accessed=10**7, transcendentals=0
-        ),
         name="project",
-    )(x, w, table, gain, seg)
+    )(x, w, table, gain, seg, wo, gu)
 
 
 def score_mask(scores, key_first, query_first, starts, diagonal):
@@ -643,35 +870,68 @@
         compiler_params=pltpu.CompilerParams(
             collective_id=2, has_side_effects=True, vmem_limit_bytes=VMEM_LIMIT
         ),
-        cost_estimate=pl.CostEstimate(
-            flops=40 * 10**9, bytes_accessed=10**7, transcendentals=0
-        ),
         name="attend",
     )(q, kv, zero)
 
 
 def attend_back_kernel(
+    n,
     q_ref,
     kvall_ref,
     do_ref,
     attn32_ref,
     lse_ref,
     bound_ref,
+    attn_ref,
+    dbranch_ref,
+    proj_ref,
+    inv_ref,
+    gain_ref,
+    tab_ref,
+    dproj_ref,
+    dgain_ref,
+    own_out,
+    x_out,
+    y_out,
     dq_ref,
-    dkv_ref,
     part,
     got,
     acc,
     delta,
+    dbranch,
+    dbranch_s,
+    attn_s,
+    ring,
+    got_o,
+    tab,
+    msg,
     send,
     recv,
+    s_send,
+    s_recv,
+    local_sem,
+    m_send,
+    m_recv,
+    o_send,
+    o_recv,
+    o_local,
 ):
     s, c, u = where_am_i()
     span, cols = q_ref.shape
+    width = dbranch_ref.shape[1]
     heads = cols // HEAD_DIM
     xn, yn = (s, c ^ 1, u), (s, c ^ 2, u)
     bx, by, bd = c ^ 1, c ^ 2, c ^ 3
-    greet(plane_peers())
+    load = [
+        pltpu.make_async_copy(tab_ref.at[rows_of(c, span)], tab, local_sem.at[0]),
+        pltpu.make_async_copy(half_columns(dbranch_ref, s), dbranch, local_sem.at[1]),
+    ]
+    for copy in load:
+        copy.start()
+    greet(plane_peers() + all_uly_peers(n) + [(None, (1 - s, c, u))])
+    sibling = Sibling(s_send, s_recv)
+    sibling.start(half_columns(dbranch_ref, 1 - s), dbranch_s)
+    sibling.start(attn_ref, attn_s)
     bound = bound_ref[:1, :1]
     nq, tq = tiles(span, 512)
     nk, tk = tiles(span, 512)
@@ -728,6 +988,20 @@
     def sent(k, src, dst, peer):
         return remote(src, dst, send.at[k], recv.at[k], peer)
 
+    def place(out, piece, part):
+        size = cols if part is None else cols // 2
+        return out.at[pl.ds((part or 0) * size, size)]
+
+    weight = PlaneReduce(ring, got_o, (own_out, x_out, y_out), place, o_send, o_recv, o_local)
+    pieces = Pieces(
+        [
+            (
+                weight,
+                0,
+                wide_piece((attn_ref, dbranch), (attn_s, dbranch_s), lambda p: slice(None)),
+            )
+        ]
+    )
     work(bd)
     copies = [
         sent(0, part.at[bd, :, lo], got.at[0, :, lo], xn),
@@ -751,38 +1025,87 @@
     more = [sent(3, part.at[by], got.at[2], yn)]
     more[0].start()
     copies += more
+    wait_all(load)
+    sibling.wait(0)
+    sibling.wait(1)
+    pieces.step()
     update(c, True)
+
+    cosine, sine = rope_factors(tab[...])
+
+    def turn_back(i):
+        inverse = inv_ref[:, i : i + 1]
+        row_dot = jnp.zeros((span, 1), F32)
+        for h in range(heads):
+            lanes = slice(h * HEAD_DIM, (h + 1) * HEAD_DIM)
+            source = dq_ref if i == 0 else acc.at[0]
+            v = source[:, lanes]
+            v = v * cosine - pltpu.roll(v, HALF, 1) * sine
+            values = proj_ref[i, :, lanes]
+            dgain_ref[i : i + 1, lanes] = jnp.sum(v * values * inverse, axis=0, keepdims=True)
+            v = v * gain_ref[i : i + 1, lanes]
+            source[:, lanes] = v
+            row_dot = row_dot + jnp.sum(values * v, axis=-1, keepdims=True)
+        return row_dot
+
+    dots_q = turn_back(0)
     sent(2, part.at[bx], got.at[1], xn).wait_recv()
     sent(3, part.at[by], got.at[2], yn).wait_recv()
-    dkv_ref[...] = acc[...] + got[1].astype(F32) + got[2].astype(F32)
+    acc[...] += got[1].astype(F32) + got[2].astype(F32)
+    dproj_ref[2] = acc[1].astype(BF16)
+    dots_k = turn_back(1)
+    total = exchange_rows(n, to_rows(dots_q, dots_k), msg, m_send, m_recv)
+    means = to_columns(total) / width
+    for i in range(2):
+        inverse = inv_ref[:, i : i + 1]
+        factor = inverse**3 * means[:, i : i + 1]
+        source = dq_ref if i == 0 else acc.at[0]
+        dproj_ref[i] = (inverse * source[...] - proj_ref[i] * factor).astype(BF16)
+    pieces.finish()
+    weight.finish(1)
+    sibling.finish()
     for copy in copies:
         copy.wait_send()
 
 
-def attend_back(q, kvall, d_out, attn32, lse, bound):
+def attend_back(n, q, kvall, d_out, attn32, lse, bound, attn, dbranch, proj, inv, gain, table):
     span, cols = q.shape
     heads = cols // HEAD_DIM
+    width = dbranch.shape[1]
+    ring, sems = piece_scratch(1, 1, cols, width // 8)
     return pl.pallas_call(
-        attend_back_kernel,
-        out_shape=(shape((span, cols), F32), shape((2, span, cols), F32)),
-        in_specs=[VM] * 6,
-        out_specs=(VM, VM),
+        functools.partial(attend_back_kernel, n),
+        out_shape=(shape((3, span, cols), BF16), shape((2, cols), F32))
+        + (shape((cols, width // 8), BF16),) * 3,
+        in_specs=[VM] * 7 + [HB, VM, VM, VM, HB],
+        out_specs=(VM, VM, HB, HB, HB),
         scratch_shapes=[
+            pltpu.VMEM((span, cols), F32),
             pltpu.VMEM((4, 2, span, cols), BF16),
             pltpu.VMEM((3, 2, span, cols), BF16),
             pltpu.VMEM((2, span, cols), F32),
             pltpu.VMEM((heads, 8, span), F32),
+            pltpu.VMEM((span, width // 2), BF16),
+            pltpu.VMEM((span, width // 2), BF16),
+            pltpu.VMEM((span, cols), BF16),
+            ring[0],
+            ring[1],
+            pltpu.VMEM((span, 128), F32),
+            pltpu.VMEM((n, 8, span), F32),
             pltpu.SemaphoreType.DMA((4,)),
             pltpu.SemaphoreType.DMA((4,)),
-        ],
+            pltpu.SemaphoreType.DMA((2,)),
+            pltpu.SemaphoreType.DMA((2,)),
+            pltpu.SemaphoreType.DMA((2,)),
+            pltpu.SemaphoreType.DMA((n - 1,)),
+            pltpu.SemaphoreType.DMA((n - 1,)),
+        ]
+        + sems,
         compiler_params=pltpu.CompilerParams(
             collective_id=3, has_side_effects=True, vmem_limit_bytes=VMEM_LIMIT
         ),
-        cost_estimate=pl.CostEstimate(
-            flops=50 * 10**9, bytes_accessed=10**7, transcendentals=0
-        ),
         name="attend_back",
-    )(q, kvall, d_out, attn32, lse, bound)
+    )(q, kvall, d_out, attn32, lse, bound, attn, dbranch, proj, inv, gain, table)
 
 
 def load_blocks(src, dst, sem, axis):
@@ -809,29 +1132,50 @@
     wo_ref,
     x_ref,
     gain_ref,
-    wg_ref,
+    wga_ref,
+    gu_ref,
+    down_ref,
     branch_ref,
     resid_ref,
     group_out,
     gate_ref,
     up_ref,
     hidden_ref,
+    wgb_out,
+    wgc_out,
+    wd_out,
     wo,
     wg,
     group,
     part,
-    from_l,
-    from_r,
+    got_rows,
     sem_o,
-    sem_g,
-    keep_sem,
+    local_sem,
+    w_send,
+    w_recv,
     *sems,
 ):
     s, c, u = where_am_i()
     rows, width = x_ref.shape
     load_o = load_blocks(wo_ref, wo, sem_o, 1)
-    load_g = load_blocks(wg_ref, wg, sem_g, 1)
-    greet(line_peers(n))
+    half = wga_ref.shape[1]
+    load_g = [
+        pltpu.make_async_copy(wga_ref, wg.at[0, :, pl.ds(0, half)], local_sem.at[0]),
+        pltpu.make_async_copy(wgb_out, wg.at[0, :, pl.ds(half, half)], local_sem.at[1]),
+        pltpu.make_async_copy(wgc_out, wg.at[1], local_sem.at[2]),
+    ]
+    load_g[0].start()
+    greet(line_peers(n) + plane_peers() + [(None, (1 - s, c, u))])
+
+    def plane(k, src, out, half_rows):
+        return PlaneGather(
+            src, lambda b: out.at[b], half_rows, w_send.at[k], w_recv.at[k], local_sem.at[4 + k]
+        )
+
+    first = plane(0, gu_ref.at[0, pl.ds(half, half)], wgb_out, half // 2)
+    second = plane(1, gu_ref.at[1], wgc_out, half)
+    third = plane(2, down_ref, wd_out, down_ref.shape[0] // 2)
+    first.start()
     wait_all(load_o)
     chunk_cols = width // part.shape[0]
     span = n * rows
@@ -847,24 +1191,47 @@
 
         lax.fori_loop(0, count, tile, 0)
 
-    LineReduce(n, rows, part, from_l, from_r, sems[:4]).run(compute, branch_ref)
+    def reduce_hook(slot):
+        if slot == 0:
+            first.middle()
+            second.start()
+        if slot == 1:
+            first.corner()
+        if slot == 2:
+            first.arrive()
+            load_g[1].start()
+
+    LineReduce(n, rows, part, got_rows, sems[:4]).run(compute, branch_ref, reduce_hook)
     branch = branch_ref[...]
     resid = x_ref[...].astype(F32) + branch * inverse_rms(branch) * gain_ref[0:1, :]
     resid_ref[...] = resid
     group[rows_of(u, rows), :] = resid.astype(BF16)
-    LineGather(n, rows, group, sems[4:]).run()
-    keep = pltpu.make_async_copy(group, group_out, keep_sem)
+    gather = LineGather(n, rows, group, sems[4:])
+    gather.send(0)
+    second.middle()
+    third.start()
+
+    def gather_hook(slot):
+        if slot == 1:
+            second.corner()
+
+    gather.run(gather_hook)
+    second.arrive()
+    load_g[2].start()
+    keep = pltpu.make_async_copy(group, group_out, local_sem.at[3])
     keep.start()
+    third.middle()
     wait_all(load_g)
-    ntile, tsize = tiles(gate_ref.shape[1], 512)
+    ff = gate_ref.shape[1]
+    ntile, tsize = tiles(ff, 512)
 
     def body(i, carry):
         lanes = pl.ds(pl.multiple_of(i * tsize, tsize), tsize)
 
         def tile(j, carry):
             where = pl.ds(pl.multiple_of(j * size, size), size)
-            gate = dot(group[where, :], wg[0, :, lanes], NN)
-            up = dot(group[where, :], wg[1, :, lanes], NN)
+            gate = dot(group[where, :], wg[0, :, :, lanes].reshape(width, tsize), NN)
+            up = dot(group[where, :], wg[1, :, :, lanes].reshape(width, tsize), NN)
             gate_ref[where, lanes] = gate.astype(BF16)
             up_ref[where, lanes] = up.astype(BF16)
             hidden_ref[where, lanes] = (gate * jax.nn.sigmoid(gate) * up).astype(BF16)
@@ -873,18 +1240,25 @@
         return lax.fori_loop(0, count, tile, carry)
 
     lax.fori_loop(0, ntile, body, 0)
+    third.corner()
+    third.arrive()
+    for work in (first, second, third):
+        work.finish()
     keep.wait()
 
 
 def reduce_scratch(n, rows, width):
-    dims = (CHUNKS, n * rows, width // CHUNKS)
-    return [pltpu.VMEM(dims, BF16)] * 3
-
-
-def mlp_in(n, attn, wo, x, gain, wg):
+    cols = width // CHUNKS
+    return [
+        pltpu.VMEM((CHUNKS, n * rows, cols), BF16),
+        pltpu.VMEM((CHUNKS, (n + 1) * rows, cols), BF16),
+    ]
+
+
+def mlp_in(n, attn, wo, x, gain, wga, gu, down):
     rows, width = x.shape
     span, cols = attn.shape
-    ff = wg.shape[3]
+    kb, ff = gu.shape[1:]
     return pl.pallas_call(
         functools.partial(mlp_in_kernel, n),
         out_shape=(
@@ -894,30 +1268,31 @@
             shape((span, ff), BF16),
             shape((span, ff), BF16),
             shape((span, ff), BF16),
+            shape((8, kb // 2, ff), BF16),
+            shape((8, kb, ff), BF16),
+            shape((8,) + down.shape, BF16),
         ),
-        in_specs=[VM, HB, VM, VM, HB],
-        out_specs=(VM, VM, HB, VM, VM, VM),
+        in_specs=[VM, HB, VM, VM, HB, HB, HB],
+        out_specs=(VM, VM, HB, VM, VM, VM, HB, HB, HB),
         scratch_shapes=[
             pltpu.VMEM((cols, width), BF16),
-            pltpu.VMEM((2, width, ff), BF16),
+            pltpu.VMEM((2, 8, kb, ff), BF16),
             pltpu.VMEM((span, width), BF16),
         ]
         + reduce_scratch(n, rows, width)
         + [
             pltpu.SemaphoreType.DMA((8,)),
-            pltpu.SemaphoreType.DMA((8,)),
-            pltpu.SemaphoreType.DMA,
+            pltpu.SemaphoreType.DMA((7,)),
+            pltpu.SemaphoreType.DMA((3, 9)),
+            pltpu.SemaphoreType.DMA((3, 9)),
         ]
         + line_sems(n, CHUNKS)
         + line_sems(n),
         compiler_params=pltpu.CompilerParams(
             collective_id=4, has_side_effects=True, vmem_limit_bytes=VMEM_LIMIT
         ),
-        cost_estimate=pl.CostEstimate(
-            flops=80 * 10**9, bytes_accessed=10**7, transcendentals=0
-        ),
         name="mlp_in",
-    )(attn, wo, x, gain, wg)
+    )(attn, wo, x, gain, wga, gu, down)
 
 
 def mlp_out_kernel(
@@ -937,8 +1312,7 @@
     mlp,
     group,
     part,
-    from_l,
-    from_r,
+    got_rows,
     sem_d,
     keep_sem,
     *sems,
@@ -962,7 +1336,7 @@
 
         lax.fori_loop(0, count, tile, 0)
 
-    LineReduce(n, rows, part, from_l, from_r, sems[:4]).run(compute, mlp)
+    LineReduce(n, rows, part, got_rows, sems[:4]).run(compute, mlp)
     values = mlp[...]
     inverse = inverse_rms(values)
     grad = cot_ref[...].astype(F32)
@@ -1025,9 +1399,6 @@
         compiler_params=pltpu.CompilerParams(
             collective_id=5, has_side_effects=True, vmem_limit_bytes=VMEM_LIMIT
         ),
-        cost_estimate=pl.CostEstimate(
-            flops=80 * 10**9, bytes_accessed=10**7, transcendentals=0
-        ),
         name="mlp_out",
     )(hidden, wd, resid, gain, cot, gate, up)
 
@@ -1035,79 +1406,228 @@
 def mlp_back_kernel(
     n,
     dgu_ref,
-    wg_ref,
+    wga_ref,
+    wgb_ref,
+    wgc_ref,
     cot_ref,
     branch_ref,
     gain_ref,
     wo_ref,
+    hidden_ref,
+    dmlp_ref,
+    resid_ref,
     dresid_ref,
     group_out,
     dattn_ref,
     dgain_ref,
+    gown_out,
+    gx_out,
+    gy_out,
+    down_own_out,
+    down_x_out,
+    down_y_out,
     wo,
     wg,
     group,
     part,
-    from_l,
-    from_r,
+    got_rows,
+    dmlp,
+    resid,
+    hidden_s,
+    dmlp_s,
+    resid_s,
+    dgu_s,
+    ring_d,
+    ring_g,
+    got_d,
+    got_g,
     sem_o,
-    sem_g,
-    keep_sem,
+    local_sem,
+    s_send,
+    s_recv,
+    d_send,
+    d_recv,
+    d_local,
+    g_send,
+    g_recv,
+    g_local,
     *sems,
 ):
     s, c, u = where_am_i()
     rows, width = cot_ref.shape
-    load_g = load_blocks(wg_ref, wg, sem_g, 1)
+    half = wga_ref.shape[1]
+    chunk_cols = width // part.shape[0]
+    per_chunk = chunk_cols // (2 * half)
+    chunks = part.shape[0]
+
+    def load_chunk(chunk):
+        slot = chunk % 2
+        where = pl.ds(chunk * per_chunk, per_chunk)
+        return [
+            pltpu.make_async_copy(
+                wga_ref.at[where], wg.at[slot, 0, :, pl.ds(0, half)], local_sem.at[slot, 0]
+            ),
+            pltpu.make_async_copy(
+                wgb_ref.at[where], wg.at[slot, 0, :, pl.ds(half, half)], local_sem.at[slot, 1]
+            ),
+            pltpu.make_async_copy(wgc_ref.at[where], wg.at[slot, 1], local_sem.at[slot, 2]),
+        ]
+
+    def start_chunk(chunk):
+        for copy in load_chunk(chunk):
+            copy.start()
+
+    start_chunk(0)
+    start_chunk(1)
+    load_m = [
+        pltpu.make_async_copy(half_columns(dmlp_ref, s), dmlp, local_sem.at[2, 0]),
+        pltpu.make_async_copy(half_columns(resid_ref, s), resid, local_sem.at[2, 1]),
+    ]
+    for copy in load_m:
+        copy.start()
     load_o = load_blocks(wo_ref, wo, sem_o, 1)
-    greet(line_peers(n))
-    wait_all(load_g)
-    chunk_cols = width // part.shape[0]
+    greet(line_peers(n) + plane_peers() + [(None, (1 - s, c, u))])
+    sibling = Sibling(s_send, s_recv)
+    sibling.start(half_columns(dmlp_ref, 1 - s), dmlp_s)
+    sibling.start(hidden_ref, hidden_s)
+    sibling.start(half_columns(resid_ref, 1 - s), resid_s)
+    sibling.start(dgu_ref, dgu_s)
     span = n * rows
     count, size = tiles(span, 512)
 
     def compute(chunk):
-        cols = slice(chunk * chunk_cols, (chunk + 1) * chunk_cols)
+        wait_all(load_chunk(chunk))
+        slot = chunk % 2
 
         def tile(i, carry):
             where = pl.ds(pl.multiple_of(i * size, size), size)
             part[chunk, where, :] = (
-                dot(dgu_ref[0, where, :], wg[0, cols, :], NT)
-                + dot(dgu_ref[1, where, :], wg[1, cols, :], NT)
+                dot(dgu_ref[0, where, :], wg[slot, 0].reshape(chunk_cols, -1), NT)
+                + dot(dgu_ref[1, where, :], wg[slot, 1].reshape(chunk_cols, -1), NT)
             ).astype(BF16)
             return carry
 
         lax.fori_loop(0, count, tile, 0)
-
-    LineReduce(n, rows, part, from_l, from_r, sems[:4]).run(compute, dresid_ref)
+        if chunk + 2 < chunks:
+            start_chunk(chunk + 2)
+
+    rows_d, cols_g = ring_d.shape[2], ring_g.shape[3]
+    tiles_g = dgu_ref.shape[2] // cols_g
+
+    def place_d(out, piece, part):
+        size = rows_d if part is None else rows_d // 2
+        return out.at[pl.ds(piece * rows_d + (part or 0) * size, size)]
+
+    def place_g(out, piece, part):
+        size = ring_g.shape[2] if part is None else ring_g.shape[2] // 2
+        ci, tile = piece // tiles_g, piece % tiles_g
+        return out.at[ci, pl.ds((part or 0) * size, size), pl.ds(tile * cols_g, cols_g)]
+
+    down = PlaneReduce(
+        ring_d, got_d, (down_own_out, down_x_out, down_y_out), place_d, d_send, d_recv, d_local
+    )
+    gate = PlaneReduce(ring_g, got_g, (gown_out, gx_out, gy_out), place_g, g_send, g_recv, g_local)
+    down_piece = wide_piece(
+        (hidden_ref, dmlp), (hidden_s, dmlp_s), lambda p: slice(p * rows_d, (p + 1) * rows_d)
+    )
+
+    def gate_right(ref, piece):
+        tile = piece % tiles_g
+        return ref[piece // tiles_g, :, tile * cols_g : (tile + 1) * cols_g]
+
+    gate_piece = tall_piece((resid, dgu_ref), (resid_s, dgu_s), gate_right)
+    n_d, n_g = got_d.shape[0], got_g.shape[0]
+    pieces = Pieces(
+        [(down, p, down_piece) for p in range(n_d)] + [(gate, p, gate_piece) for p in range(n_g)]
+    )
+
+    def reduce_hook(slot):
+        if slot == 0:
+            wait_all(load_m)
+            sibling.wait(0)
+            sibling.wait(1)
+            pieces.step(2)
+        if slot == 1:
+            pieces.step()
+        if slot == 2:
+            pieces.step()
+
+    LineReduce(n, rows, part, got_rows, sems[:4]).run(compute, dresid_ref, reduce_hook)
     d_resid = dresid_ref[...] + cot_ref[...].astype(F32)
     dresid_ref[...] = d_resid
     branch = branch_ref[...]
     inverse = inverse_rms(branch)
     d_branch = norm_back(branch, inverse, d_resid * gain_ref[0:1, :], width)
-    group[rows_of(u, rows), :] = d_branch.astype(BF16)
-    gather = LineGather(n, rows, group, sems[4:])
+    small = group.shape[0] == span
+    if small:
+        group[rows_of(u, rows), :] = d_branch.astype(BF16)
+        gather = LineGather(n, rows, group, sems[4:])
+    else:
+        group[:rows, :] = d_branch.astype(BF16)
+        own = pltpu.make_async_copy(
+            group.at[pl.ds(0, rows)], group_out.at[rows_of(u, rows)], local_sem.at[2, 2]
+        )
+        own.start()
+        own.wait()
+        gather = LineGather(n, rows, group_out, sems[4:])
     gather.send(0)
     dgain_ref[...] = jnp.sum(d_resid * branch * inverse, axis=0, keepdims=True)
     wait_all(load_o)
-    for slot in range(n - 1):
-        gather.wait(slot)
-    gather.finish()
-    keep = pltpu.make_async_copy(group, group_out, keep_sem)
-    keep.start()
+    sibling.wait(2)
+    sibling.wait(3)
+    pieces.step()
+
+    def gather_hook(slot):
+        if slot < 2:
+            pieces.step()
+
+    gather.run(gather_hook)
+    if small:
+        keep = pltpu.make_async_copy(group, group_out, local_sem.at[2, 2])
+        keep.start()
+    pieces.step()
 
     def tile(j, carry):
         where = pl.ds(pl.multiple_of(j * size, size), size)
-        dattn_ref[where, :] = dot(group[where, :], wo[...], NT).astype(BF16)
+        if small:
+            rows_in = group[where, :]
+        else:
+            fetch = pltpu.make_async_copy(group_out.at[where], group, local_sem.at[2, 2])
+            fetch.start()
+            fetch.wait()
+            rows_in = group[...]
+        dattn_ref[where, :] = dot(rows_in, wo[...], NT).astype(BF16)
         return carry
 
     lax.fori_loop(0, count, tile, 0)
-    keep.wait()
-
-
-def mlp_back(n, dgu, wg, cot, branch, gain, wo):
+    pieces.finish()
+    down.finish(n_d)
+    gate.finish(n_g)
+    sibling.finish()
+    if small:
+        keep.wait()
+
+
+def piece_scratch(slots, pieces, rows, cols):
+    return (
+        [pltpu.VMEM((slots, 4, rows, cols), BF16), pltpu.VMEM((pieces, rows, cols), BF16)],
+        [
+            pltpu.SemaphoreType.DMA((pieces, 6)),
+            pltpu.SemaphoreType.DMA((pieces, 6)),
+            pltpu.SemaphoreType.DMA((pieces,)),
+        ],
+    )
+
+
+def mlp_back(n, dgu, wga, wgb, wgc, cot, branch, gain, wo, hidden, dmlp, resid):
     rows, width = branch.shape
     span, ff = dgu.shape[1:]
     cols = wo.shape[1]
+    kb, kc = width // 8, wo.shape[2]
+    count, size = tiles(ff, 512)
+    ring_d, sems_d = piece_scratch(min(3, count), count, size, kc)
+    ring_g, sems_g = piece_scratch(3 if count > 1 else 2, 2 * count, kb, size)
+    chunk_blocks = width // CHUNKS // kb
     return pl.pallas_call(
         functools.partial(mlp_back_kernel, n),
         out_shape=(
@@ -1115,54 +1635,76 @@
             shape((span, width), BF16),
             shape((span, cols), BF16),
             shape((1, width), F32),
-        ),
-        in_specs=[VM, HB, VM, VM, VM, HB],
-        out_specs=(VM, HB, VM, VM),
+        )
+        + (shape((2, kb, ff), BF16),) * 3
+        + (shape((ff, kc), BF16),) * 3,
+        in_specs=[VM, HB, HB, HB, VM, VM, VM, HB, VM, HB, HB],
+        out_specs=(VM, HB, VM, VM) + (HB,) * 6,
         scratch_shapes=[
             pltpu.VMEM((cols, width), BF16),
-            pltpu.VMEM((2, width, ff), BF16),
-            pltpu.VMEM((span, width), BF16),
+            pltpu.VMEM((2, 2, chunk_blocks, kb, ff), BF16),
+            pltpu.VMEM((min(span, 512), width), BF16),
         ]
         + reduce_scratch(n, rows, width)
         + [
+            pltpu.VMEM((span, width // 2), BF16),
+            pltpu.VMEM((span, width // 2), BF16),
+            pltpu.VMEM((span, ff), BF16),
+            pltpu.VMEM((span, width // 2), BF16),
+            pltpu.VMEM((span, width // 2), BF16),
+            pltpu.VMEM((2, span, ff), BF16),
+            ring_d[0],
+            ring_g[0],
+            ring_d[1],
+            ring_g[1],
             pltpu.SemaphoreType.DMA((8,)),
-            pltpu.SemaphoreType.DMA((8,)),
-            pltpu.SemaphoreType.DMA,
+            pltpu.SemaphoreType.DMA((3, 3)),
+            pltpu.SemaphoreType.DMA((4,)),
+            pltpu.SemaphoreType.DMA((4,)),
         ]
+        + sems_d
+        + sems_g
         + line_sems(n, CHUNKS)
         + line_sems(n),
         compiler_params=pltpu.CompilerParams(
             collective_id=6, has_side_effects=True, vmem_limit_bytes=VMEM_LIMIT
         ),
-        cost_estimate=pl.CostEstimate(
-            flops=80 * 10**9, bytes_accessed=10**7, transcendentals=0
-        ),
         name="mlp_back",
-    )(dgu, wg, cot, branch, gain, wo)
+    )(dgu, wga, wgb, wgc, cot, branch, gain, wo, hidden, dmlp, resid)
 
 
 def proj_back_kernel(
     n,
-    dq_ref,
-    dkv_ref,
-    proj_ref,
-    inv_ref,
-    gain_ref,
-    tab_ref,
+    dproj_ref,
     wq_ref,
     dresid_ref,
+    xg_ref,
+    gcols_ref,
+    gattn_ref,
+    gmlp_ref,
     out_ref,
-    dproj_ref,
-    dgain_ref,
+    gain_ref,
+    own_out,
+    x_out,
+    y_out,
     wq,
-    tab,
-    scaled_ref,
-    total_ref,
-    msg,
+    xs,
+    xs_s,
+    dproj_s,
+    total,
     part,
-    from_l,
-    from_r,
+    got_rows,
+    ring,
+    got,
+    sums,
     local_sem,
+    s_send,
+    s_recv,
+    q_send,
+    q_recv,
+    q_local,
+    v_send,
+    v_recv,
     m_send,
     m_recv,
     *sems,
@@ -1171,38 +1713,19 @@
     rows, width = dresid_ref.shape
     span = n * rows
     load = [
-        pltpu.make_async_copy(tab_ref.at[rows_of(c, span)], tab, local_sem.at[0]),
-        pltpu.make_async_copy(wq_ref, wq, local_sem.at[1]),
+        pltpu.make_async_copy(wq_ref, wq, local_sem.at[0]),
+        pltpu.make_async_copy(half_columns(xg_ref, s), xs, local_sem.at[1]),
     ]
     for copy in load:
         copy.start()
-    greet(all_uly_peers(n))
+    corner = (s, c ^ 3, u)
+    greet(all_uly_peers(n) + plane_peers() + [(None, corner), (None, (1 - s, c, u))])
+    gains = GainSum(n, sums, (v_send, v_recv, m_send, m_recv))
+    gains.start(gcols_ref, gattn_ref, gmlp_ref)
+    sibling = Sibling(s_send, s_recv)
+    sibling.start(half_columns(xg_ref, 1 - s), xs_s)
+    sibling.start(dproj_ref, dproj_s)
     load[0].wait()
-    cosine, sine = rope_factors(tab[...])
-    heads = dq_ref.shape[1] // HEAD_DIM
-    dots = []
-    for i in range(2):
-        inverse = inv_ref[:, i : i + 1]
-        row_dot = jnp.zeros((span, 1), F32)
-        for h in range(heads):
-            cols = slice(h * HEAD_DIM, (h + 1) * HEAD_DIM)
-            v = dq_ref[:, cols] if i == 0 else dkv_ref[0, :, cols]
-            v = v * cosine - pltpu.roll(v, HALF, 1) * sine
-            values = proj_ref[i, :, cols]
-            dgain_ref[i : i + 1, cols] = jnp.sum(v * values * inverse, axis=0, keepdims=True)
-            v = v * gain_ref[i : i + 1, cols]
-            scaled_ref[i, :, cols] = v
-            row_dot = row_dot + jnp.sum(values * v, axis=-1, keepdims=True)
-        dots.append(row_dot)
-    total = exchange_rows(n, to_rows(*dots), msg, m_send, m_recv)
-    means = to_columns(total) / width
-    total_ref[...] = means
-    for i in range(2):
-        inverse = inv_ref[:, i : i + 1]
-        factor = inverse**3 * total_ref[:, i : i + 1]
-        dproj_ref[i] = (inverse * scaled_ref[i] - proj_ref[i] * factor).astype(BF16)
-    dproj_ref[2] = dkv_ref[1].astype(BF16)
-    load[1].wait()
     chunk_cols = width // part.shape[0]
     count, size = tiles(span, 512)
 
@@ -1220,45 +1743,143 @@
 
         lax.fori_loop(0, count, tile, 0)
 
-    LineReduce(n, rows, part, from_l, from_r, sems[:4]).run(compute, total_wide := sems[4])
-    out_ref[...] = (dresid_ref[...] + total_wide[...]).astype(BF16)
-
-
-def proj_back(n, dq, dkv, proj, inv, gain, table, wq, dresid):
+    def place(out, piece, part):
+        size = ring.shape[2] if part is None else ring.shape[2] // 2
+        return out.at[piece, pl.ds((part or 0) * size, size)]
+
+    weight = PlaneReduce(ring, got, (own_out, x_out, y_out), place, q_send, q_recv, q_local)
+    compute_piece = tall_piece((xs, dproj_ref), (xs_s, dproj_s), lambda ref, piece: ref[piece])
+    pieces = Pieces([(weight, p, compute_piece) for p in range(3)])
+
+    def hook(slot):
+        if slot == 0:
+            load[1].wait()
+            sibling.wait(0)
+            sibling.wait(1)
+            pieces.step(3)
+            gains.over_ctx()
+        if slot == 1:
+            pieces.catch_up()
+            gains.over_uly()
+
+    LineReduce(n, rows, part, got_rows, sems[:4]).run(compute, total, hook)
+    out_ref[...] = (dresid_ref[...] + total[...]).astype(BF16)
+    pieces.finish()
+    gains.finish(gain_ref)
+    weight.finish(3)
+    sibling.finish()
+
+
+class GainSum:
+    def __init__(self, n, refs, sems):
+        self.n = n
+        self.all, self.core, self.plane, self.line = refs
+        self.v_send, self.v_recv, self.m_send, self.m_recv = sems
+        self.s, self.c, self.u = where_am_i()
+        self.sent = []
+
+    def copy(self, k, src, dst, peer):
+        return remote(src, dst, self.v_send.at[k], self.v_recv.at[k], peer)
+
+    def go(self, copy):
+        copy.start()
+        self.sent.append(copy)
+
+    def start(self, cols, attn, mlp):
+        half, local = self.all.shape[2], cols.shape[1]
+        rows = jnp.zeros((8, half), F32)
+        for h in range(2):
+            self.all[h] = rows
+        mine = self.u * local
+        home = pl.ds(pl.multiple_of(lax.rem(mine, half), local), local)
+        self.all[pl.ds(mine // half, 1), 0:2, home] = cols[...][None]
+        for h in range(2):
+            part = slice(h * half, (h + 1) * half)
+            self.all[h, 2:3, :] = attn[:, part]
+            self.all[h, 3:4, :] = mlp[:, part]
+        self.go(self.copy(0, self.all.at[1 - self.s], self.core, (1 - self.s, self.c, self.u)))
+
+    def over_ctx(self):
+        s, c, u = self.s, self.c, self.u
+        self.copy(0, self.all.at[s], self.core, (1 - s, c, u)).wait_recv()
+        size = self.plane.shape[2]
+        total = self.all[pl.ds(s, 1)][0] + self.core[...]
+        for j in range(4):
+            self.plane[j] = total[:, j * size : (j + 1) * size]
+        for k in (1, 2, 3):
+            self.go(self.copy(k, self.plane.at[c ^ k], self.line.at[k - 1], (s, c ^ k, u)))
+
+    def over_uly(self):
+        s, c, u = self.s, self.c, self.u
+        total = self.plane[pl.ds(c, 1)][0]
+        for k in (1, 2, 3):
+            self.copy(k, self.plane.at[c ^ k], self.line.at[k - 1], (s, c ^ k, u)).wait_recv()
+            total = total + self.line[k - 1]
+        home = self.line.at[3 + u]
+        self.line[pl.ds(3 + u, 1)] = total[None]
+        for step in range(1, self.n):
+            peer = (s, c, lax.rem(u + step, self.n))
+            self.go(remote(home, home, self.m_send.at[step - 1], self.m_recv.at[step - 1], peer))
+
+    def finish(self, out):
+        s, c, u = self.s, self.c, self.u
+        for step in range(1, self.n):
+            source = lax.rem(u + self.n - step, self.n)
+            place = self.line.at[3 + source]
+            remote(
+                place, place, self.m_send.at[step - 1], self.m_recv.at[step - 1], (s, c, source)
+            ).wait_recv()
+        total = self.line[3]
+        for j in range(1, self.n):
+            total = total + self.line[3 + j]
+        out[...] = total[:4]
+        for copy in self.sent:
+            copy.wait_send()
+
+
+def proj_back(n, dproj, wq, dresid, xg, gain_cols, gain_attn, gain_mlp):
     rows, width = dresid.shape
-    span, cols = dq.shape
+    span, cols = dproj.shape[1:]
+    ring, sems = piece_scratch(3, 3, width // 8, cols)
     return pl.pallas_call(
         functools.partial(proj_back_kernel, n),
-        out_shape=(
-            shape((rows, width), BF16),
-            shape((3, span, cols), BF16),
-            shape((2, cols), F32),
-        ),
-        in_specs=[VM, VM, VM, VM, VM, HB, HB, VM],
-        out_specs=(VM, VM, VM),
+        out_shape=(shape((rows, width), BF16), shape((4, width // 8), F32))
+        + (shape((3, width // 8, cols), BF16),) * 3,
+        in_specs=[VM, HB, VM, HB, VM, VM, VM],
+        out_specs=(VM, VM, HB, HB, HB),
         scratch_shapes=[
             pltpu.VMEM((3, width, cols), BF16),
-            pltpu.VMEM((span, 128), F32),
-            pltpu.VMEM((2, span, cols), F32),
-            pltpu.VMEM((span, 128), F32),
-            pltpu.VMEM((n, 8, span), F32),
+            pltpu.VMEM((span, width // 2), BF16),
+            pltpu.VMEM((span, width // 2), BF16),
+            pltpu.VMEM((3, span, cols), BF16),
+            pltpu.VMEM((rows, width), F32),
         ]
         + reduce_scratch(n, rows, width)
+        + ring
         + [
+            (
+                pltpu.VMEM((2, 8, width // 2), F32),
+                pltpu.VMEM((8, width // 2), F32),
+                pltpu.VMEM((4, 8, width // 8), F32),
+                pltpu.VMEM((3 + n, 8, width // 8), F32),
+            ),
             pltpu.SemaphoreType.DMA((2,)),
+            pltpu.SemaphoreType.DMA((2,)),
+            pltpu.SemaphoreType.DMA((2,)),
+        ]
+        + sems
+        + [
+            pltpu.SemaphoreType.DMA((4,)),
+            pltpu.SemaphoreType.DMA((4,)),
             pltpu.SemaphoreType.DMA((n - 1,)),
             pltpu.SemaphoreType.DMA((n - 1,)),
         ]
-        + line_sems(n, CHUNKS)
-        + [pltpu.VMEM((rows, width), F32)],
+        + line_sems(n, CHUNKS),
         compiler_params=pltpu.CompilerParams(
             collective_id=7, has_side_effects=True, vmem_limit_bytes=VMEM_LIMIT
         ),
-        cost_estimate=pl.CostEstimate(
-            flops=50 * 10**9, bytes_accessed=10**7, transcendentals=0
-        ),
         name="proj_back",
-    )(dq, dkv, proj, inv, gain, table, wq, dresid)
+    )(dproj, wq, dresid, xg, gain_cols, gain_attn, gain_mlp)
 
 
 def rope_table(length):
@@ -1285,44 +1906,36 @@
     x = tokens[0]
     width = x.shape[1]
     cot = cotangent[0]
-    spread = ("slot", "ctx")
-    wo = lax.all_gather(out_weight, spread, axis=0)
-    wg = lax.all_gather(gate_up, spread, axis=0)
-    wd = lax.all_gather(down_weight, spread, axis=0)
     table = jnp.asarray(table)
-    group_x, wq, proj, q, kv, inv, zero = project(n, x, qkv_weight, table, qk_gain, segment_ids)
+    group_x, wq, wo, wga, proj, q, kv, inv, zero = project(
+        n, x, qkv_weight, table, qk_gain, segment_ids, out_weight, gate_up
+    )
     kvall, attn, attn32, lse, bound = attend(q, kv, zero)
-    branch, resid, group_resid, gate, up, hidden = mlp_in(n, attn, wo, x, post_gain, wg)
+    branch, resid, group_resid, gate, up, hidden, wgb, wgc, wd = mlp_in(
+        n, attn, wo, x, post_gain, wga, gate_up, down_weight
+    )
     block_out, group_dmlp, dgu, gain_mlp = mlp_out(n, hidden, wd, resid, post_gain, cot, gate, up)
-    down_grad = dot(hidden, group_dmlp, TN).astype(BF16)
-    d_resid, group_dbranch, d_attn, gain_attn = mlp_back(n, dgu, wg, cot, branch, post_gain, wo)
-    gate_grad = jnp.einsum(
-        "td,ctf->cdf", group_resid, dgu, preferred_element_type=F32
-    ).astype(BF16)
-    out_grad = dot(attn, group_dbranch, TN).astype(BF16)
-    dq, dkv = attend_back(q, kvall, d_attn, attn32, lse, bound)
-    input_grad, d_proj, gain_cols = proj_back(n, dq, dkv, proj, inv, qk_gain, table, wq, d_resid)
-    qkv_grad = jnp.einsum(
-        "td,cte->cde", group_x, d_proj, preferred_element_type=F32
-    ).astype(BF16)
-    local_cols = q.shape[1]
-    gain_block = lax.dynamic_update_slice(
-        jnp.zeros((2, width), F32), gain_cols, (0, lax.axis_index("uly") * local_cols)
+    d_resid, group_dbranch, d_attn, gain_attn, *grads = mlp_back(
+        n, dgu, wga, wgb, wgc, cot, branch, post_gain, wo, hidden, group_dmlp, group_resid
     )
-    gain_terms = jnp.concatenate([gain_block, gain_attn, gain_mlp], axis=0)
-    gain_totals = lax.psum(gain_terms, "uly")
-
-    def scatter(value, dim):
-        return lax.psum_scatter(value, spread, scatter_dimension=dim, tiled=True).astype(F32)
+    d_proj, gain_cols, *out_grads = attend_back(
+        n, q, kvall, d_attn, attn32, lse, bound, attn, group_dbranch, proj, inv, qk_gain, table
+    )
+    input_grad, gain_part, *qkv_grads = proj_back(
+        n, d_proj, wq, d_resid, group_x, gain_cols, gain_attn, gain_mlp
+    )
+
+    def total(parts):
+        return parts[0].astype(F32) + parts[1].astype(F32) + parts[2].astype(F32)
 
     return (
         block_out[None],
         input_grad[None],
-        scatter(qkv_grad, 1),
-        scatter(out_grad, 1),
-        scatter(gate_grad, 1),
-        scatter(down_grad, 1),
-        scatter(gain_totals, 1),
+        total(qkv_grads),
+        total(out_grads),
+        total(grads[:3]),
+        total(grads[3:]),
+        gain_part,
     )
 
 

time: 885 us -> 562 us (0.64)
  waiting for transfers between devices: 321 us -> 0 us
  Pallas kernels: 475 us -> 540 us
  matrix products: 32.4 us -> 0 us
  between operations: 14.7 us -> 1.22 us
  local copies, waits for them, and re-layouts: 15.8 us -> 3.52 us
  blocking collectives: 11.8 us -> 0 us
    reduce_scatter x4 -> x0, waiting for transfers between devices: 285 us -> none  [scatter(): lax.psum_scatter(value, spread, scatter_dimension=dim, tiled=True)]
    pallas_call x1, Pallas kernels: 84 us -> 133 us  [mlp_back(): pl.pallas_call(functools.partial(mlp_back_kernel, n), out_shape=(shape((r...]
    all_gather x3 -> x0, waiting for transfers between devices: 33.6 us -> none  [the longest x1 33.6 us: on_device(): wg = lax.all_gather(gate_up, spread, axis=0)]
    dot_general x4 -> x0, matrix products: 32.4 us -> none  [the longest x1 14.6 us: on_device(): jnp.einsum('td,ctf->cdf', group_resid, dgu, preferred_element_type=F32)]
    pallas_call x1, Pallas kernels: 71.4 us -> 43.8 us  [attend(): pl.pallas_call(attend_kernel, out_shape=(shape((4, 2, span, cols), BF16),...]
    pallas_call x1, Pallas kernels: 43 us -> 56.9 us  [attend_back(): pl.pallas_call(functools.partial(attend_back_kernel, n), out_shape=(shape...]
    pallas_call x1, Pallas kernels: 53.9 us -> 65.9 us  [project(): pl.pallas_call(functools.partial(proj_kernel, n), out_shape=(shape((span,...]
    psum x1 -> x0, blocking collectives: 11.8 us -> none  [on_device(): gain_totals = lax.psum(gain_terms, 'uly')]
  transfers between devices with their start and end apart: 8 -> 0, of which waited for: 5 -> 0; matrix products, arithmetic and copies ran while one was open for 5% -> 0% of each run, Pallas kernels for 25% -> 0%
where the time goes in v2:
time: 562 us; the launch traced here: 554 us
  Pallas kernels  540 us (96%)
  other arithmetic  8.99 us (2%)
    pallas_call x1, Pallas kernels, mlp_back(): pl.pallas_call(functools.partial(mlp_back_kernel, n), out_shape=(shape((r...  133 us
    pallas_call x1, Pallas kernels, mlp_in(): pl.pallas_call(functools.partial(mlp_in_kernel, n), out_shape=(shape((row...  98 us
    pallas_call x1, Pallas kernels, mlp_out(): pl.pallas_call(functools.partial(mlp_out_kernel, n), out_shape=(shape((ro...  90.7 us
    pallas_call x1, Pallas kernels, project(): pl.pallas_call(functools.partial(proj_kernel, n), out_shape=(shape((span,...  65.9 us
    pallas_call x1, Pallas kernels, attend_back(): pl.pallas_call(functools.partial(attend_back_kernel, n), out_shape=(shape...  56.9 us
    pallas_call x1, Pallas kernels, proj_back(): pl.pallas_call(functools.partial(proj_back_kernel, n), out_shape=(shape((...  52.2 us
    pallas_call x1, Pallas kernels, attend(): pl.pallas_call(attend_kernel, out_shape=(shape((4, 2, span, cols), BF16),...  43.8 us

profile of v2, /device:TPU:0, one launch (start us, length us, event | category | flops | bytes accessed | tf_op | source)
XLA Modules:
  0.0 553.9 jit_solution(12090624476875870210)
XLA Ops:
  0.6 65.9 %project.1 = (bf16[512,2048]{1,0:T(8,128)(2,1)}, bf16[3,2048,512]{2,1,0:T(8,128)(2,1)}, bf16[8,512,256]{2,1,0:T(8,128)(2,1)}, bf16[8,128,2048]{2,1,0:T(8,128)(2,...) custom-call(bf16[128,2048]{1,0:T(8,128)(2,1)} %bitcast.6, ...), custom_call_target="tpu_custom_call" | custom-call | tf_op jit(solution)/shard_map/project/pallas_call | solution.py:673
  66.5 43.8 %attend.1 = (bf16[4,2,512,512]{3,2,1,0:T(8,128)(2,1)}, bf16[512,512]{1,0:T(8,128)(2,1)}, f32[512,512]{1,0:T(8,128)}, f32[4,8,512]{2,1,0:T(8,128)}, s32[8,128]{1,0:T(8,128)}) custom-call(bf16[512,512]{1,0:T(8,128)(2,1)} %get-tuple-element.54.q_ref, bf16[2,512,512]{2,1,0:T(8,128)(2,1)} %get-tuple-element.55.kv_ref, f32[8,128]{1,0:T(8,128)} %get-tuple-element.56.zero_ref), custom_call_target="tpu_custom_call" | custom-call | tf_op jit(solution)/shard_map/attend/pallas_call | solution.py:847
  110.3 98.0 %mlp_in.1 = (f32[128,2048]{1,0:T(8,128)}, f32[128,2048]{1,0:T(8,128)}, bf16[512,2048]{1,0:T(8,128)(2,1)}, bf16[512,2048]{1,0:T(8,128)(2,1)}, bf16[512,2048]{1,0:...) custom-call(bf16[512,512]{1,0:T(8,128)(2,1)} %get-tuple-element.57.a, ...), custom_call_target="tpu_custom_call" | custom-call | tf_op jit(solution)/shard_map/mlp_in/pallas_call | solution.py:1262
  208.3 90.7 %mlp_out.1 = (bf16[128,2048]{1,0:T(8,128)(2,1)}, bf16[512,2048]{1,0:T(8,128)(2,1)}, bf16[2,512,2048]{2,1,0:T(8,128)(2,1)}, f32[1,2048]{1,0:T(1,128)}) custom-call(bf16[512,2048]{1,0:T(8,128)(2,1)} %get-tuple-element.60.hidden_ref, bf16[8,2048,256]{2,1,0:T(8,128)(2,1)} %get-tuple-element.61.wd_ref, f32[128,2048]{1,0:T(8,128)} %get-tuple-element.62.resid_ref, ...), custom_call_target="tpu_custom_call" | custom-call | tf_op jit(solution)/shard_map/mlp_out/pallas_call | solution.py:1380
  299.0 132.7 %mlp_back.1 = (f32[128,2048]{1,0:T(8,128)}, bf16[512,2048]{1,0:T(8,128)(2,1)}, bf16[512,512]{1,0:T(8,128)(2,1)}, f32[1,2048]{1,0:T(1,128)}, bf16[2,256,2048]{2,1...) custom-call(bf16[2,512,2048]{2,1,0:T(8,128)(2,1)} %get-tuple-element, ...), custom_call_target="tpu_custom_call" | custom-call | tf_op jit(solution)/shard_map/mlp_back/pallas_call | solution.py:1631
  431.7 56.9 %attend_back.1 = (bf16[3,512,512]{2,1,0:T(8,128)(2,1)}, f32[2,512]{1,0:T(2,128)}, bf16[512,256]{1,0:T(8,128)(2,1)}, bf16[512,256]{1,0:T(8,128)(2,1)}, bf16[512,256]{1,0:T(8,128)(2,1)}) custom-call(bf16[512,512]{1,0:T(8,128)(2,1)} %get-tuple-element.54.q_ref, bf16[4,2,512,512]{3,2,1,0:T(8,128)(2,1)} %get-tuple-element.66.kvall_ref, ...), custom_call_target="tpu_custom_call" | custom-call | tf_op jit(solution)/shard_map/attend_back/pallas_call | solution.py:1076
  488.7 0.0 copy-start.8
  488.7 0.0 copy-start.9
  488.7 0.0 copy-start.10
  488.7 52.2 %proj_back.1 = (bf16[128,2048]{1,0:T(8,128)(2,1)}, f32[4,256]{1,0:T(4,128)}, bf16[3,256,512]{2,1,0:T(8,128)(2,1)}, bf16[3,256,512]{2,1,0:T(8,128)(2,1)}, bf16[3,256,512]{2,1,0:T(8,128)(2,1)}) custom-call(bf16[3,512,512]{2,1,0:T(8,128)(2,1)} %get-tuple-element.80.dproj_ref, bf16[3,2048,512]{2,1,0:T(8,128)(2,1)} %get-tuple-element.81.wq_ref, ...), custom_call_target="tpu_custom_call" | custom-call | tf_op jit(solution)/shard_map/proj_back/pallas_call | solution.py:1844
  540.9 0.0 copy-done.8
  540.9 0.0 copy-done.9
  541.0 0.0 copy-done.10
  541.0 0.0 copy-start.4
  541.0 0.9 convert_add_fusion.3
  541.9 3.2 convert_add_fusion.2
  545.1 0.0 copy-done.4
  545.1 1.7 convert_add_fusion.1
  546.8 0.5 copy-done
  547.3 0.7 copy-done.1
  548.1 3.2 convert_add_fusion
  551.3 0.8 copy.20
  552.1 0.8 copy.21
  552.9 0.6 copy.22
  (14 shorter events, 0.0 us)
Async XLA Ops:
  488.7 52.3 %copy-start.8 = (bf16[512,256]{1,0:T(8,128)(2,1)S(1)}, bf16[512,256]{1,0:T(8,128)(2,1)}, u32[]{:S(2)}) copy-start(bf16[512,256]{1,0:T(8,128)(2,1)} %get-tuple-element.91) | copy-start | bytes 786436
  488.7 52.3 %copy-start.9 = (bf16[512,256]{1,0:T(8,128)(2,1)S(1)}, bf16[512,256]{1,0:T(8,128)(2,1)}, u32[]{:S(2)}) copy-start(bf16[512,256]{1,0:T(8,128)(2,1)} %get-tuple-element.92) | copy-start | bytes 786436
  488.7 52.3 %copy-start.10 = (bf16[512,256]{1,0:T(8,128)(2,1)S(1)}, bf16[512,256]{1,0:T(8,128)(2,1)}, u32[]{:S(2)}) copy-start(bf16[512,256]{1,0:T(8,128)(2,1)} %get-tuple-element.93) | copy-start | bytes 786436
  541.0 4.1 copy-start.4
  541.0 4.1 copy-start.5
  541.9 3.2 copy-start.3
  541.9 4.9 copy-start.2
  545.1 2.2 copy-start
  545.1 3.0 copy-start.1
  548.1 3.2 copy-start.6
  548.1 4.0 copy-start.7
  551.3 1.6 copy-start.11

commit v3 on v2

--- a/solution.py
+++ b/solution.py
@@ -20,6 +20,7 @@
 F32 = jnp.float32
 VMEM_LIMIT = 62 * 1024 * 1024
 CHUNKS = 4
+LATER = 2
 
 VM = pl.BlockSpec(memory_space=pltpu.VMEM)
 HB = pl.BlockSpec(memory_space=pl.ANY)
@@ -459,6 +460,62 @@
         lax.fori_loop(0, 2, pair, 0)
 
     return compute
+
+
+class LatePiece:
+    def __init__(self, number, ins, outs, scratch, sems):
+        s, c, u = where_am_i()
+        resid_hbm, resid_s_hbm, dgu_hbm, dgu_s_hbm = ins
+        resid, resid_s, right, right_s, ring, got = scratch
+        send, recv, local, load_sem = sems
+        cols = right.shape[1]
+        ci, tile = divmod(number, dgu_hbm.shape[2] // cols)
+        lanes = pl.ds(tile * cols, cols)
+        pairs = (
+            (half_columns(resid_hbm, s), resid),
+            (resid_s_hbm, resid_s),
+            (dgu_hbm.at[ci, :, lanes], right),
+            (dgu_s_hbm.at[ci, :, lanes], right_s),
+        )
+        self.loads = [
+            pltpu.make_async_copy(src, dst, load_sem.at[k]) for k, (src, dst) in enumerate(pairs)
+        ]
+        size = ring.shape[2]
+
+        def place(out, piece, part):
+            rows = size if part is None else size // 2
+            return out.at[ci, pl.ds((part or 0) * rows, rows), lanes]
+
+        self.plane = PlaneReduce(ring, got, outs, place, send, recv, local)
+        self.compute = tall_piece(
+            (resid, right), (resid_s, right_s), lambda ref, piece: ref[...]
+        )
+
+    def load(self):
+        for copy in self.loads:
+            copy.start()
+
+    def work(self):
+        def compute(out, piece):
+            for copy in self.loads:
+                copy.wait()
+            self.compute(out, piece)
+
+        return (self.plane, 0, compute)
+
+    @staticmethod
+    def scratch(span, width, ff):
+        cols = min(ff, 512)
+        ring, sems = piece_scratch(1, 1, width // 8, cols)
+        buffers = (
+            pltpu.VMEM((span, width // 2), BF16),
+            pltpu.VMEM((span, width // 2), BF16),
+            pltpu.VMEM((span, cols), BF16),
+            pltpu.VMEM((span, cols), BF16),
+            ring[0],
+            ring[1],
+        )
+        return [buffers, tuple(sems) + (pltpu.SemaphoreType.DMA((4,)),)]
 
 
 def half_columns(ref, s):
@@ -882,12 +939,17 @@
     attn32_ref,
     lse_ref,
     bound_ref,
-    attn_ref,
-    dbranch_ref,
     proj_ref,
     inv_ref,
     gain_ref,
     tab_ref,
+    resid_hbm,
+    resid_s_hbm,
+    dgu_hbm,
+    dgu_s_hbm,
+    own_in,
+    x_in,
+    y_in,
     dproj_ref,
     dgain_ref,
     own_out,
@@ -898,40 +960,35 @@
     got,
     acc,
     delta,
-    dbranch,
-    dbranch_s,
-    attn_s,
-    ring,
-    got_o,
     tab,
     msg,
+    late_buffers,
+    late_sems,
     send,
     recv,
-    s_send,
-    s_recv,
     local_sem,
     m_send,
     m_recv,
-    o_send,
-    o_recv,
-    o_local,
 ):
     s, c, u = where_am_i()
     span, cols = q_ref.shape
-    width = dbranch_ref.shape[1]
+    width = resid_hbm.shape[1]
     heads = cols // HEAD_DIM
     xn, yn = (s, c ^ 1, u), (s, c ^ 2, u)
     bx, by, bd = c ^ 1, c ^ 2, c ^ 3
-    load = [
-        pltpu.make_async_copy(tab_ref.at[rows_of(c, span)], tab, local_sem.at[0]),
-        pltpu.make_async_copy(half_columns(dbranch_ref, s), dbranch, local_sem.at[1]),
-    ]
-    for copy in load:
-        copy.start()
-    greet(plane_peers() + all_uly_peers(n) + [(None, (1 - s, c, u))])
-    sibling = Sibling(s_send, s_recv)
-    sibling.start(half_columns(dbranch_ref, 1 - s), dbranch_s)
-    sibling.start(attn_ref, attn_s)
+    load = pltpu.make_async_copy(tab_ref.at[rows_of(c, span)], tab, local_sem)
+    load.start()
+    last = 2 * (dgu_hbm.shape[2] // late_buffers[2].shape[1])
+    late = LatePiece(
+        last - 2,
+        (resid_hbm, resid_s_hbm, dgu_hbm, dgu_s_hbm),
+        (own_out, x_out, y_out),
+        late_buffers,
+        late_sems,
+    )
+    late.load()
+    pieces = Pieces([late.work()])
+    greet(plane_peers() + all_uly_peers(n))
     bound = bound_ref[:1, :1]
     nq, tq = tiles(span, 512)
     nk, tk = tiles(span, 512)
@@ -988,20 +1045,7 @@
     def sent(k, src, dst, peer):
         return remote(src, dst, send.at[k], recv.at[k], peer)
 
-    def place(out, piece, part):
-        size = cols if part is None else cols // 2
-        return out.at[pl.ds((part or 0) * size, size)]
-
-    weight = PlaneReduce(ring, got_o, (own_out, x_out, y_out), place, o_send, o_recv, o_local)
-    pieces = Pieces(
-        [
-            (
-                weight,
-                0,
-                wide_piece((attn_ref, dbranch), (attn_s, dbranch_s), lambda p: slice(None)),
-            )
-        ]
-    )
+    pieces.step()
     work(bd)
     copies = [
         sent(0, part.at[bd, :, lo], got.at[0, :, lo], xn),
@@ -1009,6 +1053,7 @@
     ]
     for copy in copies:
         copy.start()
+    pieces.catch_up()
     work(bx)
     sent(1, part.at[bx, :, hi], got.at[0, :, hi], yn).wait_recv()
     part[bx, :, half:, :] = (
@@ -1025,11 +1070,8 @@
     more = [sent(3, part.at[by], got.at[2], yn)]
     more[0].start()
     copies += more
-    wait_all(load)
-    sibling.wait(0)
-    sibling.wait(1)
-    pieces.step()
     update(c, True)
+    load.wait()
 
     cosine, sine = rope_factors(tab[...])
 
@@ -1062,50 +1104,46 @@
         source = dq_ref if i == 0 else acc.at[0]
         dproj_ref[i] = (inverse * source[...] - proj_ref[i] * factor).astype(BF16)
     pieces.finish()
-    weight.finish(1)
-    sibling.finish()
+    late.plane.finish(1)
     for copy in copies:
         copy.wait_send()
 
 
-def attend_back(n, q, kvall, d_out, attn32, lse, bound, attn, dbranch, proj, inv, gain, table):
+def attend_back(
+    n, q, kvall, d_out, attn32, lse, bound, proj, inv, gain, table, late, grads
+):
     span, cols = q.shape
     heads = cols // HEAD_DIM
-    width = dbranch.shape[1]
-    ring, sems = piece_scratch(1, 1, cols, width // 8)
+    width, ff = late[0].shape[1], late[2].shape[2]
     return pl.pallas_call(
         functools.partial(attend_back_kernel, n),
         out_shape=(shape((3, span, cols), BF16), shape((2, cols), F32))
-        + (shape((cols, width // 8), BF16),) * 3,
-        in_specs=[VM] * 7 + [HB, VM, VM, VM, HB],
+        + tuple(shape(g.shape, BF16) for g in grads),
+        in_specs=[VM] * 9 + [HB] * 8,
         out_specs=(VM, VM, HB, HB, HB),
+        input_output_aliases={14: 2, 15: 3, 16: 4},
         scratch_shapes=[
             pltpu.VMEM((span, cols), F32),
             pltpu.VMEM((4, 2, span, cols), BF16),
             pltpu.VMEM((3, 2, span, cols), BF16),
             pltpu.VMEM((2, span, cols), F32),
             pltpu.VMEM((heads, 8, span), F32),
-            pltpu.VMEM((span, width // 2), BF16),
-            pltpu.VMEM((span, width // 2), BF16),
-            pltpu.VMEM((span, cols), BF16),
-            ring[0],
-            ring[1],
             pltpu.VMEM((span, 128), F32),
             pltpu.VMEM((n, 8, span), F32),
+        ]
+        + LatePiece.scratch(span, width, ff)
+        + [
             pltpu.SemaphoreType.DMA((4,)),
             pltpu.SemaphoreType.DMA((4,)),
-            pltpu.SemaphoreType.DMA((2,)),
-            pltpu.SemaphoreType.DMA((2,)),
-            pltpu.SemaphoreType.DMA((2,)),
+            pltpu.SemaphoreType.DMA,
             pltpu.SemaphoreType.DMA((n - 1,)),
             pltpu.SemaphoreType.DMA((n - 1,)),
-        ]
-        + sems,
+        ],
         compiler_params=pltpu.CompilerParams(
             collective_id=3, has_side_effects=True, vmem_limit_bytes=VMEM_LIMIT
         ),
         name="attend_back",
-    )(q, kvall, d_out, attn32, lse, bound, attn, dbranch, proj, inv, gain, table)
+    )(q, kvall, d_out, attn32, lse, bound, proj, inv, gain, table, *late, *grads)
 
 
 def load_blocks(src, dst, sem, axis):
@@ -1304,10 +1342,15 @@
     cot_ref,
     gate_ref,
     up_ref,
+    gresid_ref,
     out_ref,
     group_out,
     dgu_ref,
     dgain_ref,
+    hidden_s,
+    resid_s,
+    dmlp_s,
+    dgu_s,
     wd,
     mlp,
     group,
@@ -1315,12 +1358,15 @@
     got_rows,
     sem_d,
     keep_sem,
+    s_send,
+    s_recv,
     *sems,
 ):
     s, c, u = where_am_i()
     rows, width = resid_ref.shape
     load_d = load_blocks(wd_ref, wd, sem_d, 1)
-    greet(line_peers(n))
+    greet(line_peers(n) + [(None, (1 - s, c, u))])
+    sibling = Sibling(s_send, s_recv)
     wait_all(load_d)
     chunk_cols = width // part.shape[0]
     span = n * rows
@@ -1336,7 +1382,12 @@
 
         lax.fori_loop(0, count, tile, 0)
 
-    LineReduce(n, rows, part, got_rows, sems[:4]).run(compute, mlp)
+    def hook(slot):
+        if slot == 0:
+            sibling.start(hidden_ref, hidden_s)
+            sibling.start(half_columns(gresid_ref, 1 - s), resid_s)
+
+    LineReduce(n, rows, part, got_rows, sems[:4]).run(compute, mlp, hook)
     values = mlp[...]
     inverse = inverse_rms(values)
     grad = cot_ref[...].astype(F32)
@@ -1352,6 +1403,7 @@
     gather.finish()
     keep = pltpu.make_async_copy(group, group_out, keep_sem)
     keep.start()
+    sibling.start(half_columns(group, 1 - s), dmlp_s)
     ntile, tsize = tiles(gate_ref.shape[1], 512)
 
     def body(i, carry):
@@ -1370,11 +1422,17 @@
 
         return lax.fori_loop(0, count, tile, carry)
 
-    lax.fori_loop(0, ntile, body, 0)
+    for i in range(ntile):
+        body(i, 0)
+        lanes = pl.ds(i * tsize, tsize)
+        sibling.start(dgu_ref.at[:, :, lanes], dgu_s.at[:, :, lanes])
+    for i in range(3 + ntile):
+        sibling.wait(i)
+    sibling.finish()
     keep.wait()
 
 
-def mlp_out(n, hidden, wd, resid, gain, cot, gate, up):
+def mlp_out(n, hidden, wd, resid, gain, cot, gate, up, gresid):
     rows, width = resid.shape
     span, ff = hidden.shape
     return pl.pallas_call(
@@ -1384,28 +1442,37 @@
             shape((span, width), BF16),
             shape((2, span, ff), BF16),
             shape((1, width), F32),
+            shape((span, ff), BF16),
+            shape((span, width // 2), BF16),
+            shape((span, width // 2), BF16),
+            shape((2, span, ff), BF16),
         ),
-        in_specs=[VM, HB, VM, VM, VM, VM, VM],
-        out_specs=(VM, HB, VM, VM),
+        in_specs=[VM, HB, VM, VM, VM, VM, VM, HB],
+        out_specs=(VM, HB, VM, VM, HB, HB, HB, HB),
         scratch_shapes=[
             pltpu.VMEM((ff, width), BF16),
             pltpu.VMEM((rows, width), F32),
             pltpu.VMEM((span, width), BF16),
         ]
         + reduce_scratch(n, rows, width)
-        + [pltpu.SemaphoreType.DMA((8,)), pltpu.SemaphoreType.DMA]
+        + [
+            pltpu.SemaphoreType.DMA((8,)),
+            pltpu.SemaphoreType.DMA,
+            pltpu.SemaphoreType.DMA((3 + tiles(ff, 512)[0],)),
+            pltpu.SemaphoreType.DMA((3 + tiles(ff, 512)[0],)),
+        ]
         + line_sems(n, CHUNKS)
         + line_sems(n),
         compiler_params=pltpu.CompilerParams(
             collective_id=5, has_side_effects=True, vmem_limit_bytes=VMEM_LIMIT
         ),
         name="mlp_out",
-    )(hidden, wd, resid, gain, cot, gate, up)
+    )(hidden, wd, resid, gain, cot, gate, up, gresid)
 
 
 def mlp_back_kernel(
     n,
-    dgu_ref,
+    dgu_hbm,
     wga_ref,
     wgb_ref,
     wgc_ref,
@@ -1413,9 +1480,13 @@
     branch_ref,
     gain_ref,
     wo_ref,
-    hidden_ref,
-    dmlp_ref,
-    resid_ref,
+    hidden_hbm,
+    dmlp_hbm,
+    resid_hbm,
+    hidden_s_hbm,
+    dmlp_s_hbm,
+    resid_s_hbm,
+    dgu_s_hbm,
     dresid_ref,
     group_out,
     dattn_ref,
@@ -1431,20 +1502,19 @@
     group,
     part,
     got_rows,
+    dgu_ref,
+    hidden,
+    hidden_s,
     dmlp,
-    resid,
-    hidden_s,
     dmlp_s,
-    resid_s,
-    dgu_s,
+    gate_in,
     ring_d,
     ring_g,
     got_d,
     got_g,
     sem_o,
+    sem_in,
     local_sem,
-    s_send,
-    s_recv,
     d_send,
     d_recv,
     d_local,
@@ -1477,21 +1547,31 @@
         for copy in load_chunk(chunk):
             copy.start()
 
+    def fetch(k, src, dst):
+        copy = pltpu.make_async_copy(src, dst, sem_in.at[k])
+        copy.start()
+        return copy
+
+    load_dgu = fetch(0, dgu_hbm, dgu_ref)
     start_chunk(0)
+    load_d = [
+        fetch(1, hidden_hbm, hidden),
+        fetch(2, half_columns(dmlp_hbm, s), dmlp),
+        fetch(3, hidden_s_hbm, hidden_s),
+        fetch(4, dmlp_s_hbm, dmlp_s),
+    ]
     start_chunk(1)
-    load_m = [
-        pltpu.make_async_copy(half_columns(dmlp_ref, s), dmlp, local_sem.at[2, 0]),
-        pltpu.make_async_copy(half_columns(resid_ref, s), resid, local_sem.at[2, 1]),
-    ]
-    for copy in load_m:
-        copy.start()
+    load_g = []
+    if gate_in:
+        resid, resid_s, dgu_s = gate_in
+        load_g = [
+            fetch(5, half_columns(resid_hbm, s), resid),
+            fetch(6, resid_s_hbm, resid_s),
+            fetch(7, dgu_s_hbm, dgu_s),
+        ]
     load_o = load_blocks(wo_ref, wo, sem_o, 1)
-    greet(line_peers(n) + plane_peers() + [(None, (1 - s, c, u))])
-    sibling = Sibling(s_send, s_recv)
-    sibling.start(half_columns(dmlp_ref, 1 - s), dmlp_s)
-    sibling.start(hidden_ref, hidden_s)
-    sibling.start(half_columns(resid_ref, 1 - s), resid_s)
-    sibling.start(dgu_ref, dgu_s)
+    greet(line_peers(n) + plane_peers())
+    load_dgu.wait()
     span = n * rows
     count, size = tiles(span, 512)
 
@@ -1512,7 +1592,7 @@
             start_chunk(chunk + 2)
 
     rows_d, cols_g = ring_d.shape[2], ring_g.shape[3]
-    tiles_g = dgu_ref.shape[2] // cols_g
+    tiles_g = dgu_hbm.shape[2] // cols_g
 
     def place_d(out, piece, part):
         size = rows_d if part is None else rows_d // 2
@@ -1528,31 +1608,33 @@
     )
     gate = PlaneReduce(ring_g, got_g, (gown_out, gx_out, gy_out), place_g, g_send, g_recv, g_local)
     down_piece = wide_piece(
-        (hidden_ref, dmlp), (hidden_s, dmlp_s), lambda p: slice(p * rows_d, (p + 1) * rows_d)
+        (hidden, dmlp), (hidden_s, dmlp_s), lambda p: slice(p * rows_d, (p + 1) * rows_d)
     )
 
     def gate_right(ref, piece):
         tile = piece % tiles_g
         return ref[piece // tiles_g, :, tile * cols_g : (tile + 1) * cols_g]
 
-    gate_piece = tall_piece((resid, dgu_ref), (resid_s, dgu_s), gate_right)
-    n_d, n_g = got_d.shape[0], got_g.shape[0]
-    pieces = Pieces(
-        [(down, p, down_piece) for p in range(n_d)] + [(gate, p, gate_piece) for p in range(n_g)]
-    )
+    n_d, n_g = got_d.shape[0], got_g.shape[0] if gate_in else 0
+    work = [(down, p, down_piece) for p in range(n_d)]
+    if gate_in:
+        gate_piece = tall_piece((resid, dgu_ref), (resid_s, dgu_s), gate_right)
+        work += [(gate, p, gate_piece) for p in range(n_g)]
+    pieces = Pieces(work)
+
+    def compute_and_piece(chunk):
+        compute(chunk)
+        if chunk == 0:
+            wait_all(load_d)
+        if chunk < 2:
+            pieces.step()
 
     def reduce_hook(slot):
         if slot == 0:
-            wait_all(load_m)
-            sibling.wait(0)
-            sibling.wait(1)
-            pieces.step(2)
-        if slot == 1:
-            pieces.step()
-        if slot == 2:
-            pieces.step()
-
-    LineReduce(n, rows, part, got_rows, sems[:4]).run(compute, dresid_ref, reduce_hook)
+            wait_all(load_g)
+        pieces.step()
+
+    LineReduce(n, rows, part, got_rows, sems[:4]).run(compute_and_piece, dresid_ref, reduce_hook)
     d_resid = dresid_ref[...] + cot_ref[...].astype(F32)
     dresid_ref[...] = d_resid
     branch = branch_ref[...]
@@ -1573,19 +1655,15 @@
     gather.send(0)
     dgain_ref[...] = jnp.sum(d_resid * branch * inverse, axis=0, keepdims=True)
     wait_all(load_o)
-    sibling.wait(2)
-    sibling.wait(3)
     pieces.step()
 
     def gather_hook(slot):
-        if slot < 2:
-            pieces.step()
+        pieces.step()
 
     gather.run(gather_hook)
     if small:
         keep = pltpu.make_async_copy(group, group_out, local_sem.at[2, 2])
         keep.start()
-    pieces.step()
 
     def tile(j, carry):
         where = pl.ds(pl.multiple_of(j * size, size), size)
@@ -1603,7 +1681,6 @@
     pieces.finish()
     down.finish(n_d)
     gate.finish(n_g)
-    sibling.finish()
     if small:
         keep.wait()
 
@@ -1619,14 +1696,32 @@
     )
 
 
-def mlp_back(n, dgu, wga, wgb, wgc, cot, branch, gain, wo, hidden, dmlp, resid):
+def mlp_back(
+    n,
+    dgu,
+    wga,
+    wgb,
+    wgc,
+    cot,
+    branch,
+    gain,
+    wo,
+    hidden,
+    dmlp,
+    resid,
+    hidden_s,
+    resid_s,
+    dmlp_s,
+    dgu_s,
+):
     rows, width = branch.shape
     span, ff = dgu.shape[1:]
     cols = wo.shape[1]
     kb, kc = width // 8, wo.shape[2]
     count, size = tiles(ff, 512)
     ring_d, sems_d = piece_scratch(min(3, count), count, size, kc)
-    ring_g, sems_g = piece_scratch(3 if count > 1 else 2, 2 * count, kb, size)
+    here = 2 * count - LATER
+    ring_g, sems_g = piece_scratch(min(3, max(here, 1)), max(here, 1), kb, size)
     chunk_blocks = width // CHUNKS // kb
     return pl.pallas_call(
         functools.partial(mlp_back_kernel, n),
@@ -1638,7 +1733,7 @@
         )
         + (shape((2, kb, ff), BF16),) * 3
         + (shape((ff, kc), BF16),) * 3,
-        in_specs=[VM, HB, HB, HB, VM, VM, VM, HB, VM, HB, HB],
+        in_specs=[HB, HB, HB, HB, VM, VM, VM] + [HB] * 8,
         out_specs=(VM, HB, VM, VM) + (HB,) * 6,
         scratch_shapes=[
             pltpu.VMEM((cols, width), BF16),
@@ -1647,20 +1742,25 @@
         ]
         + reduce_scratch(n, rows, width)
         + [
-            pltpu.VMEM((span, width // 2), BF16),
-            pltpu.VMEM((span, width // 2), BF16),
+            pltpu.VMEM((2, span, ff), BF16),
+            pltpu.VMEM((span, ff), BF16),
             pltpu.VMEM((span, ff), BF16),
             pltpu.VMEM((span, width // 2), BF16),
             pltpu.VMEM((span, width // 2), BF16),
-            pltpu.VMEM((2, span, ff), BF16),
+            (
+                pltpu.VMEM((span, width // 2), BF16),
+                pltpu.VMEM((span, width // 2), BF16),
+                pltpu.VMEM((2, span, ff), BF16),
+            )
+            if here > 0
+            else (),
             ring_d[0],
             ring_g[0],
             ring_d[1],
             ring_g[1],
             pltpu.SemaphoreType.DMA((8,)),
+            pltpu.SemaphoreType.DMA((8,)),
             pltpu.SemaphoreType.DMA((3, 3)),
-            pltpu.SemaphoreType.DMA((4,)),
-            pltpu.SemaphoreType.DMA((4,)),
         ]
         + sems_d
         + sems_g
@@ -1670,7 +1770,23 @@
             collective_id=6, has_side_effects=True, vmem_limit_bytes=VMEM_LIMIT
         ),
         name="mlp_back",
-    )(dgu, wga, wgb, wgc, cot, branch, gain, wo, hidden, dmlp, resid)
+    )(
+        dgu,
+        wga,
+        wgb,
+        wgc,
+        cot,
+        branch,
+        gain,
+        wo,
+        hidden,
+        dmlp,
+        resid,
+        hidden_s,
+        dmlp_s,
+        resid_s,
+        dgu_s,
+    )
 
 
 def proj_back_kernel(
@@ -1682,21 +1798,44 @@
     gcols_ref,
     gattn_ref,
     gmlp_ref,
+    attn_ref,
+    dbranch_ref,
+    resid_hbm,
+    resid_s_hbm,
+    dgu_hbm,
+    dgu_s_hbm,
+    own_in,
+    x_in,
+    y_in,
     out_ref,
     gain_ref,
     own_out,
     x_out,
     y_out,
+    oown_out,
+    ox_out,
+    oy_out,
+    gown_out,
+    gx_out,
+    gy_out,
     wq,
     xs,
     xs_s,
     dproj_s,
+    dbranch,
+    dbranch_s,
+    attn_s,
     total,
     part,
     got_rows,
     ring,
     got,
     sums,
+    ring_o,
+    got_o,
+    late_buffers,
+    late_sems,
+    o_sems,
     local_sem,
     s_send,
     s_recv,
@@ -1715,7 +1854,17 @@
     load = [
         pltpu.make_async_copy(wq_ref, wq, local_sem.at[0]),
         pltpu.make_async_copy(half_columns(xg_ref, s), xs, local_sem.at[1]),
+        pltpu.make_async_copy(half_columns(dbranch_ref, s), dbranch, local_sem.at[2]),
     ]
+    last = 2 * (dgu_hbm.shape[2] // late_buffers[2].shape[1])
+    late = LatePiece(
+        last - 1,
+        (resid_hbm, resid_s_hbm, dgu_hbm, dgu_s_hbm),
+        (gown_out, gx_out, gy_out),
+        late_buffers,
+        late_sems,
+    )
+    late.load()
     for copy in load:
         copy.start()
     corner = (s, c ^ 3, u)
@@ -1723,6 +1872,8 @@
     gains = GainSum(n, sums, (v_send, v_recv, m_send, m_recv))
     gains.start(gcols_ref, gattn_ref, gmlp_ref)
     sibling = Sibling(s_send, s_recv)
+    sibling.start(attn_ref, attn_s)
+    sibling.start(half_columns(dbranch_ref, 1 - s), dbranch_s)
     sibling.start(half_columns(xg_ref, 1 - s), xs_s)
     sibling.start(dproj_ref, dproj_s)
     load[0].wait()
@@ -1749,24 +1900,47 @@
 
     weight = PlaneReduce(ring, got, (own_out, x_out, y_out), place, q_send, q_recv, q_local)
     compute_piece = tall_piece((xs, dproj_ref), (xs_s, dproj_s), lambda ref, piece: ref[piece])
-    pieces = Pieces([(weight, p, compute_piece) for p in range(3)])
+
+    def place_o(out, piece, part):
+        size = ring_o.shape[2] if part is None else ring_o.shape[2] // 2
+        return out.at[pl.ds((part or 0) * size, size)]
+
+    out_weight = PlaneReduce(ring_o, got_o, (oown_out, ox_out, oy_out), place_o, *o_sems)
+    out_piece = wide_piece((attn_ref, dbranch), (attn_s, dbranch_s), lambda p: slice(None))
+    pieces = Pieces(
+        [late.work(), (out_weight, 0, out_piece)] + [(weight, p, compute_piece) for p in range(3)]
+    )
+
+    def compute_and_piece(chunk):
+        compute(chunk)
+        if chunk == 0:
+            pieces.step()
+        if chunk == 2:
+            load[2].wait()
+            sibling.wait(0)
+            sibling.wait(1)
+            pieces.step()
 
     def hook(slot):
         if slot == 0:
             load[1].wait()
-            sibling.wait(0)
-            sibling.wait(1)
-            pieces.step(3)
+            sibling.wait(2)
+            sibling.wait(3)
+            pieces.step()
             gains.over_ctx()
         if slot == 1:
-            pieces.catch_up()
+            pieces.step()
             gains.over_uly()
-
-    LineReduce(n, rows, part, got_rows, sems[:4]).run(compute, total, hook)
+        if slot == 2:
+            pieces.step()
+
+    LineReduce(n, rows, part, got_rows, sems[:4]).run(compute_and_piece, total, hook)
     out_ref[...] = (dresid_ref[...] + total[...]).astype(BF16)
     pieces.finish()
     gains.finish(gain_ref)
     weight.finish(3)
+    out_weight.finish(1)
+    late.plane.finish(1)
     sibling.finish()
 
 
@@ -1837,21 +2011,31 @@
             copy.wait_send()
 
 
-def proj_back(n, dproj, wq, dresid, xg, gain_cols, gain_attn, gain_mlp):
+def proj_back(
+    n, dproj, wq, dresid, xg, gain_cols, gain_attn, gain_mlp, attn, dbranch, late, grads
+):
     rows, width = dresid.shape
     span, cols = dproj.shape[1:]
     ring, sems = piece_scratch(3, 3, width // 8, cols)
+    ring_o, sems_o = piece_scratch(1, 1, cols, width // 8)
+    ff = late[2].shape[2]
     return pl.pallas_call(
         functools.partial(proj_back_kernel, n),
         out_shape=(shape((rows, width), BF16), shape((4, width // 8), F32))
-        + (shape((3, width // 8, cols), BF16),) * 3,
-        in_specs=[VM, HB, VM, HB, VM, VM, VM],
-        out_specs=(VM, VM, HB, HB, HB),
+        + (shape((3, width // 8, cols), BF16),) * 3
+        + (shape((cols, width // 8), BF16),) * 3
+        + tuple(shape(g.shape, BF16) for g in grads),
+        in_specs=[VM, HB, VM, HB, VM, VM, VM, VM] + [HB] * 8,
+        out_specs=(VM, VM) + (HB,) * 9,
+        input_output_aliases={13: 8, 14: 9, 15: 10},
         scratch_shapes=[
             pltpu.VMEM((3, width, cols), BF16),
             pltpu.VMEM((span, width // 2), BF16),
             pltpu.VMEM((span, width // 2), BF16),
             pltpu.VMEM((3, span, cols), BF16),
+            pltpu.VMEM((span, width // 2), BF16),
+            pltpu.VMEM((span, width // 2), BF16),
+            pltpu.VMEM((span, cols), BF16),
             pltpu.VMEM((rows, width), F32),
         ]
         + reduce_scratch(n, rows, width)
@@ -1863,9 +2047,14 @@
                 pltpu.VMEM((4, 8, width // 8), F32),
                 pltpu.VMEM((3 + n, 8, width // 8), F32),
             ),
-            pltpu.SemaphoreType.DMA((2,)),
-            pltpu.SemaphoreType.DMA((2,)),
-            pltpu.SemaphoreType.DMA((2,)),
+        ]
+        + ring_o
+        + LatePiece.scratch(span, width, ff)
+        + [
+            tuple(sems_o),
+            pltpu.SemaphoreType.DMA((3,)),
+            pltpu.SemaphoreType.DMA((4,)),
+            pltpu.SemaphoreType.DMA((4,)),
         ]
         + sems
         + [
@@ -1879,7 +2068,19 @@
             collective_id=7, has_side_effects=True, vmem_limit_bytes=VMEM_LIMIT
         ),
         name="proj_back",
-    )(dproj, wq, dresid, xg, gain_cols, gain_attn, gain_mlp)
+    )(
+        dproj,
+        wq,
+        dresid,
+        xg,
+        gain_cols,
+        gain_attn,
+        gain_mlp,
+        attn,
+        dbranch,
+        *late,
+        *grads,
+    )
 
 
 def rope_table(length):
@@ -1914,16 +2115,47 @@
     branch, resid, group_resid, gate, up, hidden, wgb, wgc, wd = mlp_in(
         n, attn, wo, x, post_gain, wga, gate_up, down_weight
     )
-    block_out, group_dmlp, dgu, gain_mlp = mlp_out(n, hidden, wd, resid, post_gain, cot, gate, up)
+    block_out, group_dmlp, dgu, gain_mlp, hidden_s, resid_s, dmlp_s, dgu_s = mlp_out(
+        n, hidden, wd, resid, post_gain, cot, gate, up, group_resid
+    )
     d_resid, group_dbranch, d_attn, gain_attn, *grads = mlp_back(
-        n, dgu, wga, wgb, wgc, cot, branch, post_gain, wo, hidden, group_dmlp, group_resid
+        n,
+        dgu,
+        wga,
+        wgb,
+        wgc,
+        cot,
+        branch,
+        post_gain,
+        wo,
+        hidden,
+        group_dmlp,
+        group_resid,
+        hidden_s,
+        resid_s,
+        dmlp_s,
+        dgu_s,
     )
-    d_proj, gain_cols, *out_grads = attend_back(
-        n, q, kvall, d_attn, attn32, lse, bound, attn, group_dbranch, proj, inv, qk_gain, table
+    gate_grads, down_grads = grads[:3], grads[3:]
+    late = (group_resid, resid_s, dgu, dgu_s)
+    d_proj, gain_cols, *gate_grads = attend_back(
+        n, q, kvall, d_attn, attn32, lse, bound, proj, inv, qk_gain, table, late, gate_grads
     )
-    input_grad, gain_part, *qkv_grads = proj_back(
-        n, d_proj, wq, d_resid, group_x, gain_cols, gain_attn, gain_mlp
+    input_grad, gain_part, *grads = proj_back(
+        n,
+        d_proj,
+        wq,
+        d_resid,
+        group_x,
+        gain_cols,
+        gain_attn,
+        gain_mlp,
+        attn,
+        group_dbranch,
+        late,
+        gate_grads,
     )
+    qkv_grads, out_grads, gate_grads = grads[:3], grads[3:6], grads[6:]
 
     def total(parts):
         return parts[0].astype(F32) + parts[1].astype(F32) + parts[2].astype(F32)
@@ -1933,8 +2165,8 @@
         input_grad[None],
         total(qkv_grads),
         total(out_grads),
-        total(grads[:3]),
-        total(grads[3:]),
+        total(gate_grads),
+        total(down_grads),
         gain_part,
     )
 

time: 562 us -> 546 us (0.972)
  Pallas kernels: 540 us -> 523 us
    pallas_call x1, Pallas kernels: 133 us -> 114 us  [mlp_back(): pl.pallas_call(functools.partial(mlp_back_kernel, n), out_shape=(shape((r...]
where the time goes in v3:
time: 546 us; the launch traced here: 538 us
  Pallas kernels  523 us (96%)
  other arithmetic  10.2 us (2%)
    pallas_call x1, Pallas kernels, mlp_back(): pl.pallas_call(functools.partial(mlp_back_kernel, n), out_shape=(shape((r...  114 us
    pallas_call x1, Pallas kernels, mlp_in(): pl.pallas_call(functools.partial(mlp_in_kernel, n), out_shape=(shape((row...  98.2 us
    pallas_call x1, Pallas kernels, mlp_out(): pl.pallas_call(functools.partial(mlp_out_kernel, n), out_shape=(shape((ro...  93.3 us
    pallas_call x1, Pallas kernels, project(): pl.pallas_call(functools.partial(proj_kernel, n), out_shape=(shape((span,...  65.8 us
    pallas_call x1, Pallas kernels, attend_back(): pl.pallas_call(functools.partial(attend_back_kernel, n), out_shape=(shape...  55.5 us
    pallas_call x1, Pallas kernels, proj_back(): pl.pallas_call(functools.partial(proj_back_kernel, n), out_shape=(shape((...  52.3 us
    pallas_call x1, Pallas kernels, attend(): pl.pallas_call(attend_kernel, out_shape=(shape((4, 2, span, cols), BF16),...  43.7 us

profile of v3, /device:TPU:0, one launch (start us, length us, event | category | flops | bytes accessed | tf_op | source)
XLA Modules:
  0.0 537.9 jit_solution(1721041514380225433)
XLA Ops:
  0.6 65.8 %project.1 = (bf16[512,2048]{1,0:T(8,128)(2,1)}, bf16[3,2048,512]{2,1,0:T(8,128)(2,1)}, bf16[8,512,256]{2,1,0:T(8,128)(2,1)}, bf16[8,128,2048]{2,1,0:T(8,128)(2,...) custom-call(bf16[128,2048]{1,0:T(8,128)(2,1)} %bitcast.6, ...), custom_call_target="tpu_custom_call" | custom-call | tf_op jit(solution)/shard_map/project/pallas_call | solution.py:730
  66.5 43.7 %attend.1 = (bf16[4,2,512,512]{3,2,1,0:T(8,128)(2,1)}, bf16[512,512]{1,0:T(8,128)(2,1)}, f32[512,512]{1,0:T(8,128)}, f32[4,8,512]{2,1,0:T(8,128)}, s32[8,128]{1,0:T(8,128)}) custom-call(bf16[512,512]{1,0:T(8,128)(2,1)} %get-tuple-element.64.q_ref, bf16[2,512,512]{2,1,0:T(8,128)(2,1)} %get-tuple-element.65.kv_ref, f32[8,128]{1,0:T(8,128)} %get-tuple-element.66.zero_ref), custom_call_target="tpu_custom_call" | custom-call | tf_op jit(solution)/shard_map/attend/pallas_call | solution.py:904
  110.2 98.2 %mlp_in.1 = (f32[128,2048]{1,0:T(8,128)}, f32[128,2048]{1,0:T(8,128)}, bf16[512,2048]{1,0:T(8,128)(2,1)}, bf16[512,2048]{1,0:T(8,128)(2,1)}, bf16[512,2048]{1,0:...) custom-call(bf16[512,512]{1,0:T(8,128)(2,1)} %get-tuple-element.67.a, ...), custom_call_target="tpu_custom_call" | custom-call | tf_op jit(solution)/shard_map/mlp_in/pallas_call | solution.py:1300
  208.4 93.3 %mlp_out.1 = (bf16[128,2048]{1,0:T(8,128)(2,1)}, bf16[512,2048]{1,0:T(8,128)(2,1)}, bf16[2,512,2048]{2,1,0:T(8,128)(2,1)}, f32[1,2048]{1,0:T(1,128)}, bf16[512,2...) custom-call(bf16[512,2048]{1,0:T(8,128)(2,1)} %get-tuple-element.70.hidd, ...), custom_call_target="tpu_custom_call" | custom-call | tf_op jit(solution)/shard_map/mlp_out/pallas_call | solution.py:1438
  301.7 114.4 %mlp_back.1 = (f32[128,2048]{1,0:T(8,128)}, bf16[512,2048]{1,0:T(8,128)(2,1)}, bf16[512,512]{1,0:T(8,128)(2,1)}, f32[1,2048]{1,0:T(1,128)}, bf16[2,256,2048]{2,1...) custom-call(bf16[2,512,2048]{2,1,0:T(8,128)(2,1)} %get-tuple-element, ...), custom_call_target="tpu_custom_call" | custom-call | tf_op jit(solution)/shard_map/mlp_back/pallas_call | solution.py:1726
  416.1 55.5 %attend_back.1 = (bf16[3,512,512]{2,1,0:T(8,128)(2,1)}, f32[2,512]{1,0:T(2,128)}, bf16[2,256,2048]{2,1,0:T(8,128)(2,1)}, bf16[2,256,2048]{2,1,0:T(8,128)(2,1)}, bf16[2,256,2048]{2,1,0:T(8,128)(2,1)}) custom-call(bf16[512,512]{1,0:T(8,128)(2,1)} %get-tuple-element.64.q_ref, ...), custom_call_target="tpu_custom_call", output_to_operand_aliasing={{2}: (14, {}), {3}: (15, {}), {4}: (16, {})} | custom-call | tf_op jit(solution)/shard_map/attend_back/pallas_call | solution.py:1118
  471.6 52.3 %proj_back.1 = (bf16[128,2048]{1,0:T(8,128)(2,1)}, f32[4,256]{1,0:T(4,128)}, bf16[3,256,512]{2,1,0:T(8,128)(2,1)}, bf16[3,256,512]{2,1,0:T(8,128)(2,1)}, bf16[3,...) custom-call(bf16[3,512,512]{2,1,0:T(8,128)(2,1)} %get-tuple-element., ...), custom_call_target="tpu_custom_call", output_to_operand_aliasing={{8}: (13, {}), {9}: (14, {}), {10}: (15, {})} | custom-call | tf_op jit(solution)/shard_map/proj_back/pallas_call | solution.py:2022
  523.9 0.0 copy-start.4
  523.9 0.0 copy-start.5
  523.9 2.1 convert_add_fusion.3
  526.1 3.2 convert_add_fusion.2
  529.3 0.0 copy-done.4
  529.3 0.0 copy-done.5
  529.3 0.0 copy-done.3
  529.3 0.0 copy-start
  529.3 0.0 copy-start.1
  529.3 1.7 convert_add_fusion.1
  531.0 0.5 copy-done
  531.5 0.7 copy-done.1
  532.3 3.2 convert_add_fusion
  535.5 0.8 copy.32
  536.3 0.0 copy-done.7
  536.3 0.8 copy.33
  537.1 0.6 copy.34
  (8 shorter events, 0.0 us)
Async XLA Ops:
  523.9 5.4 %copy-start.4 = (bf16[2048,256]{1,0:T(8,128)(2,1)S(1)}, bf16[2048,256]{1,0:T(8,128)(2,1)}, u32[]{:S(2)}) copy-start(bf16[2048,256]{1,0:T(8,128)(2,1)} %get-tuple-element.118) | copy-start | bytes 3145732
  523.9 5.4 copy-start.5
  526.1 3.2 copy-start.3
  526.1 4.9 copy-start.2
  529.3 2.2 copy-start
  529.3 3.0 copy-start.1
  532.3 3.2 copy-start.6
  532.3 4.0 copy-start.7
  535.5 1.6 copy-start.8

commit v4 on v3

--- a/solution.py
+++ b/solution.py
@@ -82,13 +82,18 @@
 
 
 class LineGather:
-    def __init__(self, n, rows, buf, sems):
-        self.n, self.rows, self.buf, self.sems = n, rows, buf, sems
+    def __init__(self, n, rows, buf, sems, part=None):
+        self.n, self.rows, self.buf, self.sems, self.part = n, rows, buf, sems, part
 
     def copy(self, right, slot, shard):
         s, c, u = where_am_i()
         send_r, recv_r, send_l, recv_l = self.sems
-        view = self.buf.at[rows_of(shard, self.rows)]
+        if self.part is None:
+            view = self.buf.at[rows_of(shard, self.rows)]
+        else:
+            index, size = self.part
+            view = self.buf.at[shard, pl.ds(index * size, size)]
+            send_r, recv_r, send_l, recv_l = [sem.at[:, index] for sem in self.sems]
         if right:
             return remote(view, view, send_r.at[slot], recv_r.at[slot], (s, c, u + 1))
         return remote(view, view, send_l.at[slot], recv_l.at[slot], (s, c, u - 1))
@@ -199,12 +204,13 @@
 
             self.copy(False, slot, chunk, block_l).start()
 
-    def last(self, out):
+    def last(self, out, chunks=None):
         u, n = lax.axis_index("uly"), self.n
         where = rows_of(u, self.rows)
         width = self.part.shape[2]
-        for chunk in range(self.chunks):
-            cols = slice(chunk * width, (chunk + 1) * width)
+        chunks = range(self.chunks) if chunks is None else chunks
+        for number, chunk in enumerate(chunks):
+            cols = slice(number * width, (number + 1) * width)
             out[:, cols] = self.part[chunk, where, :].astype(F32)
 
             @pl.when(u > 0)
@@ -240,6 +246,79 @@
                 hook(slot)
         self.last(out)
         self.finish()
+
+
+def reduce_norm_gather(n, reduce, gathers, compute, finish, consume, hook):
+    per_half = reduce.chunks // 2
+    slots = n - 1
+    chunks = [range(h * per_half, (h + 1) * per_half) for h in range(2)]
+    for chunk in chunks[0]:
+        compute(chunk)
+        reduce.step(0, chunk)
+    for chunk in chunks[1]:
+        compute(chunk)
+    for slot in range(1, slots):
+        for chunk in chunks[0]:
+            reduce.step(slot, chunk)
+    for chunk in chunks[1]:
+        reduce.step(0, chunk)
+    hook("sent")
+    finish(0)
+    gathers[0].send(0)
+    hook("half")
+    for slot in range(1, slots):
+        for chunk in chunks[1]:
+            reduce.step(slot, chunk)
+        gathers[0].wait(slot - 1)
+        hook(f"b{slot}")
+    finish(1)
+    gathers[1].send(0)
+    gathers[0].wait(slots - 1)
+    hook("first")
+    tiles = consume.tiles
+    done = 0
+    for slot in range(slots):
+        while done < tiles * (slot + 1) // slots:
+            consume(0, done)
+            done += 1
+        gathers[1].wait(slot)
+        hook(f"g{slot}")
+    for tile in range(tiles):
+        consume(1, tile)
+        hook(f"t{tile}")
+    reduce.finish()
+    for gather in gathers:
+        gather.finish()
+
+
+class Halves:
+    def __init__(self, n, rows):
+        self.n, self.half = n, rows // 2
+        self.per_tile = min(n, max(512 // self.half, 1))
+        self.count = n // self.per_tile
+
+    def each(self, half, body):
+        size = self.per_tile * self.half
+        for t in range(self.count):
+            index = (pl.ds(t * self.per_tile, self.per_tile), pl.ds(half * self.half, self.half))
+            body(index, t * size, size)
+
+    def load(self, ref, index, lanes=slice(None)):
+        value = ref[index[0], index[1], lanes]
+        return value.reshape(value.shape[0] * value.shape[1], value.shape[2])
+
+    def store(self, ref, index, lanes, value):
+        ref[index[0], index[1], lanes] = value.reshape(
+            self.per_tile, self.half, value.shape[1]
+        )
+
+
+class Consume:
+    def __init__(self, tiles, body):
+        self.tiles, self.body = tiles, body
+
+    def __call__(self, half, tile):
+        self.body(half, tile)
 
 
 class PlaneGather:
@@ -611,6 +690,10 @@
     return [(None, (s, c, lax.rem(u + k, n))) for k in range(1, n)]
 
 
+def spread_heads(cols):
+    return cols % (4 * HEAD_DIM) == 0
+
+
 def proj_kernel(
     n,
     x_ref,
@@ -625,8 +708,7 @@
     wo_out,
     wga_out,
     proj_ref,
-    q_ref,
-    kv_ref,
+    qkv_refs,
     inv_ref,
     zero_ref,
     xg,
@@ -683,12 +765,24 @@
 
     count, size = tiles(span, 512)
 
+    def store(i, where, first, values):
+        if len(qkv_refs) == 1:
+            (ref,) = qkv_refs
+            size = ref.shape[3]
+            for at in range(0, values.shape[1], min(size, values.shape[1])):
+                group, inside = divmod(first + at, size)
+                part = values[:, at : at + size]
+                ref[group, i, where, inside : inside + part.shape[1]] = part
+        else:
+            ref = qkv_refs[0] if i == 0 else qkv_refs[1].at[i - 1]
+            ref[where, first : first + values.shape[1]] = values
+
     def project(i, carry):
         where = pl.ds(pl.multiple_of(i * size, size), size)
         xs = xg[where, :]
         proj_ref[0, where, :] = dot(xs, wq[0], NN)
         proj_ref[1, where, :] = dot(xs, wq[1], NN)
-        kv_ref[1, where, :] = dot(xs, wq[2], NN).astype(BF16)
+        store(2, where, 0, dot(xs, wq[2], NN).astype(BF16))
         return carry
 
     lax.fori_loop(0, count, project, 0)
@@ -711,10 +805,7 @@
             cols = slice(h * HEAD_DIM, (h + 1) * HEAD_DIM)
             v = proj_ref[i, :, cols] * inverse * gain_ref[i : i + 1, cols]
             v = (v * cosine + pltpu.roll(v, HALF, 1) * sine).astype(BF16)
-            if i == 0:
-                q_ref[:, cols] = v
-            else:
-                kv_ref[0, :, cols] = v
+            store(i, slice(None), h * HEAD_DIM, v)
     second.arrive()
     third.corner()
     third.arrive()
@@ -727,6 +818,10 @@
 def project(n, x, w, table, gain, seg, wo, gu):
     rows, width = x.shape
     span, cols = n * rows, w.shape[2]
+    if spread_heads(cols):
+        qkv = (shape((4, 3, span, cols // 4), BF16),)
+    else:
+        qkv = (shape((span, cols), BF16), shape((2, span, cols), BF16))
     return pl.pallas_call(
         functools.partial(proj_kernel, n),
         out_shape=(
@@ -735,13 +830,12 @@
             shape((8,) + wo.shape, BF16),
             shape((8, gu.shape[1] // 2, gu.shape[2]), BF16),
             shape((2, span, cols), F32),
-            shape((span, cols), BF16),
-            shape((2, span, cols), BF16),
+            qkv,
             shape((span, 128), F32),
             shape((8, 128), F32),
         ),
         in_specs=[VM, HB, HB, VM, VM, HB, HB],
-        out_specs=(HB, HB, HB, HB, VM, VM, VM, VM, VM),
+        out_specs=(HB, HB, HB, HB, VM, (VM,) * len(qkv), VM, VM),
         scratch_shapes=[
             pltpu.VMEM((span, width), BF16),
             pltpu.VMEM((3, width, cols), BF16),
@@ -779,7 +873,9 @@
     q_ref,
     kv_ref,
     zero_ref,
+    gu_ref,
     kvall_out,
+    wgb_out,
     attn_ref,
     attn32_ref,
     lse_ref,
@@ -793,7 +889,10 @@
     recv,
     z_send,
     z_recv,
+    w_send,
+    w_recv,
     keep_sem,
+    w_local,
 ):
     s, c, u = where_am_i()
     span, cols = q_ref.shape
@@ -801,7 +900,8 @@
     xn, yn, dn = (s, c ^ 1, u), (s, c ^ 2, u), (s, c ^ 3, u)
     kvall[pl.ds(c, 1)] = kv_ref[...][None]
     zmsg[pl.ds(c, 1)] = zero_ref[...][None]
-    greet(plane_peers() + [(None, dn)])
+    greet(plane_peers() + [(None, dn), (None, (1 - s, c, u))])
+    weight = upper_gate(gu_ref, wgb_out, w_send, w_recv, w_local)
 
     def sent(k, view, peer):
         return remote(view, view, send.at[k], recv.at[k], peer)
@@ -881,6 +981,7 @@
     sent(3, kvall.at[bd, :, pl.ds(half, half)], xn).wait_recv()
     keep = pltpu.make_async_copy(kvall, kvall_out, keep_sem)
     keep.start()
+    weight.start()
 
     @pl.when(bd < c)
     def _():
@@ -895,23 +996,28 @@
         lse_ref[h, :1, :] = peaks[h, :1, :] + jnp.log2(total)
     for copy in copies + zs:
         copy.wait_send()
+    weight.middle()
+    weight.corner()
+    weight.arrive()
+    weight.finish()
     keep.wait()
 
 
-def attend(q, kv, zero):
+def attend(q, kv, zero, gu):
     span, cols = q.shape
     heads = cols // HEAD_DIM
     return pl.pallas_call(
         attend_kernel,
         out_shape=(
             shape((4, 2, span, cols), BF16),
+            shape((8, gu.shape[1] // 2, gu.shape[2]), BF16),
             shape((span, cols), BF16),
             shape((span, cols), F32),
             shape((heads, 8, span), F32),
             shape((8, 128), jnp.int32),
         ),
-        in_specs=[VM] * 3,
-        out_specs=(HB, VM, VM, VM, VM),
+        in_specs=[VM] * 3 + [HB],
+        out_specs=(HB, HB, VM, VM, VM, VM),
         scratch_shapes=[
             pltpu.VMEM((4, 2, span, cols), BF16),
             pltpu.VMEM((heads, 8, span), F32),
@@ -922,13 +1028,406 @@
             pltpu.SemaphoreType.DMA((4,)),
             pltpu.SemaphoreType.DMA((3,)),
             pltpu.SemaphoreType.DMA((3,)),
+            pltpu.SemaphoreType.DMA((9,)),
+            pltpu.SemaphoreType.DMA((9,)),
+            pltpu.SemaphoreType.DMA,
             pltpu.SemaphoreType.DMA,
         ],
         compiler_params=pltpu.CompilerParams(
             collective_id=2, has_side_effects=True, vmem_limit_bytes=VMEM_LIMIT
         ),
         name="attend",
-    )(q, kv, zero)
+    )(q, kv, zero, gu)
+
+
+def attend_spread_kernel(
+    qkv_ref,
+    zero_ref,
+    gu_ref,
+    all_out,
+    wgb_out,
+    attn_ref,
+    att_ref,
+    lse_ref,
+    bound_ref,
+    every,
+    peaks,
+    sums,
+    acct,
+    back,
+    zmsg,
+    send,
+    recv,
+    z_send,
+    z_recv,
+    b_send,
+    b_recv,
+    w_send,
+    w_recv,
+    keep_sem,
+    w_local,
+):
+    s, c, u = where_am_i()
+    span, cols = every.shape[2:]
+    heads = cols // HEAD_DIM
+    peers = [(s, c ^ k, u) for k in (1, 2, 3)]
+    greet([(None, peer) for peer in peers] + [(None, (1 - s, c, u))])
+    weight = upper_gate(gu_ref, wgb_out, w_send, w_recv, w_local)
+    copies, arrivals = [], []
+    zmsg[pl.ds(c, 1)] = zero_ref[...][None]
+    for k, peer in enumerate(peers):
+        there = peer[1]
+        copy = remote(qkv_ref.at[there], every.at[c], send.at[k], recv.at[k], peer)
+        copy.start()
+        small = remote(zmsg.at[c], zmsg.at[c], z_send.at[k], z_recv.at[k], peer)
+        small.start()
+        copies += [copy, small]
+        arrivals.append(remote(every.at[there], every.at[there], send.at[k], recv.at[k], peer))
+        arrivals.append(remote(zmsg.at[there], zmsg.at[there], z_send.at[k], z_recv.at[k], peer))
+    every[pl.ds(c, 1)] = qkv_ref[pl.ds(c, 1)]
+    for arrival in arrivals:
+        arrival.wait_recv()
+    weight.start()
+    keep = pltpu.make_async_copy(every, all_out, keep_sem)
+    keep.start()
+    bounds = (zmsg[0] + zmsg[1] + zmsg[2] + zmsg[3]).astype(jnp.int32)
+    bound_ref[...] = bounds
+    bound = bounds[:1, :1]
+
+    def step(k, carry):
+        i = c ^ (3 - k)
+        first_q = i * span
+        starts = segment_starts(first_q, span, bound)
+        for h in range(heads):
+            lanes = slice(h * HEAD_DIM, (h + 1) * HEAD_DIM)
+            peaks[...] = jnp.full_like(peaks, FLOOR)
+            sums[...] = jnp.zeros_like(sums)
+            acct[...] = jnp.zeros_like(acct)
+
+            def update(j, diagonal):
+                scores = dot(every[j, 1, :, lanes], every[i, 0, :, lanes], NT) * SCALE2
+                scores = score_mask(scores, j * span, first_q, starts, diagonal)
+                old = peaks[:1, :]
+                new = jnp.maximum(old, jnp.max(scores, axis=0, keepdims=True))
+                factor = jnp.exp2(old - new)
+                weights = jnp.exp2(scores - new)
+                peaks[:1, :] = new
+                sums[:1, :] = sums[:1, :] * factor + jnp.sum(weights, axis=0, keepdims=True)
+                acct[...] = acct[...] * factor + dot(
+                    every[j, 2, :, lanes], weights.astype(BF16), TN
+                )
+
+            def before(j, carry):
+                update(j, False)
+                return carry
+
+            lax.fori_loop(0, i, before, 0)
+            update(i, True)
+            total = sums[:1, :]
+            attention = acct[...] / total
+            att_ref[pl.ds(i, 1), lanes, :] = attention[None]
+            back[pl.ds(k, 1), :, lanes] = jnp.transpose(attention).astype(BF16)[None]
+            lse_ref[pl.ds(i, 1), h, :1, :] = (peaks[:1, :] + jnp.log2(total))[None]
+
+        @pl.when(k < 3)
+        def _():
+            home(k, i).start()
+
+        return carry
+
+    def home(k, i):
+        return remote(
+            back.at[k],
+            attn_ref.at[:, pl.ds(pl.multiple_of(c * cols, cols), cols)],
+            b_send.at[k],
+            b_recv.at[k],
+            (s, i, u),
+        )
+
+    lax.fori_loop(0, 4, step, 0)
+    attn_ref[:, pl.ds(pl.multiple_of(c * cols, cols), cols)] = back[3]
+    for k in range(3):
+        i = c ^ (3 - k)
+        remote(
+            back.at[k],
+            attn_ref.at[:, pl.ds(pl.multiple_of(i * cols, cols), cols)],
+            b_send.at[k],
+            b_recv.at[k],
+            (s, i, u),
+        ).wait_recv()
+        home(k, i).wait_send()
+    for copy in copies:
+        copy.wait_send()
+    weight.middle()
+    weight.corner()
+    weight.arrive()
+    weight.finish()
+    keep.wait()
+
+
+def upper_gate(gu_ref, out, send, recv, local):
+    half = gu_ref.shape[1] // 2
+    return PlaneGather(
+        gu_ref.at[0, pl.ds(half, half)], lambda b: out.at[b], half // 2, send, recv, local
+    )
+
+
+def attend_spread(qkv, zero, gu):
+    span, cols = qkv.shape[2:]
+    heads = cols // HEAD_DIM
+    return pl.pallas_call(
+        attend_spread_kernel,
+        out_shape=(
+            shape(qkv.shape, BF16),
+            shape((8, gu.shape[1] // 2, gu.shape[2]), BF16),
+            shape((span, 4 * cols), BF16),
+            shape((4, cols, span), F32),
+            shape((4, heads, 8, span), F32),
+            shape((8, 128), jnp.int32),
+        ),
+        in_specs=[VM, VM, HB],
+        out_specs=(HB, HB, VM, VM, VM, VM),
+        scratch_shapes=[
+            pltpu.VMEM(qkv.shape, BF16),
+            pltpu.VMEM((8, span), F32),
+            pltpu.VMEM((8, span), F32),
+            pltpu.VMEM((HEAD_DIM, span), F32),
+            pltpu.VMEM((4, span, cols), BF16),
+            pltpu.VMEM((4, 8, 128), F32),
+        ]
+        + [pltpu.SemaphoreType.DMA((3,))] * 6
+        + [pltpu.SemaphoreType.DMA((9,))] * 2
+        + [pltpu.SemaphoreType.DMA] * 2,
+        compiler_params=pltpu.CompilerParams(
+            collective_id=8, has_side_effects=True, vmem_limit_bytes=VMEM_LIMIT
+        ),
+        name="attend_spread",
+    )(qkv, zero, gu)
+
+
+def norms_back(n, source, keep, proj_ref, inv_ref, gain_ref, tab, dgain_ref):
+    cosine, sine = rope_factors(tab[...])
+    span, cols = keep.shape[1:]
+    dots = []
+    for i in range(2):
+        inverse = inv_ref[:, i : i + 1]
+        row_dot = jnp.zeros((span, 1), F32)
+        for h in range(cols // HEAD_DIM):
+            lanes = slice(h * HEAD_DIM, (h + 1) * HEAD_DIM)
+            v = source(i, h)
+            v = v * cosine - pltpu.roll(v, HALF, 1) * sine
+            values = proj_ref[i, :, lanes]
+            dgain_ref[i : i + 1, lanes] = jnp.sum(v * values * inverse, axis=0, keepdims=True)
+            v = v * gain_ref[i : i + 1, lanes]
+            keep[i, :, lanes] = v
+            row_dot = row_dot + jnp.sum(values * v, axis=-1, keepdims=True)
+        dots.append(row_dot)
+    return to_rows(*dots)
+
+
+def attend_spread_back_kernel(
+    n,
+    all_hbm,
+    do_ref,
+    att_hbm,
+    lse_ref,
+    bound_ref,
+    proj_hbm,
+    inv_ref,
+    gain_ref,
+    tab_ref,
+    resid_hbm,
+    resid_s_hbm,
+    dgu_hbm,
+    dgu_s_hbm,
+    own_in,
+    x_in,
+    y_in,
+    dproj_ref,
+    dgain_ref,
+    own_out,
+    x_out,
+    y_out,
+    every,
+    att,
+    proj,
+    d_out,
+    dq,
+    acc,
+    delta,
+    back,
+    got,
+    scaled,
+    tab,
+    msg,
+    late_buffers,
+    late_sems,
+    send,
+    recv,
+    b_send,
+    b_recv,
+    local_sem,
+    m_send,
+    m_recv,
+):
+    s, c, u = where_am_i()
+    span, cols = every.shape[2:]
+    width = resid_hbm.shape[1]
+    heads = cols // HEAD_DIM
+    load = [
+        pltpu.make_async_copy(all_hbm, every, local_sem.at[0]),
+        pltpu.make_async_copy(att_hbm, att, local_sem.at[1]),
+        pltpu.make_async_copy(tab_ref.at[rows_of(c, span)], tab, local_sem.at[2]),
+        pltpu.make_async_copy(proj_hbm, proj, local_sem.at[3]),
+    ]
+    last = 2 * (dgu_hbm.shape[2] // late_buffers[2].shape[1])
+    late = LatePiece(
+        last - 2,
+        (resid_hbm, resid_s_hbm, dgu_hbm, dgu_s_hbm),
+        (own_out, x_out, y_out),
+        late_buffers,
+        late_sems,
+    )
+    late.load()
+    for copy in load:
+        copy.start()
+    peers = [(s, c ^ k, u) for k in (1, 2, 3)]
+    greet([(None, peer) for peer in peers] + all_uly_peers(n))
+    copies = []
+    for k, peer in enumerate(peers):
+        copy = remote(do_ref.at[peer[1]], d_out.at[c], send.at[k], recv.at[k], peer)
+        copy.start()
+        copies.append(copy)
+    pieces = Pieces([late.work()])
+    d_out[pl.ds(c, 1)] = do_ref[pl.ds(c, 1)]
+    dq[...] = jnp.zeros_like(dq)
+    bound = bound_ref[:1, :1]
+    scale = HEAD_DIM ** (-0.5)
+    load[0].wait()
+    load[1].wait()
+    for k, peer in enumerate(peers):
+        there = d_out.at[peer[1]]
+        remote(there, there, send.at[k], recv.at[k], peer).wait_recv()
+    pieces.step()
+    for i in range(4):
+        for h in range(heads):
+            lanes = slice(h * HEAD_DIM, (h + 1) * HEAD_DIM)
+            both = jnp.transpose(d_out[i, :, lanes].astype(F32)) * att[i, lanes, :]
+            delta[i, h, :1, :] = jnp.sum(both, axis=0, keepdims=True)
+
+    def home(j):
+        return remote(back.at[j], got.at[c], b_send.at[j], b_recv.at[c], (s, j, u))
+
+    def step(j, carry):
+        acc[...] = jnp.zeros_like(acc)
+        for h in range(heads):
+            lanes = slice(h * HEAD_DIM, (h + 1) * HEAD_DIM)
+
+            def update(i, diagonal):
+                starts = segment_starts(i * span, span, bound)
+                keys, values = every[j, 1, :, lanes], every[j, 2, :, lanes]
+                query, grad = every[i, 0, :, lanes], d_out[i, :, lanes]
+                scores = dot(keys, query, NT) * SCALE2
+                scores = score_mask(scores, j * span, i * span, starts, diagonal)
+                probs = jnp.exp2(scores - lse_ref[i, h, :1, :])
+                acc[1, :, lanes] += dot(probs.astype(BF16), grad, NN)
+                d_probs = dot(values, grad, NT)
+                d_scores = (probs * (d_probs - delta[i, h, :1, :])).astype(BF16)
+                acc[0, :, lanes] += dot(d_scores, query, NN) * scale
+                dq[i, :, lanes] += dot(d_scores, keys, TN) * scale
+
+            def after(i, carry):
+                update(i, False)
+                return carry
+
+            update(j, True)
+            lax.fori_loop(j + 1, 4, after, 0)
+        back[j, 0] = dq[j].astype(BF16)
+        back[j, 1] = acc[0].astype(BF16)
+        back[j, 2] = acc[1].astype(BF16)
+
+        @pl.when(j != c)
+        def _():
+            home(j).start()
+
+        return carry
+
+    lax.fori_loop(0, 4, step, 0)
+    pieces.finish()
+    got[pl.ds(c, 1)] = back[pl.ds(c, 1)]
+    load[2].wait()
+    load[3].wait()
+    for k in (1, 2, 3):
+        j = c ^ k
+        remote(got.at[j], got.at[j], b_send.at[c], b_recv.at[j], (s, j, u)).wait_recv()
+    for j in range(4):
+        dproj_ref[2, :, j * cols : (j + 1) * cols] = got[j, 2]
+
+    def source(i, h):
+        group, inside = divmod(h, heads)
+        lanes = slice(inside * HEAD_DIM, (inside + 1) * HEAD_DIM)
+        return got[group, i, :, lanes].astype(F32)
+
+    rows = norms_back(n, source, scaled, proj, inv_ref, gain_ref, tab, dgain_ref)
+    total = exchange_rows(n, rows, msg, m_send, m_recv)
+    means = to_columns(total) / width
+    for i in range(2):
+        inverse = inv_ref[:, i : i + 1]
+        factor = inverse**3 * means[:, i : i + 1]
+        dproj_ref[i] = (inverse * scaled[i] - proj[i] * factor).astype(BF16)
+    late.plane.finish(1)
+    for j in range(4):
+
+        @pl.when(j != c)
+        def _():
+            home(j).wait_send()
+
+    for copy in copies:
+        copy.wait_send()
+
+
+def attend_spread_back(
+    n, every, d_out, att, lse, bound, proj, inv, gain, table, late, grads
+):
+    span, cols = every.shape[2:]
+    heads = cols // HEAD_DIM
+    width, ff = late[0].shape[1], late[2].shape[2]
+    return pl.pallas_call(
+        functools.partial(attend_spread_back_kernel, n),
+        out_shape=(shape((3, span, 4 * cols), BF16), shape((2, 4 * cols), F32))
+        + tuple(shape(g.shape, BF16) for g in grads),
+        in_specs=[HB, VM, HB, VM, VM, HB, VM, VM] + [HB] * 8,
+        out_specs=(VM, VM, HB, HB, HB),
+        input_output_aliases={13: 2, 14: 3, 15: 4},
+        scratch_shapes=[
+            pltpu.VMEM(every.shape, BF16),
+            pltpu.VMEM(att.shape, F32),
+            pltpu.VMEM(proj.shape, F32),
+            pltpu.VMEM((4, span, cols), BF16),
+            pltpu.VMEM((4, span, cols), F32),
+            pltpu.VMEM((2, span, cols), F32),
+            pltpu.VMEM((4, heads, 8, span), F32),
+            pltpu.VMEM((4, 3, span, cols), BF16),
+            pltpu.VMEM((4, 3, span, cols), BF16),
+            pltpu.VMEM((2, span, 4 * cols), F32),
+            pltpu.VMEM((span, 128), F32),
+            pltpu.VMEM((n, 8, span), F32),
+        ]
+        + LatePiece.scratch(span, width, ff)
+        + [
+            pltpu.SemaphoreType.DMA((3,)),
+            pltpu.SemaphoreType.DMA((3,)),
+            pltpu.SemaphoreType.DMA((4,)),
+            pltpu.SemaphoreType.DMA((4,)),
+            pltpu.SemaphoreType.DMA((4,)),
+            pltpu.SemaphoreType.DMA((n - 1,)),
+            pltpu.SemaphoreType.DMA((n - 1,)),
+        ],
+        compiler_params=pltpu.CompilerParams(
+            collective_id=9, has_side_effects=True, vmem_limit_bytes=VMEM_LIMIT
+        ),
+        name="attend_spread_back",
+    )(every, d_out, att, lse, bound, proj, inv, gain, table, *late, *grads)
 
 
 def attend_back_kernel(
@@ -1171,24 +1670,30 @@
     x_ref,
     gain_ref,
     wga_ref,
+    wgb_ref,
     gu_ref,
     down_ref,
-    branch_ref,
-    resid_ref,
+    branch_out,
+    resid_out,
     group_out,
-    gate_ref,
-    up_ref,
-    hidden_ref,
-    wgb_out,
+    gate_out,
+    up_out,
+    hidden_out,
     wgc_out,
     wd_out,
     wo,
     wg,
     group,
+    branch,
+    resid,
+    gate,
+    up,
+    hidden,
     part,
     got_rows,
     sem_o,
     local_sem,
+    keep_sem,
     w_send,
     w_recv,
     *sems,
@@ -1196,93 +1701,101 @@
     s, c, u = where_am_i()
     rows, width = x_ref.shape
     load_o = load_blocks(wo_ref, wo, sem_o, 1)
-    half = wga_ref.shape[1]
+    kb = wgc_out.shape[1]
     load_g = [
-        pltpu.make_async_copy(wga_ref, wg.at[0, :, pl.ds(0, half)], local_sem.at[0]),
-        pltpu.make_async_copy(wgb_out, wg.at[0, :, pl.ds(half, half)], local_sem.at[1]),
+        pltpu.make_async_copy(wga_ref, wg.at[0, :, pl.ds(0, kb // 2)], local_sem.at[0]),
+        pltpu.make_async_copy(wgb_ref, wg.at[0, :, pl.ds(kb // 2, kb // 2)], local_sem.at[1]),
         pltpu.make_async_copy(wgc_out, wg.at[1], local_sem.at[2]),
     ]
-    load_g[0].start()
     greet(line_peers(n) + plane_peers() + [(None, (1 - s, c, u))])
 
     def plane(k, src, out, half_rows):
         return PlaneGather(
-            src, lambda b: out.at[b], half_rows, w_send.at[k], w_recv.at[k], local_sem.at[4 + k]
+            src, lambda b: out.at[b], half_rows, w_send.at[k], w_recv.at[k], local_sem.at[3 + k]
         )
 
-    first = plane(0, gu_ref.at[0, pl.ds(half, half)], wgb_out, half // 2)
-    second = plane(1, gu_ref.at[1], wgc_out, half)
-    third = plane(2, down_ref, wd_out, down_ref.shape[0] // 2)
+    first = plane(0, gu_ref.at[1], wgc_out, kb // 2)
+    second = plane(1, down_ref, wd_out, down_ref.shape[0] // 2)
     first.start()
+    load_g[0].start()
+    load_g[1].start()
     wait_all(load_o)
-    chunk_cols = width // part.shape[0]
-    span = n * rows
-    count, size = tiles(span, 512)
+    halves = Halves(n, rows)
+    half = rows // 2
+    per_half = part.shape[0] // 2
+    chunk_cols = part.shape[2]
 
     def compute(chunk):
-        def tile(i, carry):
-            where = pl.ds(pl.multiple_of(i * size, size), size)
-            part[chunk, where, :] = dot(
-                attn_ref[where, :], wo[:, chunk * chunk_cols : (chunk + 1) * chunk_cols], NN
+        h, q = divmod(chunk, per_half)
+        cols = slice(q * chunk_cols, (q + 1) * chunk_cols)
+
+        def tile(index, start, size):
+            part[chunk, start : start + size, :] = dot(
+                halves.load(attn_ref, index), wo[:, cols], NN
             ).astype(BF16)
-            return carry
-
-        lax.fori_loop(0, count, tile, 0)
-
-    def reduce_hook(slot):
-        if slot == 0:
+
+        halves.each(h, tile)
+
+    reduce = LineReduce(n, half, part, got_rows, sems[:4])
+    gathers = [LineGather(n, rows, group, sems[4:], (h, half)) for h in range(2)]
+    kept = []
+
+    def keep(src, dst):
+        copy = pltpu.make_async_copy(src, dst, keep_sem.at[len(kept)])
+        copy.start()
+        kept.append(copy)
+
+    def finish(h):
+        where = slice(h * half, (h + 1) * half)
+        reduce.last(branch.at[h], range(h * per_half, (h + 1) * per_half))
+        values = branch[h]
+        total = x_ref[where, :].astype(F32) + values * inverse_rms(values) * gain_ref[0:1, :]
+        resid[h] = total
+        group[pl.ds(u, 1), where, :] = total.astype(BF16)[None]
+
+    ff = gate.shape[2]
+    ntile, tsize = tiles(ff, 512)
+
+    def body(h, t):
+        lanes = slice(t * tsize, (t + 1) * tsize)
+
+        def tile(index, start, size):
+            inputs = halves.load(group, index)
+            gates = dot(inputs, wg[0, :, :, lanes].reshape(width, tsize), NN)
+            ups = dot(inputs, wg[1, :, :, lanes].reshape(width, tsize), NN)
+            halves.store(gate, index, lanes, gates.astype(BF16))
+            halves.store(up, index, lanes, ups.astype(BF16))
+            halves.store(
+                hidden, index, lanes, (gates * jax.nn.sigmoid(gates) * ups).astype(BF16)
+            )
+
+        halves.each(h, tile)
+        if h == 1:
+            for src, dst in ((hidden, hidden_out), (gate, gate_out), (up, up_out)):
+                keep(src.at[:, :, lanes], dst.at[:, :, lanes])
+
+    def hook(label):
+        if label == "b1":
             first.middle()
             second.start()
-        if slot == 1:
+        if label == "first":
+            keep(branch, branch_out)
+            keep(resid, resid_out)
             first.corner()
-        if slot == 2:
             first.arrive()
-            load_g[1].start()
-
-    LineReduce(n, rows, part, got_rows, sems[:4]).run(compute, branch_ref, reduce_hook)
-    branch = branch_ref[...]
-    resid = x_ref[...].astype(F32) + branch * inverse_rms(branch) * gain_ref[0:1, :]
-    resid_ref[...] = resid
-    group[rows_of(u, rows), :] = resid.astype(BF16)
-    gather = LineGather(n, rows, group, sems[4:])
-    gather.send(0)
-    second.middle()
-    third.start()
-
-    def gather_hook(slot):
-        if slot == 1:
-            second.corner()
-
-    gather.run(gather_hook)
+            load_g[2].start()
+            wait_all(load_g)
+        if label == f"g{n - 2}":
+            keep(group, group_out)
+        if label == "t0":
+            second.middle()
+
+    reduce_norm_gather(n, reduce, gathers, compute, finish, Consume(ntile, body), hook)
+    second.corner()
     second.arrive()
-    load_g[2].start()
-    keep = pltpu.make_async_copy(group, group_out, local_sem.at[3])
-    keep.start()
-    third.middle()
-    wait_all(load_g)
-    ff = gate_ref.shape[1]
-    ntile, tsize = tiles(ff, 512)
-
-    def body(i, carry):
-        lanes = pl.ds(pl.multiple_of(i * tsize, tsize), tsize)
-
-        def tile(j, carry):
-            where = pl.ds(pl.multiple_of(j * size, size), size)
-            gate = dot(group[where, :], wg[0, :, :, lanes].reshape(width, tsize), NN)
-            up = dot(group[where, :], wg[1, :, :, lanes].reshape(width, tsize), NN)
-            gate_ref[where, lanes] = gate.astype(BF16)
-            up_ref[where, lanes] = up.astype(BF16)
-            hidden_ref[where, lanes] = (gate * jax.nn.sigmoid(gate) * up).astype(BF16)
-            return carry
-
-        return lax.fori_loop(0, count, tile, carry)
-
-    lax.fori_loop(0, ntile, body, 0)
-    third.corner()
-    third.arrive()
-    for work in (first, second, third):
+    for work in (first, second):
         work.finish()
-    keep.wait()
+    wait_all(kept)
 
 
 def reduce_scratch(n, rows, width):
@@ -1293,44 +1806,59 @@
     ]
 
 
-def mlp_in(n, attn, wo, x, gain, wga, gu, down):
+def half_scratch(n, rows, width):
+    half, cols = rows // 2, width // 2
+    return [
+        pltpu.VMEM((4, n * half, cols), BF16),
+        pltpu.VMEM((4, (n + 1) * half, cols), BF16),
+    ]
+
+
+def mlp_in(n, attn, wo, x, gain, wga, wgb, gu, down):
     rows, width = x.shape
     span, cols = attn.shape
     kb, ff = gu.shape[1:]
-    return pl.pallas_call(
+    ntile = tiles(ff, 512)[0]
+    outs = pl.pallas_call(
         functools.partial(mlp_in_kernel, n),
         out_shape=(
-            shape((rows, width), F32),
-            shape((rows, width), F32),
-            shape((span, width), BF16),
-            shape((span, ff), BF16),
-            shape((span, ff), BF16),
-            shape((span, ff), BF16),
-            shape((8, kb // 2, ff), BF16),
+            shape((2, rows // 2, width), F32),
+            shape((2, rows // 2, width), F32),
+            shape((n, rows, width), BF16),
+            shape((n, rows, ff), BF16),
+            shape((n, rows, ff), BF16),
+            shape((n, rows, ff), BF16),
             shape((8, kb, ff), BF16),
             shape((8,) + down.shape, BF16),
         ),
-        in_specs=[VM, HB, VM, VM, HB, HB, HB],
-        out_specs=(VM, VM, HB, VM, VM, VM, HB, HB, HB),
+        in_specs=[VM, HB, VM, VM, HB, HB, HB, HB],
+        out_specs=(HB,) * 8,
         scratch_shapes=[
             pltpu.VMEM((cols, width), BF16),
             pltpu.VMEM((2, 8, kb, ff), BF16),
-            pltpu.VMEM((span, width), BF16),
+            pltpu.VMEM((n, rows, width), BF16),
+            pltpu.VMEM((2, rows // 2, width), F32),
+            pltpu.VMEM((2, rows // 2, width), F32),
+            pltpu.VMEM((n, rows, ff), BF16),
+            pltpu.VMEM((n, rows, ff), BF16),
+            pltpu.VMEM((n, rows, ff), BF16),
         ]
-        + reduce_scratch(n, rows, width)
+        + half_scratch(n, rows, width)
         + [
             pltpu.SemaphoreType.DMA((8,)),
-            pltpu.SemaphoreType.DMA((7,)),
-            pltpu.SemaphoreType.DMA((3, 9)),
-            pltpu.SemaphoreType.DMA((3, 9)),
+            pltpu.SemaphoreType.DMA((5,)),
+            pltpu.SemaphoreType.DMA((3 + 3 * ntile,)),
+            pltpu.SemaphoreType.DMA((2, 9)),
+            pltpu.SemaphoreType.DMA((2, 9)),
         ]
-        + line_sems(n, CHUNKS)
-        + line_sems(n),
+        + line_sems(n, 4)
+        + line_sems(n, 2),
         compiler_params=pltpu.CompilerParams(
             collective_id=4, has_side_effects=True, vmem_limit_bytes=VMEM_LIMIT
         ),
         name="mlp_in",
-    )(attn, wo, x, gain, wga, gu, down)
+    )(attn.reshape(n, rows, cols), wo, x, gain, wga, wgb, gu, down)
+    return outs
 
 
 def mlp_out_kernel(
@@ -1340,12 +1868,12 @@
     resid_ref,
     gain_ref,
     cot_ref,
-    gate_ref,
-    up_ref,
+    gate_hbm,
+    up_hbm,
     gresid_ref,
     out_ref,
     group_out,
-    dgu_ref,
+    dgu_out,
     dgain_ref,
     hidden_s,
     resid_s,
@@ -1354,115 +1882,151 @@
     wd,
     mlp,
     group,
+    gate_ref,
+    up_ref,
+    dgu,
     part,
     got_rows,
     sem_d,
+    local_sem,
     keep_sem,
     s_send,
     s_recv,
     *sems,
 ):
     s, c, u = where_am_i()
-    rows, width = resid_ref.shape
+    rows, width = cot_ref.shape
     load_d = load_blocks(wd_ref, wd, sem_d, 1)
+    load_g = [
+        pltpu.make_async_copy(gate_hbm, gate_ref, local_sem.at[0]),
+        pltpu.make_async_copy(up_hbm, up_ref, local_sem.at[1]),
+    ]
     greet(line_peers(n) + [(None, (1 - s, c, u))])
     sibling = Sibling(s_send, s_recv)
-    wait_all(load_d)
-    chunk_cols = width // part.shape[0]
-    span = n * rows
-    count, size = tiles(span, 512)
+    halves = Halves(n, rows)
+    half = rows // 2
+    per_half = part.shape[0] // 2
+    chunk_cols = part.shape[2]
 
     def compute(chunk):
-        def tile(i, carry):
-            where = pl.ds(pl.multiple_of(i * size, size), size)
-            part[chunk, where, :] = dot(
-                hidden_ref[where, :], wd[:, chunk * chunk_cols : (chunk + 1) * chunk_cols], NN
+        h, q = divmod(chunk, per_half)
+        cols = slice(q * chunk_cols, (q + 1) * chunk_cols)
+        if h == 0:
+            wait_all(load_d[q * (8 // per_half) : (q + 1) * (8 // per_half)])
+
+        def tile(index, start, size):
+            part[chunk, start : start + size, :] = dot(
+                halves.load(hidden_ref, index), wd[:, cols], NN
             ).astype(BF16)
-            return carry
-
-        lax.fori_loop(0, count, tile, 0)
-
-    def hook(slot):
-        if slot == 0:
-            sibling.start(hidden_ref, hidden_s)
-            sibling.start(half_columns(gresid_ref, 1 - s), resid_s)
-
-    LineReduce(n, rows, part, got_rows, sems[:4]).run(compute, mlp, hook)
-    values = mlp[...]
-    inverse = inverse_rms(values)
-    grad = cot_ref[...].astype(F32)
-    d_mlp = norm_back(values, inverse, grad * gain_ref[1:2, :], width)
-    group[rows_of(u, rows), :] = d_mlp.astype(BF16)
-    gather = LineGather(n, rows, group, sems[4:])
-    gather.send(0)
-    scaled = values * inverse
-    out_ref[...] = (resid_ref[...] + scaled * gain_ref[1:2, :]).astype(BF16)
-    dgain_ref[...] = jnp.sum(grad * scaled, axis=0, keepdims=True)
-    for slot in range(n - 1):
-        gather.wait(slot)
-    gather.finish()
-    keep = pltpu.make_async_copy(group, group_out, keep_sem)
-    keep.start()
-    sibling.start(half_columns(group, 1 - s), dmlp_s)
-    ntile, tsize = tiles(gate_ref.shape[1], 512)
-
-    def body(i, carry):
-        lanes = pl.ds(pl.multiple_of(i * tsize, tsize), tsize)
-
-        def tile(j, carry):
-            where = pl.ds(pl.multiple_of(j * size, size), size)
-            d_hidden = dot(group[where, :], wd[lanes, :], NT)
-            gate = gate_ref[where, lanes].astype(F32)
-            up = up_ref[where, lanes].astype(F32)
+
+        halves.each(h, tile)
+
+    reduce = LineReduce(n, half, part, got_rows, sems[:4])
+    gathers = [LineGather(n, rows, group, sems[4:], (h, half)) for h in range(2)]
+    dgain_ref[...] = jnp.zeros_like(dgain_ref)
+
+    def finish(h):
+        where = slice(h * half, (h + 1) * half)
+        reduce.last(mlp.at[h], range(h * per_half, (h + 1) * per_half))
+        values = mlp[h]
+        grad = cot_ref[where, :].astype(F32)
+        d_mlp = norm_back(values, inverse_rms(values), grad * gain_ref[1:2, :], width)
+        group[pl.ds(u, 1), where, :] = d_mlp.astype(BF16)[None]
+
+    def rest(h):
+        where = slice(h * half, (h + 1) * half)
+        values = mlp[h]
+        scaled = values * inverse_rms(values)
+        out_ref[where, :] = (resid_ref[h] + scaled * gain_ref[1:2, :]).astype(BF16)
+        dgain_ref[...] += jnp.sum(cot_ref[where, :].astype(F32) * scaled, axis=0, keepdims=True)
+
+    ff = gate_ref.shape[2]
+    ntile, tsize = tiles(ff, 512)
+    kept = []
+
+    def keep(src, dst):
+        copy = pltpu.make_async_copy(src, dst, keep_sem.at[len(kept)])
+        copy.start()
+        kept.append(copy)
+
+    def body(h, t):
+        lanes = slice(t * tsize, (t + 1) * tsize)
+
+        def tile(index, start, size):
+            d_hidden = dot(halves.load(group, index), wd[lanes, :], NT)
+            gate = halves.load(gate_ref, index, lanes).astype(F32)
+            up = halves.load(up_ref, index, lanes).astype(F32)
             sig = jax.nn.sigmoid(gate)
             slope = sig * (1.0 + gate * (1.0 - sig))
-            dgu_ref[0, where, lanes] = (d_hidden * up * slope).astype(BF16)
-            dgu_ref[1, where, lanes] = (d_hidden * (gate * sig)).astype(BF16)
-            return carry
-
-        return lax.fori_loop(0, count, tile, carry)
-
-    for i in range(ntile):
-        body(i, 0)
-        lanes = pl.ds(i * tsize, tsize)
-        sibling.start(dgu_ref.at[:, :, lanes], dgu_s.at[:, :, lanes])
-    for i in range(3 + ntile):
+            halves.store(dgu.at[0], index, lanes, (d_hidden * up * slope).astype(BF16))
+            halves.store(dgu.at[1], index, lanes, (d_hidden * (gate * sig)).astype(BF16))
+
+        halves.each(h, tile)
+        where = pl.ds(h * half, half)
+        view = dgu.at[:, :, where, lanes]
+        sibling.start(view, dgu_s.at[:, :, where, lanes])
+        keep(view, dgu_out.at[:, :, where, lanes])
+
+    def hook(label):
+        if label == "sent":
+            sibling.start(hidden_ref, hidden_s)
+            lanes = pl.ds(pl.multiple_of((1 - s) * (width // 2), width // 2), width // 2)
+            sibling.start(gresid_ref.at[:, :, lanes], resid_s)
+            for copy in load_g:
+                copy.start()
+        if label == "half":
+            rest(0)
+        if label == "first":
+            rest(1)
+            wait_all(load_g)
+        if label == f"g{n - 2}":
+            lanes = pl.ds(pl.multiple_of((1 - s) * (width // 2), width // 2), width // 2)
+            sibling.start(group.at[:, :, lanes], dmlp_s)
+            keep(group, group_out)
+
+    reduce_norm_gather(n, reduce, gathers, compute, finish, Consume(ntile, body), hook)
+    for i in range(3 + 2 * ntile):
         sibling.wait(i)
     sibling.finish()
-    keep.wait()
+    wait_all(kept)
 
 
 def mlp_out(n, hidden, wd, resid, gain, cot, gate, up, gresid):
-    rows, width = resid.shape
-    span, ff = hidden.shape
+    rows, width = cot.shape
+    ff = hidden.shape[2]
+    ntile = tiles(ff, 512)[0]
     return pl.pallas_call(
         functools.partial(mlp_out_kernel, n),
         out_shape=(
             shape((rows, width), BF16),
-            shape((span, width), BF16),
-            shape((2, span, ff), BF16),
+            shape((n, rows, width), BF16),
+            shape((2, n, rows, ff), BF16),
             shape((1, width), F32),
-            shape((span, ff), BF16),
-            shape((span, width // 2), BF16),
-            shape((span, width // 2), BF16),
-            shape((2, span, ff), BF16),
+            shape((n, rows, ff), BF16),
+            shape((n, rows, width // 2), BF16),
+            shape((n, rows, width // 2), BF16),
+            shape((2, n, rows, ff), BF16),
         ),
-        in_specs=[VM, HB, VM, VM, VM, VM, VM, HB],
-        out_specs=(VM, HB, VM, VM, HB, HB, HB, HB),
+        in_specs=[VM, HB, VM, VM, VM, HB, HB, HB],
+        out_specs=(VM, HB, HB, VM, HB, HB, HB, HB),
         scratch_shapes=[
             pltpu.VMEM((ff, width), BF16),
-            pltpu.VMEM((rows, width), F32),
-            pltpu.VMEM((span, width), BF16),
+            pltpu.VMEM((2, rows // 2, width), F32),
+            pltpu.VMEM((n, rows, width), BF16),
+            pltpu.VMEM((n, rows, ff), BF16),
+            pltpu.VMEM((n, rows, ff), BF16),
+            pltpu.VMEM((2, n, rows, ff), BF16),
         ]
-        + reduce_scratch(n, rows, width)
+        + half_scratch(n, rows, width)
         + [
             pltpu.SemaphoreType.DMA((8,)),
-            pltpu.SemaphoreType.DMA,
-            pltpu.SemaphoreType.DMA((3 + tiles(ff, 512)[0],)),
-            pltpu.SemaphoreType.DMA((3 + tiles(ff, 512)[0],)),
+            pltpu.SemaphoreType.DMA((2,)),
+            pltpu.SemaphoreType.DMA((1 + 2 * ntile,)),
+            pltpu.SemaphoreType.DMA((3 + 2 * ntile,)),
+            pltpu.SemaphoreType.DMA((3 + 2 * ntile,)),
         ]
-        + line_sems(n, CHUNKS)
-        + line_sems(n),
+        + line_sems(n, 4)
+        + line_sems(n, 2),
         compiler_params=pltpu.CompilerParams(
             collective_id=5, has_side_effects=True, vmem_limit_bytes=VMEM_LIMIT
         ),
@@ -1674,7 +2238,13 @@
             fetch.start()
             fetch.wait()
             rows_in = group[...]
-        dattn_ref[where, :] = dot(rows_in, wo[...], NT).astype(BF16)
+        d_attn = dot(rows_in, wo[...], NT).astype(BF16)
+        if len(dattn_ref.shape) == 3:
+            cols = dattn_ref.shape[2]
+            for q in range(4):
+                dattn_ref[q, where, :] = d_attn[:, q * cols : (q + 1) * cols]
+        else:
+            dattn_ref[where, :] = d_attn
         return carry
 
     lax.fori_loop(0, count, tile, 0)
@@ -1728,7 +2298,7 @@
         out_shape=(
             shape((rows, width), F32),
             shape((span, width), BF16),
-            shape((span, cols), BF16),
+            shape((4, span, cols // 4) if spread_heads(cols) else (span, cols), BF16),
             shape((1, width), F32),
         )
         + (shape((2, kb, ff), BF16),) * 3
@@ -2108,16 +2678,27 @@
     width = x.shape[1]
     cot = cotangent[0]
     table = jnp.asarray(table)
-    group_x, wq, wo, wga, proj, q, kv, inv, zero = project(
+    group_x, wq, wo, wga, proj, qkv, inv, zero = project(
         n, x, qkv_weight, table, qk_gain, segment_ids, out_weight, gate_up
     )
-    kvall, attn, attn32, lse, bound = attend(q, kv, zero)
-    branch, resid, group_resid, gate, up, hidden, wgb, wgc, wd = mlp_in(
-        n, attn, wo, x, post_gain, wga, gate_up, down_weight
+    if len(qkv) == 1:
+        every, wgb, attn, att, lse, bound = attend_spread(qkv[0], zero, gate_up)
+        seen, back = (every,), attend_spread_back
+    else:
+        every, wgb, attn, att, lse, bound = attend(*qkv, zero, gate_up)
+        seen, back = (qkv[0], every), attend_back
+    branch, resid, group_resid, gate, up, hidden, wgc, wd = mlp_in(
+        n, attn, wo, x, post_gain, wga, wgb, gate_up, down_weight
     )
     block_out, group_dmlp, dgu, gain_mlp, hidden_s, resid_s, dmlp_s, dgu_s = mlp_out(
         n, hidden, wd, resid, post_gain, cot, gate, up, group_resid
     )
+    span, ff = n * x.shape[0], hidden.shape[2]
+    branch = branch.reshape(x.shape)
+    dgu, dgu_s = dgu.reshape(2, span, ff), dgu_s.reshape(2, span, ff)
+    hidden, hidden_s = hidden.reshape(span, ff), hidden_s.reshape(span, ff)
+    group_resid, group_dmlp = group_resid.reshape(span, width), group_dmlp.reshape(span, width)
+    resid_s, dmlp_s = resid_s.reshape(span, width // 2), dmlp_s.reshape(span, width // 2)
     d_resid, group_dbranch, d_attn, gain_attn, *grads = mlp_back(
         n,
         dgu,
@@ -2138,8 +2719,8 @@
     )
     gate_grads, down_grads = grads[:3], grads[3:]
     late = (group_resid, resid_s, dgu, dgu_s)
-    d_proj, gain_cols, *gate_grads = attend_back(
-        n, q, kvall, d_attn, attn32, lse, bound, proj, inv, qk_gain, table, late, gate_grads
+    d_proj, gain_cols, *gate_grads = back(
+        n, *seen, d_attn, att, lse, bound, proj, inv, qk_gain, table, late, gate_grads
     )
     input_grad, gain_part, *grads = proj_back(
         n,

time: 546 us -> 514 us (0.941)
  Pallas kernels: 523 us -> 493 us
    pallas_call x3, Pallas kernels: 197 us -> 180 us  [the longest x1 87.9 us: mlp_in(): pl.pallas_call(functools.partial(mlp_in_kernel, n), out_shape=(shape((2,...]
    pallas_call x1, Pallas kernels: 93.3 us -> 78.4 us  [mlp_out(): pl.pallas_call(functools.partial(mlp_out_kernel, n), out_shape=(shape((ro...]
where the time goes in v4:
time: 514 us; the launch traced here: 508 us
  Pallas kernels  493 us (96%)
  other arithmetic  10.2 us (2%)
    pallas_call x1, Pallas kernels, mlp_back(): pl.pallas_call(functools.partial(mlp_back_kernel, n), out_shape=(shape((r...  114 us
    pallas_call x1, Pallas kernels, mlp_in(): pl.pallas_call(functools.partial(mlp_in_kernel, n), out_shape=(shape((2,...  87.9 us
    pallas_call x1, Pallas kernels, mlp_out(): pl.pallas_call(functools.partial(mlp_out_kernel, n), out_shape=(shape((ro...  78.4 us
    pallas_call x1, Pallas kernels, project(): pl.pallas_call(functools.partial(proj_kernel, n), out_shape=(shape((span,...  65.8 us
    pallas_call x1, Pallas kernels, proj_back(): pl.pallas_call(functools.partial(proj_back_kernel, n), out_shape=(shape((...  54.9 us
    pallas_call x1, Pallas kernels, attend_spread(): pl.pallas_call(attend_spread_kernel, out_shape=(shape(qkv.shape, BF16), s...  51.3 us
    pallas_call x1, Pallas kernels, attend_spread_back(): pl.pallas_call(functools.partial(attend_spread_back_kernel, n), out_shape...  41.1 us

profile of v4, /device:TPU:0, one launch (start us, length us, event | category | flops | bytes accessed | tf_op | source)
XLA Modules:
  0.0 508.1 jit_solution(16841496869621141906)
XLA Ops:
  0.6 65.8 %project.1 = (bf16[512,2048]{1,0:T(8,128)(2,1)}, bf16[3,2048,512]{2,1,0:T(8,128)(2,1)}, bf16[8,512,256]{2,1,0:T(8,128)(2,1)}, bf16[8,128,2048]{2,1,0:T(8,128)(2,...) custom-call(bf16[128,2048]{1,0:T(8,128)(2,1)} %bitcast.31, ...), custom_call_target="tpu_custom_call" | custom-call | tf_op jit(solution)/shard_map/project/pallas_call | solution.py:825
  66.4 51.3 %attend_spread.1 = (bf16[4,3,512,128]{3,2,1,0:T(8,128)(2,1)}, bf16[8,128,2048]{2,1,0:T(8,128)(2,1)}, bf16[512,512]{1,0:T(8,128)(2,1)}, f32[4,128,512]{2,1,0:T(8,...) custom-call(bf16[4,3,512,128]{3,2,1,0:T(8,128)(2,1)} %get-tuple-element.63.qkv_ref, ...), custom_call_target="tpu_custom_call" | custom-call | tf_op jit(solution)/shard_map/attend_spread/pallas_call | solution.py:1178
  117.7 87.9 %mlp_in.1 = (f32[2,64,2048]{2,1,0:T(8,128)}, f32[2,64,2048]{2,1,0:T(8,128)}, bf16[4,128,2048]{2,1,0:T(8,128)(2,1)}, bf16[4,128,2048]{2,1,0:T(8,128)(2,1)}, bf16[...) custom-call(bf16[4,128,512]{2,1,0:T(8,128)(2,1)} %bitcast.33, ...), custom_call_target="tpu_custom_call" | custom-call | tf_op jit(solution)/shard_map/mlp_in/pallas_call | solution.py:1822
  205.6 78.4 %mlp_out.1 = (bf16[128,2048]{1,0:T(8,128)(2,1)}, bf16[4,128,2048]{2,1,0:T(8,128)(2,1)}, bf16[2,4,128,2048]{3,2,1,0:T(8,128)(2,1)}, f32[1,2048]{1,0:T(1,128)}, bf...) custom-call(bf16[4,128,2048]{2,1,0:T(8,128)(2,1)} %get-tuple-element, ...), custom_call_target="tpu_custom_call" | custom-call | tf_op jit(solution)/shard_map/mlp_out/pallas_call | solution.py:1998
  284.0 113.8 %mlp_back.1 = (f32[128,2048]{1,0:T(8,128)}, bf16[512,2048]{1,0:T(8,128)(2,1)}, bf16[4,512,128]{2,1,0:T(8,128)(2,1)}, f32[1,2048]{1,0:T(1,128)}, bf16[2,256,2048]...) custom-call(bf16[2,512,2048]{2,1,0:T(8,128)(2,1)} %bitcast.14, ...), custom_call_target="tpu_custom_call" | custom-call | tf_op jit(solution)/shard_map/mlp_back/pallas_call | solution.py:2296
  397.9 41.1 %attend_spread_back.1 = (bf16[3,512,512]{2,1,0:T(8,128)(2,1)}, f32[2,512]{1,0:T(2,128)}, bf16[2,256,2048]{2,1,0:T(8,128)(2,1)}, bf16[2,256,2048]{2,1,0:T(8,128)(2,1)}, bf16[2,256,2048]{2,1,0:T(8,128)(2,1)}) custom-call(bf16[4,3,512,128]{3,2,1,0:T(8,128)(2,1)} %get-tuple-element.76.all_hbm, ...), custom_call_target="tpu_custom_call", output_to_operand_aliasing={{2}: (13, {}), {3}: (14, {}), {4}: (15, {})} | custom-call | tf_op jit(solution)/shard_map/attend_spread_back/pallas_call | solution.py:1395
  439.0 54.9 %proj_back.1 = (bf16[128,2048]{1,0:T(8,128)(2,1)}, f32[4,256]{1,0:T(4,128)}, bf16[3,256,512]{2,1,0:T(8,128)(2,1)}, bf16[3,256,512]{2,1,0:T(8,128)(2,1)}, bf16[3,...) custom-call(bf16[3,512,512]{2,1,0:T(8,128)(2,1)} %get-tuple-element., ...), custom_call_target="tpu_custom_call", output_to_operand_aliasing={{8}: (13, {}), {9}: (14, {}), {10}: (15, {})} | custom-call | tf_op jit(solution)/shard_map/proj_back/pallas_call | solution.py:2592
  493.8 0.0 copy-start.4
  493.9 0.0 copy-start.5
  493.9 2.1 convert_add_fusion.3
  496.0 3.2 convert_add_fusion.2
  499.2 0.0 copy-done.4
  499.2 0.0 copy-done.5
  499.2 0.0 copy-done.3
  499.2 0.0 copy-start
  499.3 0.0 copy-start.1
  499.3 1.7 convert_add_fusion.1
  500.9 0.5 copy-done
  501.5 0.7 copy-done.1
  502.2 3.2 convert_add_fusion
  505.5 0.8 copy.32
  506.3 0.8 copy.33
  507.0 0.0 copy-done.8
  507.0 0.6 copy.34
  (8 shorter events, 0.0 us)
Async XLA Ops:
  493.8 5.4 %copy-start.4 = (bf16[2048,256]{1,0:T(8,128)(2,1)S(1)}, bf16[2048,256]{1,0:T(8,128)(2,1)}, u32[]{:S(2)}) copy-start(bf16[2048,256]{1,0:T(8,128)(2,1)} %get-tuple-element.116) | copy-start | bytes 3145732
  493.9 5.4 %copy-start.5 = (bf16[2048,256]{1,0:T(8,128)(2,1)S(1)}, bf16[2048,256]{1,0:T(8,128)(2,1)}, u32[]{:S(2)}) copy-start(bf16[2048,256]{1,0:T(8,128)(2,1)} %get-tuple-element.117) | copy-start | bytes 3145732
  496.0 3.2 copy-start.3
  496.0 4.9 copy-start.2
  499.2 2.2 copy-start
  499.3 3.0 copy-start.1
  502.2 3.2 copy-start.6
  502.2 4.0 copy-start.7
  505.5 1.6 copy-start.8

commit v5 on v4

--- a/solution.py
+++ b/solution.py
@@ -20,6 +20,7 @@
 F32 = jnp.float32
 VMEM_LIMIT = 62 * 1024 * 1024
 CHUNKS = 4
+AHEAD = 1
 LATER = 2
 
 VM = pl.BlockSpec(memory_space=pltpu.VMEM)
@@ -257,6 +258,7 @@
         reduce.step(0, chunk)
     for chunk in chunks[1]:
         compute(chunk)
+    hook("started")
     for slot in range(1, slots):
         for chunk in chunks[0]:
             reduce.step(slot, chunk)
@@ -420,7 +422,7 @@
             remotes, own = self.open.pop(piece)
             for copy in remotes:
                 copy.wait_send()
-            own.wait()
+            wait_all(own)
 
     def first(self, piece):
         c = self.c
@@ -436,29 +438,35 @@
         ]
         for copy in copies:
             copy.start()
-        own = pltpu.make_async_copy(
-            blocks.at[c], self.place(own_out, piece, None), self.local.at[piece]
-        )
-        own.start()
+        own = self.own_copies(piece, blocks)
+        for copy in own:
+            copy.start()
         self.open[piece] = (copies, own)
 
+    def own_copies(self, piece, blocks):
+        place = self.place(self.outs[0], piece, None)
+        return [pltpu.make_async_copy(blocks.at[self.c], place, self.local.at[piece])]
+
+    def add(self, slot, block, half, piece):
+        h = self.rows // 2
+        where = slice(half * h, (half + 1) * h)
+        self.ring[slot, block, where, :] = (
+            self.ring[slot, block, where, :].astype(F32) + self.got[piece, where, :].astype(F32)
+        ).astype(BF16)
+
     def second(self, piece):
-        c, h = self.c, self.rows // 2
+        c = self.c
         lo, hi = self.halves()
         slot = piece % self.slots
         blocks = self.ring.at[slot]
         own_out, out_x, out_y = self.outs
         bx, by, bd = c ^ 1, c ^ 2, c ^ 3
         self.copy(piece, 0, blocks.at[bd, lo], self.got.at[piece, lo], self.xn).wait_recv()
-        self.ring[slot, by, :h, :] = (
-            self.ring[slot, by, :h, :].astype(F32) + self.got[piece, :h, :].astype(F32)
-        ).astype(BF16)
+        self.add(slot, by, 0, piece)
         first = self.copy(piece, 4, blocks.at[by, lo], self.place(out_y, piece, 0), self.yn)
         first.start()
         self.copy(piece, 1, blocks.at[bd, hi], self.got.at[piece, hi], self.yn).wait_recv()
-        self.ring[slot, bx, h:, :] = (
-            self.ring[slot, bx, h:, :].astype(F32) + self.got[piece, h:, :].astype(F32)
-        ).astype(BF16)
+        self.add(slot, bx, 1, piece)
         second = self.copy(piece, 5, blocks.at[bx, hi], self.place(out_x, piece, 1), self.xn)
         second.start()
         self.open[piece][0].extend([first, second])
@@ -480,8 +488,8 @@
 
 
 class Pieces:
-    def __init__(self, work):
-        self.work, self.done, self.behind = work, 0, []
+    def __init__(self, work, ahead=2):
+        self.work, self.done, self.behind, self.ahead = work, 0, [], ahead
 
     def step(self, count=1):
         for _ in range(count):
@@ -491,7 +499,7 @@
                 plane.first(piece)
                 self.behind.append((plane, piece))
                 self.done += 1
-                if len(self.behind) > 2:
+                if len(self.behind) > self.ahead:
                     self.catch_up()
 
     def catch_up(self):
@@ -1040,131 +1048,6 @@
     )(q, kv, zero, gu)
 
 
-def attend_spread_kernel(
-    qkv_ref,
-    zero_ref,
-    gu_ref,
-    all_out,
-    wgb_out,
-    attn_ref,
-    att_ref,
-    lse_ref,
-    bound_ref,
-    every,
-    peaks,
-    sums,
-    acct,
-    back,
-    zmsg,
-    send,
-    recv,
-    z_send,
-    z_recv,
-    b_send,
-    b_recv,
-    w_send,
-    w_recv,
-    keep_sem,
-    w_local,
-):
-    s, c, u = where_am_i()
-    span, cols = every.shape[2:]
-    heads = cols // HEAD_DIM
-    peers = [(s, c ^ k, u) for k in (1, 2, 3)]
-    greet([(None, peer) for peer in peers] + [(None, (1 - s, c, u))])
-    weight = upper_gate(gu_ref, wgb_out, w_send, w_recv, w_local)
-    copies, arrivals = [], []
-    zmsg[pl.ds(c, 1)] = zero_ref[...][None]
-    for k, peer in enumerate(peers):
-        there = peer[1]
-        copy = remote(qkv_ref.at[there], every.at[c], send.at[k], recv.at[k], peer)
-        copy.start()
-        small = remote(zmsg.at[c], zmsg.at[c], z_send.at[k], z_recv.at[k], peer)
-        small.start()
-        copies += [copy, small]
-        arrivals.append(remote(every.at[there], every.at[there], send.at[k], recv.at[k], peer))
-        arrivals.append(remote(zmsg.at[there], zmsg.at[there], z_send.at[k], z_recv.at[k], peer))
-    every[pl.ds(c, 1)] = qkv_ref[pl.ds(c, 1)]
-    for arrival in arrivals:
-        arrival.wait_recv()
-    weight.start()
-    keep = pltpu.make_async_copy(every, all_out, keep_sem)
-    keep.start()
-    bounds = (zmsg[0] + zmsg[1] + zmsg[2] + zmsg[3]).astype(jnp.int32)
-    bound_ref[...] = bounds
-    bound = bounds[:1, :1]
-
-    def step(k, carry):
-        i = c ^ (3 - k)
-        first_q = i * span
-        starts = segment_starts(first_q, span, bound)
-        for h in range(heads):
-            lanes = slice(h * HEAD_DIM, (h + 1) * HEAD_DIM)
-            peaks[...] = jnp.full_like(peaks, FLOOR)
-            sums[...] = jnp.zeros_like(sums)
-            acct[...] = jnp.zeros_like(acct)
-
-            def update(j, diagonal):
-                scores = dot(every[j, 1, :, lanes], every[i, 0, :, lanes], NT) * SCALE2
-                scores = score_mask(scores, j * span, first_q, starts, diagonal)
-                old = peaks[:1, :]
-                new = jnp.maximum(old, jnp.max(scores, axis=0, keepdims=True))
-                factor = jnp.exp2(old - new)
-                weights = jnp.exp2(scores - new)
-                peaks[:1, :] = new
-                sums[:1, :] = sums[:1, :] * factor + jnp.sum(weights, axis=0, keepdims=True)
-                acct[...] = acct[...] * factor + dot(
-                    every[j, 2, :, lanes], weights.astype(BF16), TN
-                )
-
-            def before(j, carry):
-                update(j, False)
-                return carry
-
-            lax.fori_loop(0, i, before, 0)
-            update(i, True)
-            total = sums[:1, :]
-            attention = acct[...] / total
-            att_ref[pl.ds(i, 1), lanes, :] = attention[None]
-            back[pl.ds(k, 1), :, lanes] = jnp.transpose(attention).astype(BF16)[None]
-            lse_ref[pl.ds(i, 1), h, :1, :] = (peaks[:1, :] + jnp.log2(total))[None]
-
-        @pl.when(k < 3)
-        def _():
-            home(k, i).start()
-
-        return carry
-
-    def home(k, i):
-        return remote(
-            back.at[k],
-            attn_ref.at[:, pl.ds(pl.multiple_of(c * cols, cols), cols)],
-            b_send.at[k],
-            b_recv.at[k],
-            (s, i, u),
-        )
-
-    lax.fori_loop(0, 4, step, 0)
-    attn_ref[:, pl.ds(pl.multiple_of(c * cols, cols), cols)] = back[3]
-    for k in range(3):
-        i = c ^ (3 - k)
-        remote(
-            back.at[k],
-            attn_ref.at[:, pl.ds(pl.multiple_of(i * cols, cols), cols)],
-            b_send.at[k],
-            b_recv.at[k],
-            (s, i, u),
-        ).wait_recv()
-        home(k, i).wait_send()
-    for copy in copies:
-        copy.wait_send()
-    weight.middle()
-    weight.corner()
-    weight.arrive()
-    weight.finish()
-    keep.wait()
-
-
 def upper_gate(gu_ref, out, send, recv, local):
     half = gu_ref.shape[1] // 2
     return PlaneGather(
@@ -1172,42 +1055,9 @@
     )
 
 
-def attend_spread(qkv, zero, gu):
-    span, cols = qkv.shape[2:]
-    heads = cols // HEAD_DIM
-    return pl.pallas_call(
-        attend_spread_kernel,
-        out_shape=(
-            shape(qkv.shape, BF16),
-            shape((8, gu.shape[1] // 2, gu.shape[2]), BF16),
-            shape((span, 4 * cols), BF16),
-            shape((4, cols, span), F32),
-            shape((4, heads, 8, span), F32),
-            shape((8, 128), jnp.int32),
-        ),
-        in_specs=[VM, VM, HB],
-        out_specs=(HB, HB, VM, VM, VM, VM),
-        scratch_shapes=[
-            pltpu.VMEM(qkv.shape, BF16),
-            pltpu.VMEM((8, span), F32),
-            pltpu.VMEM((8, span), F32),
-            pltpu.VMEM((HEAD_DIM, span), F32),
-            pltpu.VMEM((4, span, cols), BF16),
-            pltpu.VMEM((4, 8, 128), F32),
-        ]
-        + [pltpu.SemaphoreType.DMA((3,))] * 6
-        + [pltpu.SemaphoreType.DMA((9,))] * 2
-        + [pltpu.SemaphoreType.DMA] * 2,
-        compiler_params=pltpu.CompilerParams(
-            collective_id=8, has_side_effects=True, vmem_limit_bytes=VMEM_LIMIT
-        ),
-        name="attend_spread",
-    )(qkv, zero, gu)
-
-
-def norms_back(n, source, keep, proj_ref, inv_ref, gain_ref, tab, dgain_ref):
+def norms_back(source, keep, proj_ref, inv_ref, gain_ref, tab, dgain_ref):
     cosine, sine = rope_factors(tab[...])
-    span, cols = keep.shape[1:]
+    span, cols = proj_ref.shape[1:]
     dots = []
     for i in range(2):
         inverse = inv_ref[:, i : i + 1]
@@ -1219,215 +1069,10 @@
             values = proj_ref[i, :, lanes]
             dgain_ref[i : i + 1, lanes] = jnp.sum(v * values * inverse, axis=0, keepdims=True)
             v = v * gain_ref[i : i + 1, lanes]
-            keep[i, :, lanes] = v
+            keep(i, h, v)
             row_dot = row_dot + jnp.sum(values * v, axis=-1, keepdims=True)
         dots.append(row_dot)
     return to_rows(*dots)
-
-
-def attend_spread_back_kernel(
-    n,
-    all_hbm,
-    do_ref,
-    att_hbm,
-    lse_ref,
-    bound_ref,
-    proj_hbm,
-    inv_ref,
-    gain_ref,
-    tab_ref,
-    resid_hbm,
-    resid_s_hbm,
-    dgu_hbm,
-    dgu_s_hbm,
-    own_in,
-    x_in,
-    y_in,
-    dproj_ref,
-    dgain_ref,
-    own_out,
-    x_out,
-    y_out,
-    every,
-    att,
-    proj,
-    d_out,
-    dq,
-    acc,
-    delta,
-    back,
-    got,
-    scaled,
-    tab,
-    msg,
-    late_buffers,
-    late_sems,
-    send,
-    recv,
-    b_send,
-    b_recv,
-    local_sem,
-    m_send,
-    m_recv,
-):
-    s, c, u = where_am_i()
-    span, cols = every.shape[2:]
-    width = resid_hbm.shape[1]
-    heads = cols // HEAD_DIM
-    load = [
-        pltpu.make_async_copy(all_hbm, every, local_sem.at[0]),
-        pltpu.make_async_copy(att_hbm, att, local_sem.at[1]),
-        pltpu.make_async_copy(tab_ref.at[rows_of(c, span)], tab, local_sem.at[2]),
-        pltpu.make_async_copy(proj_hbm, proj, local_sem.at[3]),
-    ]
-    last = 2 * (dgu_hbm.shape[2] // late_buffers[2].shape[1])
-    late = LatePiece(
-        last - 2,
-        (resid_hbm, resid_s_hbm, dgu_hbm, dgu_s_hbm),
-        (own_out, x_out, y_out),
-        late_buffers,
-        late_sems,
-    )
-    late.load()
-    for copy in load:
-        copy.start()
-    peers = [(s, c ^ k, u) for k in (1, 2, 3)]
-    greet([(None, peer) for peer in peers] + all_uly_peers(n))
-    copies = []
-    for k, peer in enumerate(peers):
-        copy = remote(do_ref.at[peer[1]], d_out.at[c], send.at[k], recv.at[k], peer)
-        copy.start()
-        copies.append(copy)
-    pieces = Pieces([late.work()])
-    d_out[pl.ds(c, 1)] = do_ref[pl.ds(c, 1)]
-    dq[...] = jnp.zeros_like(dq)
-    bound = bound_ref[:1, :1]
-    scale = HEAD_DIM ** (-0.5)
-    load[0].wait()
-    load[1].wait()
-    for k, peer in enumerate(peers):
-        there = d_out.at[peer[1]]
-        remote(there, there, send.at[k], recv.at[k], peer).wait_recv()
-    pieces.step()
-    for i in range(4):
-        for h in range(heads):
-            lanes = slice(h * HEAD_DIM, (h + 1) * HEAD_DIM)
-            both = jnp.transpose(d_out[i, :, lanes].astype(F32)) * att[i, lanes, :]
-            delta[i, h, :1, :] = jnp.sum(both, axis=0, keepdims=True)
-
-    def home(j):
-        return remote(back.at[j], got.at[c], b_send.at[j], b_recv.at[c], (s, j, u))
-
-    def step(j, carry):
-        acc[...] = jnp.zeros_like(acc)
-        for h in range(heads):
-            lanes = slice(h * HEAD_DIM, (h + 1) * HEAD_DIM)
-
-            def update(i, diagonal):
-                starts = segment_starts(i * span, span, bound)
-                keys, values = every[j, 1, :, lanes], every[j, 2, :, lanes]
-                query, grad = every[i, 0, :, lanes], d_out[i, :, lanes]
-                scores = dot(keys, query, NT) * SCALE2
-                scores = score_mask(scores, j * span, i * span, starts, diagonal)
-                probs = jnp.exp2(scores - lse_ref[i, h, :1, :])
-                acc[1, :, lanes] += dot(probs.astype(BF16), grad, NN)
-                d_probs = dot(values, grad, NT)
-                d_scores = (probs * (d_probs - delta[i, h, :1, :])).astype(BF16)
-                acc[0, :, lanes] += dot(d_scores, query, NN) * scale
-                dq[i, :, lanes] += dot(d_scores, keys, TN) * scale
-
-            def after(i, carry):
-                update(i, False)
-                return carry
-
-            update(j, True)
-            lax.fori_loop(j + 1, 4, after, 0)
-        back[j, 0] = dq[j].astype(BF16)
-        back[j, 1] = acc[0].astype(BF16)
-        back[j, 2] = acc[1].astype(BF16)
-
-        @pl.when(j != c)
-        def _():
-            home(j).start()
-
-        return carry
-
-    lax.fori_loop(0, 4, step, 0)
-    pieces.finish()
-    got[pl.ds(c, 1)] = back[pl.ds(c, 1)]
-    load[2].wait()
-    load[3].wait()
-    for k in (1, 2, 3):
-        j = c ^ k
-        remote(got.at[j], got.at[j], b_send.at[c], b_recv.at[j], (s, j, u)).wait_recv()
-    for j in range(4):
-        dproj_ref[2, :, j * cols : (j + 1) * cols] = got[j, 2]
-
-    def source(i, h):
-        group, inside = divmod(h, heads)
-        lanes = slice(inside * HEAD_DIM, (inside + 1) * HEAD_DIM)
-        return got[group, i, :, lanes].astype(F32)
-
-    rows = norms_back(n, source, scaled, proj, inv_ref, gain_ref, tab, dgain_ref)
-    total = exchange_rows(n, rows, msg, m_send, m_recv)
-    means = to_columns(total) / width
-    for i in range(2):
-        inverse = inv_ref[:, i : i + 1]
-        factor = inverse**3 * means[:, i : i + 1]
-        dproj_ref[i] = (inverse * scaled[i] - proj[i] * factor).astype(BF16)
-    late.plane.finish(1)
-    for j in range(4):
-
-        @pl.when(j != c)
-        def _():
-            home(j).wait_send()
-
-    for copy in copies:
-        copy.wait_send()
-
-
-def attend_spread_back(
-    n, every, d_out, att, lse, bound, proj, inv, gain, table, late, grads
-):
-    span, cols = every.shape[2:]
-    heads = cols // HEAD_DIM
-    width, ff = late[0].shape[1], late[2].shape[2]
-    return pl.pallas_call(
-        functools.partial(attend_spread_back_kernel, n),
-        out_shape=(shape((3, span, 4 * cols), BF16), shape((2, 4 * cols), F32))
-        + tuple(shape(g.shape, BF16) for g in grads),
-        in_specs=[HB, VM, HB, VM, VM, HB, VM, VM] + [HB] * 8,
-        out_specs=(VM, VM, HB, HB, HB),
-        input_output_aliases={13: 2, 14: 3, 15: 4},
-        scratch_shapes=[
-            pltpu.VMEM(every.shape, BF16),
-            pltpu.VMEM(att.shape, F32),
-            pltpu.VMEM(proj.shape, F32),
-            pltpu.VMEM((4, span, cols), BF16),
-            pltpu.VMEM((4, span, cols), F32),
-            pltpu.VMEM((2, span, cols), F32),
-            pltpu.VMEM((4, heads, 8, span), F32),
-            pltpu.VMEM((4, 3, span, cols), BF16),
-            pltpu.VMEM((4, 3, span, cols), BF16),
-            pltpu.VMEM((2, span, 4 * cols), F32),
-            pltpu.VMEM((span, 128), F32),
-            pltpu.VMEM((n, 8, span), F32),
-        ]
-        + LatePiece.scratch(span, width, ff)
-        + [
-            pltpu.SemaphoreType.DMA((3,)),
-            pltpu.SemaphoreType.DMA((3,)),
-            pltpu.SemaphoreType.DMA((4,)),
-            pltpu.SemaphoreType.DMA((4,)),
-            pltpu.SemaphoreType.DMA((4,)),
-            pltpu.SemaphoreType.DMA((n - 1,)),
-            pltpu.SemaphoreType.DMA((n - 1,)),
-        ],
-        compiler_params=pltpu.CompilerParams(
-            collective_id=9, has_side_effects=True, vmem_limit_bytes=VMEM_LIMIT
-        ),
-        name="attend_spread_back",
-    )(every, d_out, att, lse, bound, proj, inv, gain, table, *late, *grads)
 
 
 def attend_back_kernel(
@@ -1643,6 +1288,388 @@
         ),
         name="attend_back",
     )(q, kvall, d_out, attn32, lse, bound, proj, inv, gain, table, *late, *grads)
+
+
+class Keep:
+    def __init__(self, sems):
+        self.sems, self.copies = sems, []
+
+    def __call__(self, src, dst):
+        copy = pltpu.make_async_copy(src, dst, self.sems.at[len(self.copies)])
+        copy.start()
+        self.copies.append(copy)
+        return copy
+
+    def finish(self, but=()):
+        for copy in self.copies:
+            if not any(copy is done for done in but):
+                copy.wait()
+
+
+def forward_kernel(n, names, *refs):
+    ref = dict(zip(names, refs))
+    (x_ref, w_ref, tab_ref, gain_ref, seg_ref, wo_ref, gu_ref, down_ref, post_ref) = [
+        ref[name] for name in ("x", "w", "table", "gain", "seg", "wo", "gu", "down", "post")
+    ]
+    s, c, u = where_am_i()
+    rows, width = x_ref.shape
+    span, half = n * rows, rows // 2
+    kb = w_ref.shape[1]
+    xg, wq, proj, qkv = ref["v_xg"], ref["v_wq"], ref["v_proj"], ref["v_qkv"]
+    every, back, attn = ref["v_every"], ref["v_back"], ref["v_attn"]
+    cols = proj.shape[2]
+    quarter = cols // 4
+    keep, load = Keep(ref["keep_sem"]), Keep(ref["load_sem"])
+    table = load(tab_ref.at[rows_of(c, span)], ref["v_tab"])
+    xg[rows_of(u, rows), :] = x_ref[...]
+    peers = [(s, c ^ k, u) for k in (1, 2, 3)]
+    greet(all_uly_peers(n) + [(None, peer) for peer in peers] + [(None, (1 - s, c, u))])
+
+    def plane(k, src, block, half_rows):
+        return PlaneGather(
+            src, block, half_rows, ref["w_send"].at[k], ref["w_recv"].at[k], ref["w_local"].at[k]
+        )
+
+    def plane_to(k, src, out):
+        return plane(k, src, lambda b: out.at[b], src.shape[0] // 2)
+
+    lower, upper = pl.ds(0, kb // 2), pl.ds(kb // 2, kb // 2)
+    w_qkv = plane(0, w_ref, lambda b: wq.at[:, rows_of(b, kb)], kb // 2)
+    w_out = plane_to(1, wo_ref, ref["o_wo"])
+    w_a = plane_to(2, gu_ref.at[0, lower], ref["o_wga"])
+    w_b = plane_to(3, gu_ref.at[0, upper], ref["o_wgb"])
+    w_c = plane_to(4, gu_ref.at[1], ref["o_wgc"])
+    w_d = plane_to(5, down_ref, ref["o_wd"])
+
+    gather = LineGather(n, rows, xg, [ref[f"x_sem{i}"] for i in range(4)])
+    gather.send(0)
+    w_qkv.start()
+    gather.wait(0)
+    w_qkv.middle()
+    w_out.start()
+    if n > 2:
+        gather.wait(1)
+    w_qkv.corner()
+    w_a.start()
+    w_out.middle()
+    for slot in range(2 if n > 2 else 1, n - 1):
+        gather.wait(slot)
+    w_qkv.arrive()
+    keep(xg, ref["o_xg"])
+    keep(wq, ref["o_wq"])
+    count, size = tiles(span, 512)
+
+    def project(i, carry):
+        where = pl.ds(pl.multiple_of(i * size, size), size)
+        xs = xg[where, :]
+        proj[0, where, :] = dot(xs, wq[0], NN)
+        proj[1, where, :] = dot(xs, wq[1], NN)
+        value = dot(xs, wq[2], NN).astype(BF16)
+        for q in range(4):
+            qkv[q, 2, where, :] = value[:, q * quarter : (q + 1) * quarter]
+        return carry
+
+    lax.fori_loop(0, count, project, 0)
+    keep(proj, ref["o_proj"])
+    squares = [jnp.sum(proj[i] * proj[i], axis=-1, keepdims=True) for i in range(2)]
+    mine = to_rows(*squares)
+    zeros = jnp.sum((1 - seg_ref[...]).astype(F32))
+    row = lax.broadcasted_iota(jnp.int32, mine.shape, 0)
+    mine = jnp.where(row == 2, zeros, mine)
+    total = exchange_rows(n, mine, ref["v_msg"], ref["m_send"], ref["m_recv"])
+    zmsg = ref["v_zmsg"]
+    zmsg[pl.ds(c, 1)] = jnp.broadcast_to(total[2:3, :128], (1, 8, 128))
+    inv = ref["v_inv"]
+    inv[...] = lax.rsqrt(to_columns(total) / width + EPS)
+    table.wait()
+    cosine, sine = rope_factors(ref["v_tab"][...])
+    for i in range(2):
+        inverse = inv[:, i : i + 1]
+        for h in range(cols // HEAD_DIM):
+            lanes = slice(h * HEAD_DIM, (h + 1) * HEAD_DIM)
+            v = proj[i, :, lanes] * inverse * gain_ref[i : i + 1, lanes]
+            v = (v * cosine + pltpu.roll(v, HALF, 1) * sine).astype(BF16)
+            group, inside = divmod(h * HEAD_DIM, quarter)
+            qkv[group, i, :, inside : inside + HEAD_DIM] = v
+
+    copies, arrivals = [], []
+    a_send, a_recv, z_send, z_recv = ref["a_send"], ref["a_recv"], ref["z_send"], ref["z_recv"]
+    for k, peer in enumerate(peers):
+        there = peer[1]
+        copy = remote(qkv.at[there], every.at[c], a_send.at[k], a_recv.at[k], peer)
+        copy.start()
+        small = remote(zmsg.at[c], zmsg.at[c], z_send.at[k], z_recv.at[k], peer)
+        small.start()
+        copies += [copy, small]
+        arrivals.append(remote(every.at[there], every.at[there], a_send.at[k], a_recv.at[k], peer))
+        arrivals.append(remote(zmsg.at[there], zmsg.at[there], z_send.at[k], z_recv.at[k], peer))
+    every[pl.ds(c, 1)] = qkv[pl.ds(c, 1)]
+    keep(inv, ref["o_inv"])
+    w_a.middle()
+    w_out.corner()
+    w_out.arrive()
+    load_o = load_blocks(ref["o_wo"], ref["v_wo"], ref["wo_sem"], 1)
+    for arrival in arrivals:
+        arrival.wait_recv()
+    w_b.start()
+    keep(every, ref["o_every"])
+    bounds = (zmsg[0] + zmsg[1] + zmsg[2] + zmsg[3]).astype(jnp.int32)
+    ref["v_bound"][...] = bounds
+    bound = bounds[:1, :1]
+    peaks, sums, acct = ref["v_peaks"], ref["v_sums"], ref["v_acct"]
+    att, lse = ref["v_att"], ref["v_lse"]
+
+    def attend(k, carry):
+        i = c ^ (3 - k)
+        first_q = i * span
+        starts = segment_starts(first_q, span, bound)
+        for h in range(quarter // HEAD_DIM):
+            lanes = slice(h * HEAD_DIM, (h + 1) * HEAD_DIM)
+            peaks[...] = jnp.full_like(peaks, FLOOR)
+            sums[...] = jnp.zeros_like(sums)
+            acct[...] = jnp.zeros_like(acct)
+
+            def update(j, diagonal):
+                scores = dot(every[j, 1, :, lanes], every[i, 0, :, lanes], NT) * SCALE2
+                scores = score_mask(scores, j * span, first_q, starts, diagonal)
+                old = peaks[:1, :]
+                new = jnp.maximum(old, jnp.max(scores, axis=0, keepdims=True))
+                factor = jnp.exp2(old - new)
+                weights = jnp.exp2(scores - new)
+                peaks[:1, :] = new
+                sums[:1, :] = sums[:1, :] * factor + jnp.sum(weights, axis=0, keepdims=True)
+                acct[...] = acct[...] * factor + dot(
+                    every[j, 2, :, lanes], weights.astype(BF16), TN
+                )
+
+            def before(j, carry):
+                update(j, False)
+                return carry
+
+            lax.fori_loop(0, i, before, 0)
+            update(i, True)
+            total = sums[:1, :]
+            attention = acct[...] / total
+            att[pl.ds(i, 1), lanes, :] = attention[None]
+            back[pl.ds(k, 1), :, :, lanes] = (
+                jnp.transpose(attention).astype(BF16).reshape(1, n, rows, HEAD_DIM)
+            )
+            lse[pl.ds(i, 1), h, :1, :] = (peaks[:1, :] + jnp.log2(total))[None]
+
+        @pl.when(k < 3)
+        def _():
+            home(k, i, c).start()
+
+        return carry
+
+    def home(k, i, owner):
+        return remote(
+            back.at[k],
+            attn.at[:, :, pl.ds(pl.multiple_of(owner * quarter, quarter), quarter)],
+            ref["b_send"].at[k],
+            ref["b_recv"].at[k],
+            (s, i, u),
+        )
+
+    lax.fori_loop(0, 4, attend, 0)
+    attn[:, :, pl.ds(pl.multiple_of(c * quarter, quarter), quarter)] = back[3]
+    keep(att, ref["o_att"])
+    keep(lse, ref["o_lse"])
+    keep(ref["v_bound"], ref["o_bound"])
+    w_a.corner()
+    for k in range(3):
+        i = c ^ (3 - k)
+        home(k, i, i).wait_recv()
+    keep(attn, ref["o_attn"])
+    wait_all(load_o)
+    w_a.arrive()
+    wg = ref["v_wg"]
+    load(ref["o_wga"], wg.at[0, :, lower])
+
+    wo, part, group = ref["v_wo"], ref["v_part"], ref["v_group"]
+    halves = Halves(n, rows)
+    per_half, chunk_cols = part.shape[0] // 2, part.shape[2]
+
+    def compute(chunk):
+        h, q = divmod(chunk, per_half)
+        lanes = slice(q * chunk_cols, (q + 1) * chunk_cols)
+
+        def tile(index, start, size):
+            part[chunk, start : start + size, :] = dot(
+                halves.load(attn, index), wo[:, lanes], NN
+            ).astype(BF16)
+
+        halves.each(h, tile)
+
+    reduce = LineReduce(n, half, part, ref["v_got"], [ref[f"r_sem{i}"] for i in range(4)])
+    g_sems = [ref[f"g_sem{i}"] for i in range(4)]
+    gathers = [LineGather(n, rows, group, g_sems, (h, half)) for h in range(2)]
+    branch, resid = ref["v_branch"], ref["v_resid"]
+    gate, up, hidden = ref["v_gate"], ref["v_up"], ref["v_hidden"]
+
+    def finish(h):
+        where = slice(h * half, (h + 1) * half)
+        reduce.last(branch.at[h], range(h * per_half, (h + 1) * per_half))
+        values = branch[h]
+        total = x_ref[where, :].astype(F32) + values * inverse_rms(values) * post_ref[0:1, :]
+        resid[h] = total
+        group[pl.ds(u, 1), where, :] = total.astype(BF16)[None]
+
+    ff = gate.shape[2]
+    ntile, tsize = tiles(ff, 512)
+
+    def body(h, t):
+        lanes = slice(t * tsize, (t + 1) * tsize)
+
+        def tile(index, start, size):
+            inputs = halves.load(group, index)
+            gates = dot(inputs, wg[0, :, :, lanes].reshape(width, tsize), NN)
+            ups = dot(inputs, wg[1, :, :, lanes].reshape(width, tsize), NN)
+            halves.store(gate, index, lanes, gates.astype(BF16))
+            halves.store(up, index, lanes, ups.astype(BF16))
+            halves.store(
+                hidden, index, lanes, (gates * jax.nn.sigmoid(gates) * ups).astype(BF16)
+            )
+
+        halves.each(h, tile)
+        if h == 1:
+            for name, src in (("o_hidden", hidden), ("o_gate", gate), ("o_up", up)):
+                keep(src.at[:, :, lanes], ref[name].at[:, :, lanes])
+
+    def hook(label):
+        if label == "started":
+            w_b.middle()
+            w_c.start()
+        if label == "sent":
+            w_b.corner()
+        if label == "b1":
+            w_b.arrive()
+            load(ref["o_wgb"], wg.at[0, :, upper])
+        if label == f"b{n - 2}":
+            w_c.middle()
+        if label == "first":
+            keep(branch, ref["o_branch"])
+            keep(resid, ref["o_resid"])
+            w_c.corner()
+            w_d.start()
+            w_c.arrive()
+            load(ref["o_wgc"], wg.at[1])
+            load.finish((table,))
+        if label == f"g{n - 2}":
+            keep(group, ref["o_group"])
+
+    reduce_norm_gather(n, reduce, gathers, compute, finish, Consume(ntile, body), hook)
+    w_d.middle()
+    w_d.corner()
+    w_d.arrive()
+    for k in range(3):
+        home(k, c ^ (3 - k), c).wait_send()
+    for copy in copies:
+        copy.wait_send()
+    for work in (w_qkv, w_out, w_a, w_b, w_c, w_d, gather):
+        work.finish()
+    keep.finish()
+
+
+def forward(n, x, w, table, gain, seg, wo, gu, down, post):
+    rows, width = x.shape
+    span, cols, half = n * rows, w.shape[2], rows // 2
+    quarter = cols // 4
+    kb, ff = gu.shape[1:]
+    ntile = tiles(ff, 512)[0]
+    dma = pltpu.SemaphoreType.DMA
+    ins = {
+        "x": (x, VM),
+        "w": (w, HB),
+        "table": (table, HB),
+        "gain": (gain, VM),
+        "seg": (seg, VM),
+        "wo": (wo, HB),
+        "gu": (gu, HB),
+        "down": (down, HB),
+        "post": (post, VM),
+    }
+    outs = {
+        "o_xg": ((span, width), BF16),
+        "o_wq": ((3, width, cols), BF16),
+        "o_wo": ((8,) + wo.shape, BF16),
+        "o_wga": ((8, kb // 2, ff), BF16),
+        "o_wgb": ((8, kb // 2, ff), BF16),
+        "o_wgc": ((8, kb, ff), BF16),
+        "o_wd": ((8,) + down.shape, BF16),
+        "o_proj": ((2, span, cols), F32),
+        "o_inv": ((span, 128), F32),
+        "o_every": ((4, 3, span, quarter), BF16),
+        "o_att": ((4, quarter, span), F32),
+        "o_lse": ((4, quarter // HEAD_DIM, 8, span), F32),
+        "o_bound": ((8, 128), jnp.int32),
+        "o_attn": ((n, rows, cols), BF16),
+        "o_branch": ((2, half, width), F32),
+        "o_resid": ((2, half, width), F32),
+        "o_group": ((n, rows, width), BF16),
+        "o_gate": ((n, rows, ff), BF16),
+        "o_up": ((n, rows, ff), BF16),
+        "o_hidden": ((n, rows, ff), BF16),
+    }
+    buffers = {
+        "v_xg": ((span, width), BF16),
+        "v_wq": ((3, width, cols), BF16),
+        "v_tab": ((span, 128), F32),
+        "v_proj": ((2, span, cols), F32),
+        "v_inv": ((span, 128), F32),
+        "v_msg": ((n, 8, span), F32),
+        "v_qkv": ((4, 3, span, quarter), BF16),
+        "v_every": ((4, 3, span, quarter), BF16),
+        "v_back": ((4, n, rows, quarter), BF16),
+        "v_zmsg": ((4, 8, 128), F32),
+        "v_bound": ((8, 128), jnp.int32),
+        "v_peaks": ((8, span), F32),
+        "v_sums": ((8, span), F32),
+        "v_acct": ((HEAD_DIM, span), F32),
+        "v_att": ((4, quarter, span), F32),
+        "v_lse": ((4, quarter // HEAD_DIM, 8, span), F32),
+        "v_attn": ((n, rows, cols), BF16),
+        "v_wo": ((cols, width), BF16),
+        "v_wg": ((2, 8, kb, ff), BF16),
+        "v_group": ((n, rows, width), BF16),
+        "v_branch": ((2, half, width), F32),
+        "v_resid": ((2, half, width), F32),
+        "v_gate": ((n, rows, ff), BF16),
+        "v_up": ((n, rows, ff), BF16),
+        "v_hidden": ((n, rows, ff), BF16),
+        "v_part": ((4, n * half, width // 2), BF16),
+        "v_got": ((4, (n + 1) * half, width // 2), BF16),
+    }
+    sems = {
+        "keep_sem": (12 + 3 * ntile,),
+        "load_sem": (4,),
+        "wo_sem": (8,),
+        "w_send": (6, 9),
+        "w_recv": (6, 9),
+        "w_local": (6,),
+        "m_send": (n - 1,),
+        "m_recv": (n - 1,),
+    }
+    for name in ("a_send", "a_recv", "z_send", "z_recv", "b_send", "b_recv"):
+        sems[name] = (3,)
+    for i in range(4):
+        sems[f"x_sem{i}"] = (n - 1,)
+        sems[f"r_sem{i}"] = (n - 1, 4)
+        sems[f"g_sem{i}"] = (n - 1, 2)
+    names = [*ins, *outs, *buffers, *sems]
+    results = pl.pallas_call(
+        functools.partial(forward_kernel, n, names),
+        out_shape=[shape(*out) for out in outs.values()],
+        in_specs=[spec for value, spec in ins.values()],
+        out_specs=[HB] * len(outs),
+        scratch_shapes=[pltpu.VMEM(*buffer) for buffer in buffers.values()]
+        + [dma(dims) for dims in sems.values()],
+        compiler_params=pltpu.CompilerParams(
+            collective_id=10, has_side_effects=True, vmem_limit_bytes=VMEM_LIMIT
+        ),
+        name="forward",
+    )(*[value for value, spec in ins.values()])
+    return dict(zip(outs, results))
 
 
 def load_blocks(src, dst, sem, axis):
@@ -2653,6 +2680,528 @@
     )
 
 
+class PiecePlane(PlaneReduce):
+    def __init__(self, ring, got, place, send, recv, local):
+        super().__init__(ring, got, (0, 1, 2), place, send, recv, local)
+
+    def halves(self):
+        return 0, 1
+
+    def own_copies(self, piece, blocks):
+        return [
+            pltpu.make_async_copy(
+                blocks.at[self.c, h], self.place(0, piece, h), self.local.at[piece, h]
+            )
+            for h in range(2)
+        ]
+
+    def add(self, slot, block, half, piece):
+        self.ring[slot, block, half] = (
+            self.ring[slot, block, half].astype(F32) + self.got[piece, half].astype(F32)
+        ).astype(BF16)
+
+
+class Stream:
+    def __init__(self, slots, sem, source, count):
+        self.slots, self.sem, self.source, self.count = slots, sem, source, count
+        for tile in range(slots.shape[0]):
+            self.start(tile)
+
+    def copy(self, tile):
+        slot = tile % self.slots.shape[0]
+        return pltpu.make_async_copy(self.source(tile), self.slots.at[slot], self.sem.at[slot])
+
+    def start(self, tile):
+        if tile < self.count:
+            self.copy(tile).start()
+
+    def wait(self, tile):
+        self.copy(tile).wait()
+
+
+def wide_blocks(own, other, out):
+    rows = out.shape[2]
+
+    def pair(i, carry):
+        where = pl.ds(pl.multiple_of(i * 2 * rows, 2 * rows), 2 * rows)
+        total = dot(own[0][...], own[1][:, where], TN) + dot(other[0][...], other[1][:, where], TN)
+        total = total.astype(BF16)
+        for j in range(2):
+            part = total[:, j * rows : (j + 1) * rows]
+            out[pl.ds(2 * i + j, 1)] = part.reshape(1, 2, rows, rows)
+        return carry
+
+    lax.fori_loop(0, 2, pair, 0)
+
+
+def tall_blocks(own, other, out):
+    rows = out.shape[2]
+
+    def pair(i, carry):
+        where = pl.ds(pl.multiple_of(i * 2 * rows, 2 * rows), 2 * rows)
+        total = dot(own[0][:, where], own[1][...], TN) + dot(other[0][:, where], other[1][...], TN)
+        total = total.astype(BF16)
+        for j in range(2):
+            for h in range(2):
+                out[pl.ds(2 * i + j, 1), h] = total[
+                    j * rows : (j + 1) * rows, h * rows : (h + 1) * rows
+                ][None]
+        return carry
+
+    lax.fori_loop(0, 2, pair, 0)
+
+
+def backward_kernel(n, names, *refs):
+    ref = dict(zip(names, refs))
+    s, c, u = where_am_i()
+    cot_ref, gain_ref, qk_gain_ref = ref["cot"], ref["post"], ref["gain"]
+    rows, width = cot_ref.shape
+    span = n * rows
+    weights, dgu, dgu_s = ref["v_weights"], ref["v_dgu"], ref["v_dgu_s"]
+    hidden, hidden_s, dmlp, dmlp_s = [
+        ref[f"v_{k}"] for k in ("hidden", "hidden_s", "dmlp", "dmlp_s")
+    ]
+    resid, resid_s, branch, attn = [ref[f"v_{k}"] for k in ("resid", "resid_s", "branch", "attn")]
+    part, group, dresid = ref["v_part"], ref["v_group"], ref["v_dresid"]
+    load = Keep(ref["load_sem"])
+    chunks, chunk_cols = part.shape[0], part.shape[2]
+    kb = ref["wgc"].shape[1]
+    per_chunk = chunk_cols // kb
+    lower, upper = kb // 2, kb // 2
+
+
+    rows_g = ref["v_ring"].shape[3]
+    rows_d = cols_g = 2 * rows_g
+    tiles_g = dgu.shape[2] // cols_g
+    n_d, n_g = hidden.shape[1] // rows_d, 2 * tiles_g
+
+    def hidden_tile(view, piece):
+        return view.at[:, pl.ds(piece * rows_d, rows_d)]
+
+    def gate_tile(view, piece):
+        ci, tile = divmod(piece, tiles_g)
+        return view.at[ci, :, pl.ds(tile * cols_g, cols_g)]
+
+    def load_chunk(chunk):
+        slot, copies = chunk % 2, []
+        for b in range(per_chunk):
+            block = chunk * per_chunk + b
+            at = slot * 2 * chunk_cols + b * kb
+            for k, (src, first, size) in enumerate(
+                (
+                    (ref["wga"], at, lower),
+                    (ref["wgb"], at + lower, upper),
+                    (ref["wgc"], at + chunk_cols, kb),
+                )
+            ):
+                copies.append(
+                    pltpu.make_async_copy(
+                        src.at[block],
+                        weights.at[pl.ds(first, size)],
+                        ref["chunk_sem"].at[slot, 3 * b + k],
+                    )
+                )
+        return copies
+
+    def start_chunk(chunk):
+        for copy in load_chunk(chunk):
+            copy.start()
+
+    load_dgu = load(ref["dgu"], dgu)
+    start_chunk(0)
+    load_d = [
+        load(ref["hidden"], hidden),
+        load(half_columns(ref["dmlp"], s), dmlp),
+        load(ref["dmlp_s"], dmlp_s),
+    ]
+    stream_d = Stream(hidden_s, ref["hs_sem"], lambda p: hidden_tile(ref["hidden_s"], p), n_d)
+    start_chunk(1)
+    load_g = [
+        load(half_columns(ref["resid"], s), resid),
+        load(ref["resid_s"], resid_s),
+        load(ref["branch"], branch),
+        load(ref["attn"], attn),
+    ]
+    stream_g = Stream(dgu_s, ref["ds_sem"], lambda p: gate_tile(ref["dgu_s"], p), n_g)
+    wo_row = 4 * chunk_cols
+    wo_cols = ref["wo"].shape[1]
+    wo_view = weights.at[pl.ds(wo_row, wo_cols)]
+    load_o = load_blocks(ref["wo"], wo_view, ref["wo_sem"], 1)
+    peers = [(s, c ^ k, u) for k in (1, 2, 3)]
+    greet(all_uly_peers(n) + [(None, peer) for peer in peers] + [(None, (1 - s, c, u))])
+    sibling = Sibling(ref["s_send"], ref["s_recv"])
+    sibling.start(half_columns(ref["xg"], 1 - s), ref["v_xs_s"])
+    load_dgu.wait()
+    count, size = tiles(span, 512)
+
+    def compute(chunk):
+        wait_all(load_chunk(chunk))
+        at = (chunk % 2) * 2 * chunk_cols
+
+        def tile(i, carry):
+            where = pl.ds(pl.multiple_of(i * size, size), size)
+            part[chunk, where, :] = (
+                dot(dgu[0, where, :], weights[at : at + chunk_cols, :], NT)
+                + dot(dgu[1, where, :], weights[at + chunk_cols : at + 2 * chunk_cols, :], NT)
+            ).astype(BF16)
+            return carry
+
+        lax.fori_loop(0, count, tile, 0)
+        if chunk + 2 < chunks:
+            start_chunk(chunk + 2)
+
+    def place(index, piece, half):
+        if piece < n_d or piece == n_d + n_g:
+            name, first = ("down", piece * rows_d) if piece < n_d else ("out", 0)
+            rows = pl.ds(first + half * rows_g, rows_g)
+            return ref[f"o_{name}{index}"].at[rows]
+        if piece < n_d + n_g:
+            ci, tile = divmod(piece - n_d, tiles_g)
+            lanes = pl.ds(tile * cols_g + half * rows_g, rows_g)
+            return ref[f"o_gate{index}"].at[ci, :, lanes]
+        lanes = pl.ds(half * rows_g, rows_g)
+        return ref[f"o_qkv{index}"].at[piece - n_d - n_g - 1, :, lanes]
+
+    plane = PiecePlane(
+        ref["v_ring"], ref["v_got_p"], place, ref["p_send"], ref["p_recv"], ref["p_local"]
+    )
+    def down_piece(out, piece):
+        stream_d.wait(piece)
+        own, other = hidden_tile(hidden, piece), hidden_s.at[piece % hidden_s.shape[0]]
+        wide_blocks((own, dmlp), (other, dmlp_s), out)
+        stream_d.start(piece + hidden_s.shape[0])
+
+    def gate_piece(out, piece):
+        number = piece - n_d
+        stream_g.wait(number)
+        own, other = gate_tile(dgu, number), dgu_s.at[number % dgu_s.shape[0]]
+        tall_blocks((resid, own), (resid_s, other), out)
+        stream_g.start(number + dgu_s.shape[0])
+
+    def out_piece(out, piece):
+        own = (attn, half_columns(group, s))
+        wide_blocks(own, (ref["v_attn_s"], ref["v_dbranch_s"]), out)
+
+    cols = attn.shape[1]
+    dproj = hidden.at[:, pl.ds(0, 3 * cols)]
+
+    def qkv_piece(out, piece):
+        lanes = pl.ds((piece - n_d - n_g - 1) * cols, cols)
+        own = (dmlp, hidden.at[:, lanes])
+        tall_blocks(own, (ref["v_xs_s"], ref["v_dproj_s"].at[:, lanes]), out)
+
+    kinds = [down_piece] * n_d + [gate_piece] * n_g + [out_piece] + [qkv_piece] * 3
+    pieces = Pieces([(plane, p, kind) for p, kind in enumerate(kinds)], AHEAD)
+
+    def compute_and_piece(chunk):
+        compute(chunk)
+        if chunk == 0:
+            wait_all(load_d)
+        if chunk < 2:
+            pieces.step()
+
+    def reduce_hook(slot):
+        if slot == 0:
+            wait_all(load_g)
+        pieces.step()
+
+    sem_r = [ref[f"r_sem{i}"] for i in range(4)]
+    sem_b = [ref[f"b_sem{i}"] for i in range(4)]
+    LineReduce(n, rows, part, ref["v_got"], sem_r).run(compute_and_piece, dresid, reduce_hook)
+    d_resid = dresid[...] + cot_ref[...].astype(F32)
+    dresid[...] = d_resid
+    values = branch[...]
+    inverse = inverse_rms(values)
+    d_branch = norm_back(values, inverse, d_resid * gain_ref[0:1, :], width)
+    group[rows_of(u, rows), :] = d_branch.astype(BF16)
+    gather = LineGather(n, rows, group, [ref[f"g_sem{i}"] for i in range(4)])
+    gather.send(0)
+    gain_attn = jnp.sum(d_resid * values * inverse, axis=0, keepdims=True)
+    ref["v_gattn"][...] = gain_attn
+    quarter = cols // 4
+    load_a = [
+        load(ref["every"].at[i, t], weights.at[pl.ds(0, span), pl.ds((3 * i + t) * quarter, quarter)])
+        for i in range(4)
+        for t in range(3)
+    ]
+    att, proj, tab = ref["v_att"], ref["v_proj"], ref["v_tab"]
+    load_a.append(load(ref["att"], att))
+    load_p = [load(ref["proj"], proj), load(ref["table"].at[rows_of(c, span)], tab)]
+    pieces.step()
+
+    def gather_hook(slot):
+        if slot == 0:
+            pieces.step(2)
+        if slot == 1:
+            pieces.step()
+
+    gather.run(gather_hook)
+    wait_all(load_o)
+    dattn, d_out = ref["v_dattn"], ref["v_d_out"]
+
+    def tile(j, carry):
+        where = pl.ds(pl.multiple_of(j * size, size), size)
+        d_attn = dot(group[where, :], weights[wo_row : wo_row + wo_cols, :], NT).astype(BF16)
+        for q in range(4):
+            dattn[q, where, :] = d_attn[:, q * quarter : (q + 1) * quarter]
+        return carry
+
+    lax.fori_loop(0, count, tile, 0)
+
+    a_send, a_recv, h_send, h_recv = ref["a_send"], ref["a_recv"], ref["h_send"], ref["h_recv"]
+    copies = []
+    for k, peer in enumerate(peers):
+        copy = remote(dattn.at[peer[1]], d_out.at[c], a_send.at[k], a_recv.at[k], peer)
+        copy.start()
+        copies.append(copy)
+    sibling.start(attn, ref["v_attn_s"])
+    sibling.start(half_columns(group, 1 - s), ref["v_dbranch_s"])
+    d_out[pl.ds(c, 1)] = dattn[pl.ds(c, 1)]
+    dq, acc, delta, got = ref["v_dq"], ref["v_acc"], ref["v_delta"], ref["v_home"]
+    lse_ref = ref["lse"]
+    dq[...] = jnp.zeros_like(dq)
+    bound = ref["bound"][:1, :1]
+    scale = HEAD_DIM ** (-0.5)
+    heads = quarter // HEAD_DIM
+    wait_all(load_a)
+    for k, peer in enumerate(peers):
+        there = d_out.at[peer[1]]
+        remote(there, there, a_send.at[k], a_recv.at[k], peer).wait_recv()
+    pieces.step()
+    for i in range(4):
+        for h in range(heads):
+            lanes = slice(h * HEAD_DIM, (h + 1) * HEAD_DIM)
+            both = jnp.transpose(d_out[i, :, lanes].astype(F32)) * att[i, lanes, :]
+            delta[i, h, :1, :] = jnp.sum(both, axis=0, keepdims=True)
+
+    def seen(i, t, h):
+        first = (3 * i + t) * quarter + h * HEAD_DIM
+        return weights[:span, pl.ds(pl.multiple_of(first, HEAD_DIM), HEAD_DIM)]
+
+    def going(j):
+        first = pl.multiple_of(3 * j * quarter, 3 * quarter)
+        return weights.at[pl.ds(wo_row, span), pl.ds(first, 3 * quarter)]
+
+    def home(j):
+        return remote(going(j), got.at[c], h_send.at[j], h_recv.at[c], (s, j, u))
+
+    def step(j, carry):
+        acc[...] = jnp.zeros_like(acc)
+        for h in range(heads):
+            lanes = slice(h * HEAD_DIM, (h + 1) * HEAD_DIM)
+
+            def update(i, diagonal):
+                starts = segment_starts(i * span, span, bound)
+                keys, values = seen(j, 1, h), seen(j, 2, h)
+                query, grad = seen(i, 0, h), d_out[i, :, lanes]
+                scores = dot(keys, query, NT) * SCALE2
+                scores = score_mask(scores, j * span, i * span, starts, diagonal)
+                probs = jnp.exp2(scores - lse_ref[i, h, :1, :])
+                acc[1, :, lanes] += dot(probs.astype(BF16), grad, NN)
+                d_probs = dot(values, grad, NT)
+                d_scores = (probs * (d_probs - delta[i, h, :1, :])).astype(BF16)
+                acc[0, :, lanes] += dot(d_scores, query, NN) * scale
+                dq[i, :, lanes] += dot(d_scores, keys, TN) * scale
+
+            def after(i, carry):
+                update(i, False)
+                return carry
+
+            update(j, True)
+            lax.fori_loop(j + 1, 4, after, 0)
+        first = pl.multiple_of(3 * j * quarter, 3 * quarter)
+        weights[wo_row : wo_row + span, pl.ds(first, 3 * quarter)] = jnp.concatenate(
+            [dq[j].astype(BF16), acc[0].astype(BF16), acc[1].astype(BF16)], axis=1
+        )
+
+        @pl.when(j != c)
+        def _():
+            home(j).start()
+
+        return carry
+
+    lax.fori_loop(0, 4, step, 0)
+    load_q = [
+        load(ref["wq"].at[i], weights.at[pl.ds(0, width), pl.ds(i * cols, cols)]) for i in range(3)
+    ]
+    load_x = load(half_columns(ref["xg"], s), dmlp)
+    got[pl.ds(c, 1)] = going(c)[...][None]
+    wait_all(load_p)
+    for k in (1, 2, 3):
+        j = c ^ k
+        remote(got.at[j], got.at[j], h_send.at[c], h_recv.at[j], (s, j, u)).wait_recv()
+    pieces.step()
+    kept, inv_ref = (dq, ref["v_dk"]), ref["inv"]
+    for j in range(4):
+        hidden[:, 2 * cols + j * quarter : 2 * cols + (j + 1) * quarter] = got[
+            j, :, 2 * quarter : 3 * quarter
+        ]
+
+    def source(i, h):
+        group, inside = divmod(h, heads)
+        first = i * quarter + inside * HEAD_DIM
+        return got[group, :, first : first + HEAD_DIM].astype(F32)
+
+    gcols = ref["v_gcols"]
+
+    def store(i, h, values):
+        group, inside = divmod(h, heads)
+        kept[i][group, :, inside * HEAD_DIM : (inside + 1) * HEAD_DIM] = values
+
+    dots = norms_back(source, store, proj, inv_ref, qk_gain_ref, tab, gcols)
+    total = exchange_rows(n, dots, ref["v_msg"], ref["m_send"], ref["m_recv"])
+    means = to_columns(total) / width
+    for i in range(2):
+        inverse = inv_ref[:, i : i + 1]
+        factor = inverse**3 * means[:, i : i + 1]
+        for j in range(4):
+            lanes = slice(j * quarter, (j + 1) * quarter)
+            hidden[:, i * cols + j * quarter : i * cols + (j + 1) * quarter] = (
+                inverse * kept[i][j] - proj[i, :, lanes] * factor
+            ).astype(BF16)
+    sibling.start(dproj, ref["v_dproj_s"])
+    gains = GainSum(
+        n,
+        [ref[f"v_sum{i}"] for i in range(4)],
+        (ref["v_send"], ref["v_recv"], ref["n_send"], ref["n_recv"]),
+    )
+    gains.start(gcols, ref["v_gattn"], ref["gmlp"])
+    wait_all(load_q)
+
+    def compute_input(chunk):
+        lanes = slice(chunk * chunk_cols, (chunk + 1) * chunk_cols)
+
+        def tile(i, carry):
+            where = pl.ds(pl.multiple_of(i * size, size), size)
+            part[chunk, where, :] = dot(
+                hidden[where, : 3 * cols], weights[lanes, : 3 * cols], NT
+            ).astype(BF16)
+            return carry
+
+        lax.fori_loop(0, count, tile, 0)
+        if chunk == 0:
+            pieces.step()
+        if chunk == 2:
+            sibling.wait(1)
+            sibling.wait(2)
+            pieces.step()
+
+    def input_hook(slot):
+        if slot == 0:
+            load_x.wait()
+            sibling.wait(0)
+            sibling.wait(3)
+            gains.over_ctx()
+        if slot == 1:
+            gains.over_uly()
+        pieces.step()
+
+    LineReduce(n, rows, part, ref["v_got"], sem_b).run(compute_input, branch, input_hook)
+    ref["o_input"][...] = (dresid[...] + branch[...]).astype(BF16)
+    pieces.finish()
+    gains.finish(ref["o_gain"])
+    plane.finish(len(kinds))
+    sibling.finish()
+    for j in range(4):
+
+        @pl.when(j != c)
+        def _():
+            home(j).wait_send()
+
+    for copy in copies:
+        copy.wait_send()
+
+
+def backward(n, ins):
+    rows, width = ins["cot"][0].shape
+    span, ff = n * rows, ins["hidden"][0].shape[1]
+    cols = ins["attn"][0].shape[1]
+    quarter = cols // 4
+    kb, kc = width // 8, ins["wo"][0].shape[2]
+    n_d, size = tiles(ff, 512)
+    dma = pltpu.SemaphoreType.DMA
+    outs = {"o_input": ((rows, width), BF16), "o_gain": ((4, width // 8), F32)}
+    for i in range(3):
+        outs[f"o_down{i}"] = ((ff, kc), BF16)
+        outs[f"o_gate{i}"] = ((2, kb, ff), BF16)
+        outs[f"o_out{i}"] = ((cols, kc), BF16)
+        outs[f"o_qkv{i}"] = ((3, kb, cols), BF16)
+    buffers = {
+        "v_weights": ((width + cols, width), BF16),
+        "v_dgu": ((2, span, ff), BF16),
+        "v_dgu_s": ((3, span, size), BF16),
+        "v_hidden": ((span, ff), BF16),
+        "v_hidden_s": ((2, span, size), BF16),
+        "v_dmlp": ((span, width // 2), BF16),
+        "v_dmlp_s": ((span, width // 2), BF16),
+        "v_resid": ((span, width // 2), BF16),
+        "v_resid_s": ((span, width // 2), BF16),
+        "v_branch": ((rows, width), F32),
+        "v_attn": ((span, cols), BF16),
+        "v_dresid": ((rows, width), F32),
+        "v_group": ((span, width), BF16),
+        "v_part": ((CHUNKS, span, width // CHUNKS), BF16),
+        "v_got": ((CHUNKS, span + rows, width // CHUNKS), BF16),
+        "v_ring": ((AHEAD + 1, 4, 2, kb, kb), BF16),
+        "v_got_p": ((3 * n_d + 4, 2, kb, kb), BF16),
+        "v_gattn": ((1, width), F32),
+        "v_att": ((4, quarter, span), F32),
+        "v_proj": ((2, span, cols), F32),
+        "v_tab": ((span, 128), F32),
+        "v_dattn": ((4, span, quarter), BF16),
+        "v_d_out": ((4, span, quarter), BF16),
+        "v_dq": ((4, span, quarter), F32),
+        "v_acc": ((2, span, quarter), F32),
+        "v_delta": ((4, quarter // HEAD_DIM, 8, span), F32),
+        "v_home": ((4, span, 3 * quarter), BF16),
+        "v_dk": ((4, span, quarter), F32),
+        "v_gcols": ((2, cols), F32),
+        "v_msg": ((n, 8, span), F32),
+        "v_xs_s": ((span, width // 2), BF16),
+        "v_attn_s": ((span, cols), BF16),
+        "v_dbranch_s": ((span, width // 2), BF16),
+        "v_dproj_s": ((span, 3 * cols), BF16),
+        "v_sum0": ((2, 8, width // 2), F32),
+        "v_sum1": ((8, width // 2), F32),
+        "v_sum2": ((4, 8, width // 8), F32),
+        "v_sum3": ((3 + n, 8, width // 8), F32),
+    }
+    sems = {
+        "load_sem": (32,),
+        "chunk_sem": (2, 3 * (width // CHUNKS // kb)),
+        "wo_sem": (8,),
+        "hs_sem": (2,),
+        "ds_sem": (3,),
+        "p_send": (3 * n_d + 4, 6),
+        "p_recv": (3 * n_d + 4, 6),
+        "p_local": (3 * n_d + 4, 2),
+        "a_send": (3,),
+        "a_recv": (3,),
+    }
+    for name in ("s_send", "s_recv", "h_send", "h_recv", "v_send", "v_recv"):
+        sems[name] = (4,)
+    for name in ("m_send", "m_recv", "n_send", "n_recv"):
+        sems[name] = (n - 1,)
+    for i in range(4):
+        sems[f"r_sem{i}"] = (n - 1, CHUNKS)
+        sems[f"b_sem{i}"] = (n - 1, CHUNKS)
+        sems[f"g_sem{i}"] = (n - 1,)
+    names = [*ins, *outs, *buffers, *sems]
+    results = pl.pallas_call(
+        functools.partial(backward_kernel, n, names),
+        out_shape=[shape(*out) for out in outs.values()],
+        in_specs=[spec for value, spec in ins.values()],
+        out_specs=[VM, VM] + [HB] * 12,
+        scratch_shapes=[pltpu.VMEM(*buffer) for buffer in buffers.values()]
+        + [dma(dims) for dims in sems.values()],
+        compiler_params=pltpu.CompilerParams(
+            collective_id=11, has_side_effects=True, vmem_limit_bytes=63 * 1024 * 1024
+        ),
+        name="backward",
+    )(*[value for value, spec in ins.values()])
+    return dict(zip(outs, results))
+
+
 def rope_table(length):
     freqs = np.power(
         np.float32(ROPE_BASE), -(np.arange(HALF, dtype=np.float32) * 2.0 / HEAD_DIM)
@@ -2678,18 +3227,35 @@
     width = x.shape[1]
     cot = cotangent[0]
     table = jnp.asarray(table)
-    group_x, wq, wo, wga, proj, qkv, inv, zero = project(
-        n, x, qkv_weight, table, qk_gain, segment_ids, out_weight, gate_up
-    )
-    if len(qkv) == 1:
-        every, wgb, attn, att, lse, bound = attend_spread(qkv[0], zero, gate_up)
-        seen, back = (every,), attend_spread_back
+    if spread_heads(qkv_weight.shape[2]):
+        o = forward(
+            n,
+            x,
+            qkv_weight,
+            table,
+            qk_gain,
+            segment_ids,
+            out_weight,
+            gate_up,
+            down_weight,
+            post_gain,
+        )
+        group_x, wq, wo, proj, inv = [o[f"o_{k}"] for k in ("xg", "wq", "wo", "proj", "inv")]
+        wga, wgb, wgc, wd = [o[f"o_{k}"] for k in ("wga", "wgb", "wgc", "wd")]
+        att, lse, bound, attn = [o[f"o_{k}"] for k in ("att", "lse", "bound", "attn")]
+        branch, resid, group_resid = [o[f"o_{k}"] for k in ("branch", "resid", "group")]
+        gate, up, hidden = [o[f"o_{k}"] for k in ("gate", "up", "hidden")]
+        attn = attn.reshape(group_x.shape[0], -1)
+        seen = (o["o_every"],)
     else:
+        group_x, wq, wo, wga, proj, qkv, inv, zero = project(
+            n, x, qkv_weight, table, qk_gain, segment_ids, out_weight, gate_up
+        )
         every, wgb, attn, att, lse, bound = attend(*qkv, zero, gate_up)
         seen, back = (qkv[0], every), attend_back
-    branch, resid, group_resid, gate, up, hidden, wgc, wd = mlp_in(
-        n, attn, wo, x, post_gain, wga, wgb, gate_up, down_weight
-    )
+        branch, resid, group_resid, gate, up, hidden, wgc, wd = mlp_in(
+            n, attn, wo, x, post_gain, wga, wgb, gate_up, down_weight
+        )
     block_out, group_dmlp, dgu, gain_mlp, hidden_s, resid_s, dmlp_s, dgu_s = mlp_out(
         n, hidden, wd, resid, post_gain, cot, gate, up, group_resid
     )
@@ -2699,44 +3265,82 @@
     hidden, hidden_s = hidden.reshape(span, ff), hidden_s.reshape(span, ff)
     group_resid, group_dmlp = group_resid.reshape(span, width), group_dmlp.reshape(span, width)
     resid_s, dmlp_s = resid_s.reshape(span, width // 2), dmlp_s.reshape(span, width // 2)
-    d_resid, group_dbranch, d_attn, gain_attn, *grads = mlp_back(
-        n,
-        dgu,
-        wga,
-        wgb,
-        wgc,
-        cot,
-        branch,
-        post_gain,
-        wo,
-        hidden,
-        group_dmlp,
-        group_resid,
-        hidden_s,
-        resid_s,
-        dmlp_s,
-        dgu_s,
-    )
-    gate_grads, down_grads = grads[:3], grads[3:]
-    late = (group_resid, resid_s, dgu, dgu_s)
-    d_proj, gain_cols, *gate_grads = back(
-        n, *seen, d_attn, att, lse, bound, proj, inv, qk_gain, table, late, gate_grads
-    )
-    input_grad, gain_part, *grads = proj_back(
-        n,
-        d_proj,
-        wq,
-        d_resid,
-        group_x,
-        gain_cols,
-        gain_attn,
-        gain_mlp,
-        attn,
-        group_dbranch,
-        late,
-        gate_grads,
-    )
-    qkv_grads, out_grads, gate_grads = grads[:3], grads[3:6], grads[6:]
+    if spread_heads(qkv_weight.shape[2]):
+        o = backward(
+            n,
+            {
+                "dgu": (dgu, HB),
+                "dgu_s": (dgu_s, HB),
+                "wga": (wga, HB),
+                "wgb": (wgb, HB),
+                "wgc": (wgc, HB),
+                "cot": (cot, VM),
+                "branch": (branch, HB),
+                "post": (post_gain, VM),
+                "gain": (qk_gain, VM),
+                "wo": (wo, HB),
+                "hidden": (hidden, HB),
+                "hidden_s": (hidden_s, HB),
+                "dmlp": (group_dmlp, HB),
+                "dmlp_s": (dmlp_s, HB),
+                "resid": (group_resid, HB),
+                "resid_s": (resid_s, HB),
+                "every": (seen[0], HB),
+                "att": (att, HB),
+                "lse": (lse, VM),
+                "bound": (bound, VM),
+                "attn": (attn, HB),
+                "proj": (proj, HB),
+                "inv": (inv, VM),
+                "table": (table, HB),
+                "wq": (wq, HB),
+                "xg": (group_x, HB),
+                "gmlp": (gain_mlp, VM),
+            },
+        )
+        input_grad, gain_part = o["o_input"], o["o_gain"]
+        qkv_grads, out_grads, gate_grads, down_grads = [
+            [o[f"o_{k}{i}"] for i in range(3)] for k in ("qkv", "out", "gate", "down")
+        ]
+    else:
+        d_resid, group_dbranch, d_attn, gain_attn, *grads = mlp_back(
+            n,
+            dgu,
+            wga,
+            wgb,
+            wgc,
+            cot,
+            branch,
+            post_gain,
+            wo,
+            hidden,
+            group_dmlp,
+            group_resid,
+            hidden_s,
+            resid_s,
+            dmlp_s,
+            dgu_s,
+        )
+        gate_grads, down_grads = grads[:3], grads[3:]
+        late = (group_resid, resid_s, dgu, dgu_s)
+        d_proj, gain_cols, *gate_grads = back(
+            n, *seen, d_attn, att, lse, bound, proj, inv, qk_gain, table, late, gate_grads
+        )
+        input_grad, gain_part, *grads = proj_back(
+            n,
+            d_proj,
+            wq,
+            d_resid,
+            group_x,
+            gain_cols,
+            gain_attn,
+            gain_mlp,
+            attn,
+            group_dbranch,
+            late,
+            gate_grads,
+        )
+        qkv_grads, out_grads, gate_grads = grads[:3], grads[3:6], grads[6:]
 
     def total(parts):
         return parts[0].astype(F32) + parts[1].astype(F32) + parts[2].astype(F32)

time: 514 us -> 475 us (0.924)
  Pallas kernels: 493 us -> 455 us
    pallas_call x6 -> x2, Pallas kernels: 415 us -> 377 us  [the longest x1 192 us: backward(): pl.pallas_call(functools.partial(backward_kernel, n, names), out_shape=[s...]
where the time goes in v5:
time: 475 us; the launch traced here: 470 us
  Pallas kernels  455 us (96%)
  other arithmetic  10.2 us (2%)
    pallas_call x1, Pallas kernels, backward(): pl.pallas_call(functools.partial(backward_kernel, n, names), out_shape=[s...  192 us
    pallas_call x1, Pallas kernels, forward(): pl.pallas_call(functools.partial(forward_kernel, n, names), out_shape=[sh...  185 us
    pallas_call x1, Pallas kernels, mlp_out(): pl.pallas_call(functools.partial(mlp_out_kernel, n), out_shape=(shape((ro...  77.8 us
    add x4, other arithmetic, total(): return parts[0].astype(F32) + parts[1].astype(F32) + parts[2].astype(F32)  10.2 us

profile of v5, /device:TPU:0, one launch (start us, length us, event | category | flops | bytes accessed | tf_op | source)
XLA Modules:
  0.0 469.7 jit_solution(15499285254081769214)
XLA Ops:
  0.6 185.4 %forward.1 = (bf16[512,2048]{1,0:T(8,128)(2,1)}, bf16[3,2048,512]{2,1,0:T(8,128)(2,1)}, bf16[8,512,256]{2,1,0:T(8,128)(2,1)}, bf16[8,128,2048]{2,1,0:T(8,128)(2,...) custom-call(bf16[128,2048]{1,0:T(8,128)(2,1)} %bitcast.28, ...), custom_call_target="tpu_custom_call" | custom-call | tf_op jit(solution)/shard_map/forward/pallas_call | solution.py:1660
  186.0 77.8 %mlp_out.1 = (bf16[128,2048]{1,0:T(8,128)(2,1)}, bf16[4,128,2048]{2,1,0:T(8,128)(2,1)}, bf16[2,4,128,2048]{3,2,1,0:T(8,128)(2,1)}, f32[1,2048]{1,0:T(1,128)}, bf...) custom-call(bf16[4,128,2048]{2,1,0:T(8,128)(2,1)} %get-tuple-element, ...), custom_call_target="tpu_custom_call" | custom-call | tf_op jit(solution)/shard_map/mlp_out/pallas_call | solution.py:2025
  263.8 191.7 %backward.1 = (bf16[128,2048]{1,0:T(8,128)(2,1)}, f32[4,256]{1,0:T(4,128)}, bf16[2048,256]{1,0:T(8,128)(2,1)}, bf16[2,256,2048]{2,1,0:T(8,128)(2,1)}, bf16[512,2...) custom-call(bf16[2,512,2048]{2,1,0:T(8,128)(2,1)} %bitcast.16, ...), custom_call_target="tpu_custom_call" | custom-call | tf_op jit(solution)/shard_map/backward/pallas_call | solution.py:3190
  455.5 0.0 copy-start.4
  455.5 0.0 copy-start.5
  455.5 2.1 convert_add_fusion.3
  457.6 0.0 copy-start.3
  457.6 3.2 convert_add_fusion.2
  460.9 0.0 copy-done.4
  460.9 0.0 copy-done.5
  460.9 0.0 copy-done.3
  460.9 0.0 copy-start
  460.9 0.0 copy-start.1
  460.9 1.7 convert_add_fusion.1
  462.6 0.0 copy-done.2
  462.6 0.5 copy-done
  463.1 0.7 copy-done.1
  463.9 3.2 convert_add_fusion
  467.1 0.0 copy-done.6
  467.1 0.8 copy.20
  467.9 0.0 copy-done.7
  467.9 0.8 copy.21
  468.7 0.0 copy-done.8
  468.7 0.6 copy.22
  (4 shorter events, 0.0 us)
Async XLA Ops:
  455.5 5.4 %copy-start.4 = (bf16[2048,256]{1,0:T(8,128)(2,1)S(1)}, bf16[2048,256]{1,0:T(8,128)(2,1)}, u32[]{:S(2)}) copy-start(bf16[2048,256]{1,0:T(8,128)(2,1)} %get-tuple-element.88) | copy-start | bytes 3145732
  455.5 5.4 %copy-start.5 = (bf16[2048,256]{1,0:T(8,128)(2,1)S(1)}, bf16[2048,256]{1,0:T(8,128)(2,1)}, u32[]{:S(2)}) copy-start(bf16[2048,256]{1,0:T(8,128)(2,1)} %get-tuple-element.89) | copy-start | bytes 3145732
  457.6 3.2 copy-start.3
  457.6 4.9 %copy-start.2 = (bf16[2,256,2048]{2,1,0:T(8,128)(2,1)S(1)}, bf16[2,256,2048]{2,1,0:T(8,128)(2,1)}, u32[]{:S(2)}) copy-start(bf16[2,256,2048]{2,1,0:T(8,128)(2,1)} %get-tuple-element.86) | copy-start | bytes 6291460
  460.9 2.2 copy-start
  460.9 3.0 copy-start.1
  463.9 3.2 copy-start.6
  463.9 4.0 copy-start.7
  467.1 1.6 copy-start.8

commit v6 on v5

--- a/solution.py
+++ b/solution.py
@@ -1,4 +1,5 @@
 import functools
+from types import SimpleNamespace
 
 import jax
 import jax.numpy as jnp
@@ -1307,27 +1308,26 @@
 
 
 def forward_kernel(n, names, *refs):
-    ref = dict(zip(names, refs))
-    (x_ref, w_ref, tab_ref, gain_ref, seg_ref, wo_ref, gu_ref, down_ref, post_ref) = [
-        ref[name] for name in ("x", "w", "table", "gain", "seg", "wo", "gu", "down", "post")
-    ]
+    ref = SimpleNamespace(**dict(zip(names, refs)))
+    x_ref, w_ref, tab_ref, gain_ref, seg_ref = ref.x, ref.w, ref.table, ref.gain, ref.seg
+    wo_ref, gu_ref, down_ref, post_ref = ref.wo, ref.gu, ref.down, ref.post
     s, c, u = where_am_i()
     rows, width = x_ref.shape
     span, half = n * rows, rows // 2
     kb = w_ref.shape[1]
-    xg, wq, proj, qkv = ref["v_xg"], ref["v_wq"], ref["v_proj"], ref["v_qkv"]
-    every, back, attn = ref["v_every"], ref["v_back"], ref["v_attn"]
+    xg, wq, proj, qkv = ref.v_xg, ref.v_wq, ref.v_proj, ref.v_qkv
+    every, back, attn = ref.v_every, ref.v_back, ref.v_attn
     cols = proj.shape[2]
     quarter = cols // 4
-    keep, load = Keep(ref["keep_sem"]), Keep(ref["load_sem"])
-    table = load(tab_ref.at[rows_of(c, span)], ref["v_tab"])
+    keep, load = Keep(ref.keep_sem), Keep(ref.load_sem)
+    table = load(tab_ref.at[rows_of(c, span)], ref.v_tab)
     xg[rows_of(u, rows), :] = x_ref[...]
     peers = [(s, c ^ k, u) for k in (1, 2, 3)]
     greet(all_uly_peers(n) + [(None, peer) for peer in peers] + [(None, (1 - s, c, u))])
 
     def plane(k, src, block, half_rows):
         return PlaneGather(
-            src, block, half_rows, ref["w_send"].at[k], ref["w_recv"].at[k], ref["w_local"].at[k]
+            src, block, half_rows, ref.w_send.at[k], ref.w_recv.at[k], ref.w_local.at[k]
         )
 
     def plane_to(k, src, out):
@@ -1335,13 +1335,13 @@
 
     lower, upper = pl.ds(0, kb // 2), pl.ds(kb // 2, kb // 2)
     w_qkv = plane(0, w_ref, lambda b: wq.at[:, rows_of(b, kb)], kb // 2)
-    w_out = plane_to(1, wo_ref, ref["o_wo"])
-    w_a = plane_to(2, gu_ref.at[0, lower], ref["o_wga"])
-    w_b = plane_to(3, gu_ref.at[0, upper], ref["o_wgb"])
-    w_c = plane_to(4, gu_ref.at[1], ref["o_wgc"])
-    w_d = plane_to(5, down_ref, ref["o_wd"])
-
-    gather = LineGather(n, rows, xg, [ref[f"x_sem{i}"] for i in range(4)])
+    w_out = plane_to(1, wo_ref, ref.o_wo)
+    w_a = plane_to(2, gu_ref.at[0, lower], ref.o_wga)
+    w_b = plane_to(3, gu_ref.at[0, upper], ref.o_wgb)
+    w_c = plane_to(4, gu_ref.at[1], ref.o_wgc)
+    w_d = plane_to(5, down_ref, ref.o_wd)
+
+    gather = LineGather(n, rows, xg, ref.x_sems)
     gather.send(0)
     w_qkv.start()
     gather.wait(0)
@@ -1355,8 +1355,8 @@
     for slot in range(2 if n > 2 else 1, n - 1):
         gather.wait(slot)
     w_qkv.arrive()
-    keep(xg, ref["o_xg"])
-    keep(wq, ref["o_wq"])
+    keep(xg, ref.o_xg)
+    keep(wq, ref.o_wq)
     count, size = tiles(span, 512)
 
     def project(i, carry):
@@ -1370,19 +1370,19 @@
         return carry
 
     lax.fori_loop(0, count, project, 0)
-    keep(proj, ref["o_proj"])
+    keep(proj, ref.o_proj)
     squares = [jnp.sum(proj[i] * proj[i], axis=-1, keepdims=True) for i in range(2)]
     mine = to_rows(*squares)
     zeros = jnp.sum((1 - seg_ref[...]).astype(F32))
     row = lax.broadcasted_iota(jnp.int32, mine.shape, 0)
     mine = jnp.where(row == 2, zeros, mine)
-    total = exchange_rows(n, mine, ref["v_msg"], ref["m_send"], ref["m_recv"])
-    zmsg = ref["v_zmsg"]
+    total = exchange_rows(n, mine, ref.v_msg, ref.m_send, ref.m_recv)
+    zmsg = ref.v_zmsg
     zmsg[pl.ds(c, 1)] = jnp.broadcast_to(total[2:3, :128], (1, 8, 128))
-    inv = ref["v_inv"]
+    inv = ref.v_inv
     inv[...] = lax.rsqrt(to_columns(total) / width + EPS)
     table.wait()
-    cosine, sine = rope_factors(ref["v_tab"][...])
+    cosine, sine = rope_factors(ref.v_tab[...])
     for i in range(2):
         inverse = inv[:, i : i + 1]
         for h in range(cols // HEAD_DIM):
@@ -1393,7 +1393,7 @@
             qkv[group, i, :, inside : inside + HEAD_DIM] = v
 
     copies, arrivals = [], []
-    a_send, a_recv, z_send, z_recv = ref["a_send"], ref["a_recv"], ref["z_send"], ref["z_recv"]
+    a_send, a_recv, z_send, z_recv = ref.a_send, ref.a_recv, ref.z_send, ref.z_recv
     for k, peer in enumerate(peers):
         there = peer[1]
         copy = remote(qkv.at[there], every.at[c], a_send.at[k], a_recv.at[k], peer)
@@ -1404,20 +1404,20 @@
         arrivals.append(remote(every.at[there], every.at[there], a_send.at[k], a_recv.at[k], peer))
         arrivals.append(remote(zmsg.at[there], zmsg.at[there], z_send.at[k], z_recv.at[k], peer))
     every[pl.ds(c, 1)] = qkv[pl.ds(c, 1)]
-    keep(inv, ref["o_inv"])
+    keep(inv, ref.o_inv)
     w_a.middle()
     w_out.corner()
     w_out.arrive()
-    load_o = load_blocks(ref["o_wo"], ref["v_wo"], ref["wo_sem"], 1)
+    load_o = load_blocks(ref.o_wo, ref.v_wo, ref.wo_sem, 1)
     for arrival in arrivals:
         arrival.wait_recv()
     w_b.start()
-    keep(every, ref["o_every"])
+    keep(every, ref.o_every)
     bounds = (zmsg[0] + zmsg[1] + zmsg[2] + zmsg[3]).astype(jnp.int32)
-    ref["v_bound"][...] = bounds
+    ref.v_bound[...] = bounds
     bound = bounds[:1, :1]
-    peaks, sums, acct = ref["v_peaks"], ref["v_sums"], ref["v_acct"]
-    att, lse = ref["v_att"], ref["v_lse"]
+    peaks, sums, acct = ref.v_peaks, ref.v_sums, ref.v_acct
+    att, lse = ref.v_att, ref.v_lse
 
     def attend(k, carry):
         i = c ^ (3 - k)
@@ -1466,27 +1466,27 @@
         return remote(
             back.at[k],
             attn.at[:, :, pl.ds(pl.multiple_of(owner * quarter, quarter), quarter)],
-            ref["b_send"].at[k],
-            ref["b_recv"].at[k],
+            ref.b_send.at[k],
+            ref.b_recv.at[k],
             (s, i, u),
         )
 
     lax.fori_loop(0, 4, attend, 0)
     attn[:, :, pl.ds(pl.multiple_of(c * quarter, quarter), quarter)] = back[3]
-    keep(att, ref["o_att"])
-    keep(lse, ref["o_lse"])
-    keep(ref["v_bound"], ref["o_bound"])
+    keep(att, ref.o_att)
+    keep(lse, ref.o_lse)
+    keep(ref.v_bound, ref.o_bound)
     w_a.corner()
     for k in range(3):
         i = c ^ (3 - k)
         home(k, i, i).wait_recv()
-    keep(attn, ref["o_attn"])
+    keep(attn, ref.o_attn)
     wait_all(load_o)
     w_a.arrive()
-    wg = ref["v_wg"]
-    load(ref["o_wga"], wg.at[0, :, lower])
-
-    wo, part, group = ref["v_wo"], ref["v_part"], ref["v_group"]
+    wg = ref.v_wg
+    load(ref.o_wga, wg.at[0, :, lower])
+
+    wo, part, group = ref.v_wo, ref.v_part, ref.v_group
     halves = Halves(n, rows)
     per_half, chunk_cols = part.shape[0] // 2, part.shape[2]
 
@@ -1501,11 +1501,11 @@
 
         halves.each(h, tile)
 
-    reduce = LineReduce(n, half, part, ref["v_got"], [ref[f"r_sem{i}"] for i in range(4)])
-    g_sems = [ref[f"g_sem{i}"] for i in range(4)]
+    reduce = LineReduce(n, half, part, ref.v_got, ref.r_sems)
+    g_sems = ref.g_sems
     gathers = [LineGather(n, rows, group, g_sems, (h, half)) for h in range(2)]
-    branch, resid = ref["v_branch"], ref["v_resid"]
-    gate, up, hidden = ref["v_gate"], ref["v_up"], ref["v_hidden"]
+    branch, resid = ref.v_branch, ref.v_resid
+    gate, up, hidden = ref.v_gate, ref.v_up, ref.v_hidden
 
     def finish(h):
         where = slice(h * half, (h + 1) * half)
@@ -1533,8 +1533,8 @@
 
         halves.each(h, tile)
         if h == 1:
-            for name, src in (("o_hidden", hidden), ("o_gate", gate), ("o_up", up)):
-                keep(src.at[:, :, lanes], ref[name].at[:, :, lanes])
+            for out, src in ((ref.o_hidden, hidden), (ref.o_gate, gate), (ref.o_up, up)):
+                keep(src.at[:, :, lanes], out.at[:, :, lanes])
 
     def hook(label):
         if label == "started":
@@ -1544,19 +1544,19 @@
             w_b.corner()
         if label == "b1":
             w_b.arrive()
-            load(ref["o_wgb"], wg.at[0, :, upper])
+            load(ref.o_wgb, wg.at[0, :, upper])
         if label == f"b{n - 2}":
             w_c.middle()
         if label == "first":
-            keep(branch, ref["o_branch"])
-            keep(resid, ref["o_resid"])
+            keep(branch, ref.o_branch)
+            keep(resid, ref.o_resid)
             w_c.corner()
             w_d.start()
             w_c.arrive()
-            load(ref["o_wgc"], wg.at[1])
+            load(ref.o_wgc, wg.at[1])
             load.finish((table,))
         if label == f"g{n - 2}":
-            keep(group, ref["o_group"])
+            keep(group, ref.o_group)
 
     reduce_norm_gather(n, reduce, gathers, compute, finish, Consume(ntile, body), hook)
     w_d.middle()
@@ -1578,98 +1578,95 @@
     kb, ff = gu.shape[1:]
     ntile = tiles(ff, 512)[0]
     dma = pltpu.SemaphoreType.DMA
-    ins = {
-        "x": (x, VM),
-        "w": (w, HB),
-        "table": (table, HB),
-        "gain": (gain, VM),
-        "seg": (seg, VM),
-        "wo": (wo, HB),
-        "gu": (gu, HB),
-        "down": (down, HB),
-        "post": (post, VM),
-    }
-    outs = {
-        "o_xg": ((span, width), BF16),
-        "o_wq": ((3, width, cols), BF16),
-        "o_wo": ((8,) + wo.shape, BF16),
-        "o_wga": ((8, kb // 2, ff), BF16),
-        "o_wgb": ((8, kb // 2, ff), BF16),
-        "o_wgc": ((8, kb, ff), BF16),
-        "o_wd": ((8,) + down.shape, BF16),
-        "o_proj": ((2, span, cols), F32),
-        "o_inv": ((span, 128), F32),
-        "o_every": ((4, 3, span, quarter), BF16),
-        "o_att": ((4, quarter, span), F32),
-        "o_lse": ((4, quarter // HEAD_DIM, 8, span), F32),
-        "o_bound": ((8, 128), jnp.int32),
-        "o_attn": ((n, rows, cols), BF16),
-        "o_branch": ((2, half, width), F32),
-        "o_resid": ((2, half, width), F32),
-        "o_group": ((n, rows, width), BF16),
-        "o_gate": ((n, rows, ff), BF16),
-        "o_up": ((n, rows, ff), BF16),
-        "o_hidden": ((n, rows, ff), BF16),
-    }
-    buffers = {
-        "v_xg": ((span, width), BF16),
-        "v_wq": ((3, width, cols), BF16),
-        "v_tab": ((span, 128), F32),
-        "v_proj": ((2, span, cols), F32),
-        "v_inv": ((span, 128), F32),
-        "v_msg": ((n, 8, span), F32),
-        "v_qkv": ((4, 3, span, quarter), BF16),
-        "v_every": ((4, 3, span, quarter), BF16),
-        "v_back": ((4, n, rows, quarter), BF16),
-        "v_zmsg": ((4, 8, 128), F32),
-        "v_bound": ((8, 128), jnp.int32),
-        "v_peaks": ((8, span), F32),
-        "v_sums": ((8, span), F32),
-        "v_acct": ((HEAD_DIM, span), F32),
-        "v_att": ((4, quarter, span), F32),
-        "v_lse": ((4, quarter // HEAD_DIM, 8, span), F32),
-        "v_attn": ((n, rows, cols), BF16),
-        "v_wo": ((cols, width), BF16),
-        "v_wg": ((2, 8, kb, ff), BF16),
-        "v_group": ((n, rows, width), BF16),
-        "v_branch": ((2, half, width), F32),
-        "v_resid": ((2, half, width), F32),
-        "v_gate": ((n, rows, ff), BF16),
-        "v_up": ((n, rows, ff), BF16),
-        "v_hidden": ((n, rows, ff), BF16),
-        "v_part": ((4, n * half, width // 2), BF16),
-        "v_got": ((4, (n + 1) * half, width // 2), BF16),
-    }
-    sems = {
-        "keep_sem": (12 + 3 * ntile,),
-        "load_sem": (4,),
-        "wo_sem": (8,),
-        "w_send": (6, 9),
-        "w_recv": (6, 9),
-        "w_local": (6,),
-        "m_send": (n - 1,),
-        "m_recv": (n - 1,),
-    }
-    for name in ("a_send", "a_recv", "z_send", "z_recv", "b_send", "b_recv"):
-        sems[name] = (3,)
-    for i in range(4):
-        sems[f"x_sem{i}"] = (n - 1,)
-        sems[f"r_sem{i}"] = (n - 1, 4)
-        sems[f"g_sem{i}"] = (n - 1, 2)
-    names = [*ins, *outs, *buffers, *sems]
+    ins = dict(
+        x=(x, VM),
+        w=(w, HB),
+        table=(table, HB),
+        gain=(gain, VM),
+        seg=(seg, VM),
+        wo=(wo, HB),
+        gu=(gu, HB),
+        down=(down, HB),
+        post=(post, VM),
+    )
+    outs = dict(
+        o_xg=((span, width), BF16),
+        o_wq=((3, width, cols), BF16),
+        o_wo=((8,) + wo.shape, BF16),
+        o_wga=((8, kb // 2, ff), BF16),
+        o_wgb=((8, kb // 2, ff), BF16),
+        o_wgc=((8, kb, ff), BF16),
+        o_wd=((8,) + down.shape, BF16),
+        o_proj=((2, span, cols), F32),
+        o_inv=((span, 128), F32),
+        o_every=((4, 3, span, quarter), BF16),
+        o_att=((4, quarter, span), F32),
+        o_lse=((4, quarter // HEAD_DIM, 8, span), F32),
+        o_bound=((8, 128), jnp.int32),
+        o_attn=((n, rows, cols), BF16),
+        o_branch=((2, half, width), F32),
+        o_resid=((2, half, width), F32),
+        o_group=((n, rows, width), BF16),
+        o_gate=((n, rows, ff), BF16),
+        o_up=((n, rows, ff), BF16),
+        o_hidden=((n, rows, ff), BF16),
+    )
+    buffers = dict(
+        v_xg=((span, width), BF16),
+        v_wq=((3, width, cols), BF16),
+        v_tab=((span, 128), F32),
+        v_proj=((2, span, cols), F32),
+        v_inv=((span, 128), F32),
+        v_msg=((n, 8, span), F32),
+        v_qkv=((4, 3, span, quarter), BF16),
+        v_every=((4, 3, span, quarter), BF16),
+        v_back=((4, n, rows, quarter), BF16),
+        v_zmsg=((4, 8, 128), F32),
+        v_bound=((8, 128), jnp.int32),
+        v_peaks=((8, span), F32),
+        v_sums=((8, span), F32),
+        v_acct=((HEAD_DIM, span), F32),
+        v_att=((4, quarter, span), F32),
+        v_lse=((4, quarter // HEAD_DIM, 8, span), F32),
+        v_attn=((n, rows, cols), BF16),
+        v_wo=((cols, width), BF16),
+        v_wg=((2, 8, kb, ff), BF16),
+        v_group=((n, rows, width), BF16),
+        v_branch=((2, half, width), F32),
+        v_resid=((2, half, width), F32),
+        v_gate=((n, rows, ff), BF16),
+        v_up=((n, rows, ff), BF16),
+        v_hidden=((n, rows, ff), BF16),
+        v_part=((4, n * half, width // 2), BF16),
+        v_got=((4, (n + 1) * half, width // 2), BF16),
+    )
+    sems = dict(
+        keep_sem=(12 + 3 * ntile,),
+        load_sem=(4,),
+        wo_sem=(8,),
+        w_send=(6, 9),
+        w_recv=(6, 9),
+        w_local=(6,),
+        m_send=(n - 1,),
+        m_recv=(n - 1,),
+    )
+    three, fours = (3,), dict(x_sems=(n - 1,), r_sems=(n - 1, 4), g_sems=(n - 1, 2))
+    sems.update(a_send=three, a_recv=three, z_send=three, z_recv=three, b_send=three, b_recv=three)
+    names = [*ins, *outs, *buffers, *sems, *fours]
     results = pl.pallas_call(
         functools.partial(forward_kernel, n, names),
         out_shape=[shape(*out) for out in outs.values()],
         in_specs=[spec for value, spec in ins.values()],
         out_specs=[HB] * len(outs),
         scratch_shapes=[pltpu.VMEM(*buffer) for buffer in buffers.values()]
-        + [dma(dims) for dims in sems.values()],
+        + [dma(dims) for dims in sems.values()]
+        + [(dma(dims),) * 4 for dims in fours.values()],
         compiler_params=pltpu.CompilerParams(
             collective_id=10, has_side_effects=True, vmem_limit_bytes=VMEM_LIMIT
         ),
         name="forward",
     )(*[value for value, spec in ins.values()])
-    return dict(zip(outs, results))
+    return SimpleNamespace(**dict(zip(outs, results)))
 
 
 def load_blocks(src, dst, sem, axis):
@@ -2752,25 +2749,23 @@
 
 
 def backward_kernel(n, names, *refs):
-    ref = dict(zip(names, refs))
+    ref = SimpleNamespace(**dict(zip(names, refs)))
     s, c, u = where_am_i()
-    cot_ref, gain_ref, qk_gain_ref = ref["cot"], ref["post"], ref["gain"]
+    cot_ref, gain_ref, qk_gain_ref = ref.cot, ref.post, ref.gain
     rows, width = cot_ref.shape
     span = n * rows
-    weights, dgu, dgu_s = ref["v_weights"], ref["v_dgu"], ref["v_dgu_s"]
-    hidden, hidden_s, dmlp, dmlp_s = [
-        ref[f"v_{k}"] for k in ("hidden", "hidden_s", "dmlp", "dmlp_s")
-    ]
-    resid, resid_s, branch, attn = [ref[f"v_{k}"] for k in ("resid", "resid_s", "branch", "attn")]
-    part, group, dresid = ref["v_part"], ref["v_group"], ref["v_dresid"]
-    load = Keep(ref["load_sem"])
+    weights, dgu, dgu_s = ref.v_weights, ref.v_dgu, ref.v_dgu_s
+    hidden, hidden_s, dmlp, dmlp_s = ref.v_hidden, ref.v_hidden_s, ref.v_dmlp, ref.v_dmlp_s
+    resid, resid_s, branch, attn = ref.v_resid, ref.v_resid_s, ref.v_branch, ref.v_attn
+    part, group, dresid = ref.v_part, ref.v_group, ref.v_dresid
+    load = Keep(ref.load_sem)
     chunks, chunk_cols = part.shape[0], part.shape[2]
-    kb = ref["wgc"].shape[1]
+    kb = ref.wgc.shape[1]
     per_chunk = chunk_cols // kb
     lower, upper = kb // 2, kb // 2
 
 
-    rows_g = ref["v_ring"].shape[3]
+    rows_g = ref.v_ring.shape[3]
     rows_d = cols_g = 2 * rows_g
     tiles_g = dgu.shape[2] // cols_g
     n_d, n_g = hidden.shape[1] // rows_d, 2 * tiles_g
@@ -2789,16 +2784,16 @@
             at = slot * 2 * chunk_cols + b * kb
             for k, (src, first, size) in enumerate(
                 (
-                    (ref["wga"], at, lower),
-                    (ref["wgb"], at + lower, upper),
-                    (ref["wgc"], at + chunk_cols, kb),
+                    (ref.wga, at, lower),
+                    (ref.wgb, at + lower, upper),
+                    (ref.wgc, at + chunk_cols, kb),
                 )
             ):
                 copies.append(
                     pltpu.make_async_copy(
                         src.at[block],
                         weights.at[pl.ds(first, size)],
-                        ref["chunk_sem"].at[slot, 3 * b + k],
+                        ref.chunk_sem.at[slot, 3 * b + k],
                     )
                 )
         return copies
@@ -2807,30 +2802,30 @@
         for copy in load_chunk(chunk):
             copy.start()
 
-    load_dgu = load(ref["dgu"], dgu)
+    load_dgu = load(ref.dgu, dgu)
     start_chunk(0)
     load_d = [
-        load(ref["hidden"], hidden),
-        load(half_columns(ref["dmlp"], s), dmlp),
-        load(ref["dmlp_s"], dmlp_s),
+        load(ref.hidden, hidden),
+        load(half_columns(ref.dmlp, s), dmlp),
+        load(ref.dmlp_s, dmlp_s),
     ]
-    stream_d = Stream(hidden_s, ref["hs_sem"], lambda p: hidden_tile(ref["hidden_s"], p), n_d)
+    stream_d = Stream(hidden_s, ref.hs_sem, lambda p: hidden_tile(ref.hidden_s, p), n_d)
     start_chunk(1)
     load_g = [
-        load(half_columns(ref["resid"], s), resid),
-        load(ref["resid_s"], resid_s),
-        load(ref["branch"], branch),
-        load(ref["attn"], attn),
+        load(half_columns(ref.resid, s), resid),
+        load(ref.resid_s, resid_s),
+        load(ref.branch, branch),
+        load(ref.attn, attn),
     ]
-    stream_g = Stream(dgu_s, ref["ds_sem"], lambda p: gate_tile(ref["dgu_s"], p), n_g)
+    stream_g = Stream(dgu_s, ref.ds_sem, lambda p: gate_tile(ref.dgu_s, p), n_g)
     wo_row = 4 * chunk_cols
-    wo_cols = ref["wo"].shape[1]
+    wo_cols = ref.wo.shape[1]
     wo_view = weights.at[pl.ds(wo_row, wo_cols)]
-    load_o = load_blocks(ref["wo"], wo_view, ref["wo_sem"], 1)
+    load_o = load_blocks(ref.wo, wo_view, ref.wo_sem, 1)
     peers = [(s, c ^ k, u) for k in (1, 2, 3)]
     greet(all_uly_peers(n) + [(None, peer) for peer in peers] + [(None, (1 - s, c, u))])
-    sibling = Sibling(ref["s_send"], ref["s_recv"])
-    sibling.start(half_columns(ref["xg"], 1 - s), ref["v_xs_s"])
+    sibling = Sibling(ref.s_send, ref.s_recv)
+    sibling.start(half_columns(ref.xg, 1 - s), ref.v_xs_s)
     load_dgu.wait()
     count, size = tiles(span, 512)
 
@@ -2852,18 +2847,17 @@
 
     def place(index, piece, half):
         if piece < n_d or piece == n_d + n_g:
-            name, first = ("down", piece * rows_d) if piece < n_d else ("out", 0)
-            rows = pl.ds(first + half * rows_g, rows_g)
-            return ref[f"o_{name}{index}"].at[rows]
+            outs, first = (ref.o_down, piece * rows_d) if piece < n_d else (ref.o_out, 0)
+            return outs[index].at[pl.ds(first + half * rows_g, rows_g)]
         if piece < n_d + n_g:
             ci, tile = divmod(piece - n_d, tiles_g)
             lanes = pl.ds(tile * cols_g + half * rows_g, rows_g)
-            return ref[f"o_gate{index}"].at[ci, :, lanes]
+            return ref.o_gate[index].at[ci, :, lanes]
         lanes = pl.ds(half * rows_g, rows_g)
-        return ref[f"o_qkv{index}"].at[piece - n_d - n_g - 1, :, lanes]
+        return ref.o_qkv[index].at[piece - n_d - n_g - 1, :, lanes]
 
     plane = PiecePlane(
-        ref["v_ring"], ref["v_got_p"], place, ref["p_send"], ref["p_recv"], ref["p_local"]
+        ref.v_ring, ref.v_got_p, place, ref.p_send, ref.p_recv, ref.p_local
     )
     def down_piece(out, piece):
         stream_d.wait(piece)
@@ -2880,7 +2874,7 @@
 
     def out_piece(out, piece):
         own = (attn, half_columns(group, s))
-        wide_blocks(own, (ref["v_attn_s"], ref["v_dbranch_s"]), out)
+        wide_blocks(own, (ref.v_attn_s, ref.v_dbranch_s), out)
 
     cols = attn.shape[1]
     dproj = hidden.at[:, pl.ds(0, 3 * cols)]
@@ -2888,7 +2882,7 @@
     def qkv_piece(out, piece):
         lanes = pl.ds((piece - n_d - n_g - 1) * cols, cols)
         own = (dmlp, hidden.at[:, lanes])
-        tall_blocks(own, (ref["v_xs_s"], ref["v_dproj_s"].at[:, lanes]), out)
+        tall_blocks(own, (ref.v_xs_s, ref.v_dproj_s.at[:, lanes]), out)
 
     kinds = [down_piece] * n_d + [gate_piece] * n_g + [out_piece] + [qkv_piece] * 3
     pieces = Pieces([(plane, p, kind) for p, kind in enumerate(kinds)], AHEAD)
@@ -2905,28 +2899,28 @@
             wait_all(load_g)
         pieces.step()
 
-    sem_r = [ref[f"r_sem{i}"] for i in range(4)]
-    sem_b = [ref[f"b_sem{i}"] for i in range(4)]
-    LineReduce(n, rows, part, ref["v_got"], sem_r).run(compute_and_piece, dresid, reduce_hook)
+    sem_r = ref.r_sems
+    sem_b = ref.b_sems
+    LineReduce(n, rows, part, ref.v_got, sem_r).run(compute_and_piece, dresid, reduce_hook)
     d_resid = dresid[...] + cot_ref[...].astype(F32)
     dresid[...] = d_resid
     values = branch[...]
     inverse = inverse_rms(values)
     d_branch = norm_back(values, inverse, d_resid * gain_ref[0:1, :], width)
     group[rows_of(u, rows), :] = d_branch.astype(BF16)
-    gather = LineGather(n, rows, group, [ref[f"g_sem{i}"] for i in range(4)])
+    gather = LineGather(n, rows, group, ref.g_sems)
     gather.send(0)
     gain_attn = jnp.sum(d_resid * values * inverse, axis=0, keepdims=True)
-    ref["v_gattn"][...] = gain_attn
+    ref.v_gattn[...] = gain_attn
     quarter = cols // 4
     load_a = [
-        load(ref["every"].at[i, t], weights.at[pl.ds(0, span), pl.ds((3 * i + t) * quarter, quarter)])
+        load(ref.every.at[i, t], weights.at[pl.ds(0, span), pl.ds((3 * i + t) * quarter, quarter)])
         for i in range(4)
         for t in range(3)
     ]
-    att, proj, tab = ref["v_att"], ref["v_proj"], ref["v_tab"]
-    load_a.append(load(ref["att"], att))
-    load_p = [load(ref["proj"], proj), load(ref["table"].at[rows_of(c, span)], tab)]
+    att, proj, tab = ref.v_att, ref.v_proj, ref.v_tab
+    load_a.append(load(ref.att, att))
+    load_p = [load(ref.proj, proj), load(ref.table.at[rows_of(c, span)], tab)]
     pieces.step()
 
     def gather_hook(slot):
@@ -2937,7 +2931,7 @@
 
     gather.run(gather_hook)
     wait_all(load_o)
-    dattn, d_out = ref["v_dattn"], ref["v_d_out"]
+    dattn, d_out = ref.v_dattn, ref.v_d_out
 
     def tile(j, carry):
         where = pl.ds(pl.multiple_of(j * size, size), size)
@@ -2948,19 +2942,19 @@
 
     lax.fori_loop(0, count, tile, 0)
 
-    a_send, a_recv, h_send, h_recv = ref["a_send"], ref["a_recv"], ref["h_send"], ref["h_recv"]
+    a_send, a_recv, h_send, h_recv = ref.a_send, ref.a_recv, ref.h_send, ref.h_recv
     copies = []
     for k, peer in enumerate(peers):
         copy = remote(dattn.at[peer[1]], d_out.at[c], a_send.at[k], a_recv.at[k], peer)
         copy.start()
         copies.append(copy)
-    sibling.start(attn, ref["v_attn_s"])
-    sibling.start(half_columns(group, 1 - s), ref["v_dbranch_s"])
+    sibling.start(attn, ref.v_attn_s)
+    sibling.start(half_columns(group, 1 - s), ref.v_dbranch_s)
     d_out[pl.ds(c, 1)] = dattn[pl.ds(c, 1)]
-    dq, acc, delta, got = ref["v_dq"], ref["v_acc"], ref["v_delta"], ref["v_home"]
-    lse_ref = ref["lse"]
+    dq, acc, delta, got = ref.v_dq, ref.v_acc, ref.v_delta, ref.v_home
+    lse_ref = ref.lse
     dq[...] = jnp.zeros_like(dq)
-    bound = ref["bound"][:1, :1]
+    bound = ref.bound[:1, :1]
     scale = HEAD_DIM ** (-0.5)
     heads = quarter // HEAD_DIM
     wait_all(load_a)
@@ -3022,16 +3016,16 @@
 
     lax.fori_loop(0, 4, step, 0)
     load_q = [
-        load(ref["wq"].at[i], weights.at[pl.ds(0, width), pl.ds(i * cols, cols)]) for i in range(3)
+        load(ref.wq.at[i], weights.at[pl.ds(0, width), pl.ds(i * cols, cols)]) for i in range(3)
     ]
-    load_x = load(half_columns(ref["xg"], s), dmlp)
+    load_x = load(half_columns(ref.xg, s), dmlp)
     got[pl.ds(c, 1)] = going(c)[...][None]
     wait_all(load_p)
     for k in (1, 2, 3):
         j = c ^ k
         remote(got.at[j], got.at[j], h_send.at[c], h_recv.at[j], (s, j, u)).wait_recv()
     pieces.step()
-    kept, inv_ref = (dq, ref["v_dk"]), ref["inv"]
+    kept, inv_ref = (dq, ref.v_dk), ref.inv
     for j in range(4):
         hidden[:, 2 * cols + j * quarter : 2 * cols + (j + 1) * quarter] = got[
             j, :, 2 * quarter : 3 * quarter
@@ -3042,14 +3036,14 @@
         first = i * quarter + inside * HEAD_DIM
         return got[group, :, first : first + HEAD_DIM].astype(F32)
 
-    gcols = ref["v_gcols"]
+    gcols = ref.v_gcols
 
     def store(i, h, values):
         group, inside = divmod(h, heads)
         kept[i][group, :, inside * HEAD_DIM : (inside + 1) * HEAD_DIM] = values
 
     dots = norms_back(source, store, proj, inv_ref, qk_gain_ref, tab, gcols)
-    total = exchange_rows(n, dots, ref["v_msg"], ref["m_send"], ref["m_recv"])
+    total = exchange_rows(n, dots, ref.v_msg, ref.m_send, ref.m_recv)
     means = to_columns(total) / width
     for i in range(2):
         inverse = inv_ref[:, i : i + 1]
@@ -3059,13 +3053,13 @@
             hidden[:, i * cols + j * quarter : i * cols + (j + 1) * quarter] = (
                 inverse * kept[i][j] - proj[i, :, lanes] * factor
             ).astype(BF16)
-    sibling.start(dproj, ref["v_dproj_s"])
+    sibling.start(dproj, ref.v_dproj_s)
     gains = GainSum(
         n,
-        [ref[f"v_sum{i}"] for i in range(4)],
-        (ref["v_send"], ref["v_recv"], ref["n_send"], ref["n_recv"]),
+        ref.v_sums,
+        (ref.v_send, ref.v_recv, ref.n_send, ref.n_recv),
     )
-    gains.start(gcols, ref["v_gattn"], ref["gmlp"])
+    gains.start(gcols, ref.v_gattn, ref.gmlp)
     wait_all(load_q)
 
     def compute_input(chunk):
@@ -3096,10 +3090,10 @@
             gains.over_uly()
         pieces.step()
 
-    LineReduce(n, rows, part, ref["v_got"], sem_b).run(compute_input, branch, input_hook)
-    ref["o_input"][...] = (dresid[...] + branch[...]).astype(BF16)
+    LineReduce(n, rows, part, ref.v_got, sem_b).run(compute_input, branch, input_hook)
+    ref.o_input[...] = (dresid[...] + branch[...]).astype(BF16)
     pieces.finish()
-    gains.finish(ref["o_gain"])
+    gains.finish(ref.o_gain)
     plane.finish(len(kinds))
     sibling.finish()
     for j in range(4):
@@ -3113,93 +3107,91 @@
 
 
 def backward(n, ins):
-    rows, width = ins["cot"][0].shape
-    span, ff = n * rows, ins["hidden"][0].shape[1]
-    cols = ins["attn"][0].shape[1]
+    given = SimpleNamespace(**ins)
+    rows, width = given.cot[0].shape
+    span, ff = n * rows, given.hidden[0].shape[1]
+    cols = given.attn[0].shape[1]
     quarter = cols // 4
-    kb, kc = width // 8, ins["wo"][0].shape[2]
+    kb, kc = width // 8, given.wo[0].shape[2]
     n_d, size = tiles(ff, 512)
     dma = pltpu.SemaphoreType.DMA
-    outs = {"o_input": ((rows, width), BF16), "o_gain": ((4, width // 8), F32)}
-    for i in range(3):
-        outs[f"o_down{i}"] = ((ff, kc), BF16)
-        outs[f"o_gate{i}"] = ((2, kb, ff), BF16)
-        outs[f"o_out{i}"] = ((cols, kc), BF16)
-        outs[f"o_qkv{i}"] = ((3, kb, cols), BF16)
-    buffers = {
-        "v_weights": ((width + cols, width), BF16),
-        "v_dgu": ((2, span, ff), BF16),
-        "v_dgu_s": ((3, span, size), BF16),
-        "v_hidden": ((span, ff), BF16),
-        "v_hidden_s": ((2, span, size), BF16),
-        "v_dmlp": ((span, width // 2), BF16),
-        "v_dmlp_s": ((span, width // 2), BF16),
-        "v_resid": ((span, width // 2), BF16),
-        "v_resid_s": ((span, width // 2), BF16),
-        "v_branch": ((rows, width), F32),
-        "v_attn": ((span, cols), BF16),
-        "v_dresid": ((rows, width), F32),
-        "v_group": ((span, width), BF16),
-        "v_part": ((CHUNKS, span, width // CHUNKS), BF16),
-        "v_got": ((CHUNKS, span + rows, width // CHUNKS), BF16),
-        "v_ring": ((AHEAD + 1, 4, 2, kb, kb), BF16),
-        "v_got_p": ((3 * n_d + 4, 2, kb, kb), BF16),
-        "v_gattn": ((1, width), F32),
-        "v_att": ((4, quarter, span), F32),
-        "v_proj": ((2, span, cols), F32),
-        "v_tab": ((span, 128), F32),
-        "v_dattn": ((4, span, quarter), BF16),
-        "v_d_out": ((4, span, quarter), BF16),
-        "v_dq": ((4, span, quarter), F32),
-        "v_acc": ((2, span, quarter), F32),
-        "v_delta": ((4, quarter // HEAD_DIM, 8, span), F32),
-        "v_home": ((4, span, 3 * quarter), BF16),
-        "v_dk": ((4, span, quarter), F32),
-        "v_gcols": ((2, cols), F32),
-        "v_msg": ((n, 8, span), F32),
-        "v_xs_s": ((span, width // 2), BF16),
-        "v_attn_s": ((span, cols), BF16),
-        "v_dbranch_s": ((span, width // 2), BF16),
-        "v_dproj_s": ((span, 3 * cols), BF16),
-        "v_sum0": ((2, 8, width // 2), F32),
-        "v_sum1": ((8, width // 2), F32),
-        "v_sum2": ((4, 8, width // 8), F32),
-        "v_sum3": ((3 + n, 8, width // 8), F32),
-    }
-    sems = {
-        "load_sem": (32,),
-        "chunk_sem": (2, 3 * (width // CHUNKS // kb)),
-        "wo_sem": (8,),
-        "hs_sem": (2,),
-        "ds_sem": (3,),
-        "p_send": (3 * n_d + 4, 6),
-        "p_recv": (3 * n_d + 4, 6),
-        "p_local": (3 * n_d + 4, 2),
-        "a_send": (3,),
-        "a_recv": (3,),
-    }
-    for name in ("s_send", "s_recv", "h_send", "h_recv", "v_send", "v_recv"):
-        sems[name] = (4,)
-    for name in ("m_send", "m_recv", "n_send", "n_recv"):
-        sems[name] = (n - 1,)
-    for i in range(4):
-        sems[f"r_sem{i}"] = (n - 1, CHUNKS)
-        sems[f"b_sem{i}"] = (n - 1, CHUNKS)
-        sems[f"g_sem{i}"] = (n - 1,)
-    names = [*ins, *outs, *buffers, *sems]
+    outs = dict(
+        o_input=shape((rows, width), BF16),
+        o_gain=shape((4, width // 8), F32),
+        o_down=(shape((ff, kc), BF16),) * 3,
+        o_gate=(shape((2, kb, ff), BF16),) * 3,
+        o_out=(shape((cols, kc), BF16),) * 3,
+        o_qkv=(shape((3, kb, cols), BF16),) * 3,
+    )
+    buffers = dict(
+        v_weights=((width + cols, width), BF16),
+        v_dgu=((2, span, ff), BF16),
+        v_dgu_s=((3, span, size), BF16),
+        v_hidden=((span, ff), BF16),
+        v_hidden_s=((2, span, size), BF16),
+        v_dmlp=((span, width // 2), BF16),
+        v_dmlp_s=((span, width // 2), BF16),
+        v_resid=((span, width // 2), BF16),
+        v_resid_s=((span, width // 2), BF16),
+        v_branch=((rows, width), F32),
+        v_attn=((span, cols), BF16),
+        v_dresid=((rows, width), F32),
+        v_group=((span, width), BF16),
+        v_part=((CHUNKS, span, width // CHUNKS), BF16),
+        v_got=((CHUNKS, span + rows, width // CHUNKS), BF16),
+        v_ring=((AHEAD + 1, 4, 2, kb, kb), BF16),
+        v_got_p=((3 * n_d + 4, 2, kb, kb), BF16),
+        v_gattn=((1, width), F32),
+        v_att=((4, quarter, span), F32),
+        v_proj=((2, span, cols), F32),
+        v_tab=((span, 128), F32),
+        v_dattn=((4, span, quarter), BF16),
+        v_d_out=((4, span, quarter), BF16),
+        v_dq=((4, span, quarter), F32),
+        v_acc=((2, span, quarter), F32),
+        v_delta=((4, quarter // HEAD_DIM, 8, span), F32),
+        v_home=((4, span, 3 * quarter), BF16),
+        v_dk=((4, span, quarter), F32),
+        v_gcols=((2, cols), F32),
+        v_msg=((n, 8, span), F32),
+        v_xs_s=((span, width // 2), BF16),
+        v_attn_s=((span, cols), BF16),
+        v_dbranch_s=((span, width // 2), BF16),
+        v_dproj_s=((span, 3 * cols), BF16),
+    )
+    sums = tuple(pltpu.VMEM(dims, F32) for dims in (((2, 8, width // 2), F32)[0], ((8, width // 2), F32)[0], ((4, 8, width // 8), F32)[0], ((3 + n, 8, width // 8), F32)[0]))
+    sems = dict(
+        load_sem=(32,),
+        chunk_sem=(2, 3 * (width // CHUNKS // kb)),
+        wo_sem=(8,),
+        hs_sem=(2,),
+        ds_sem=(3,),
+        p_send=(3 * n_d + 4, 6),
+        p_recv=(3 * n_d + 4, 6),
+        p_local=(3 * n_d + 4, 2),
+        a_send=(3,),
+        a_recv=(3,),
+    )
+    four, line = (4,), (n - 1,)
+    sems.update(s_send=four, s_recv=four, h_send=four, h_recv=four, v_send=four, v_recv=four)
+    sems.update(m_send=line, m_recv=line, n_send=line, n_recv=line)
+    fours = dict(r_sems=(n - 1, CHUNKS), b_sems=(n - 1, CHUNKS), g_sems=line)
+    tuples = dict(v_sums=sums, **{name: (dma(dims),) * 4 for name, dims in fours.items()})
+    names = [*ins, *outs, *buffers, *sems, *tuples]
     results = pl.pallas_call(
         functools.partial(backward_kernel, n, names),
-        out_shape=[shape(*out) for out in outs.values()],
+        out_shape=list(outs.values()),
         in_specs=[spec for value, spec in ins.values()],
-        out_specs=[VM, VM] + [HB] * 12,
+        out_specs=[VM, VM] + [(HB,) * 3] * 4,
         scratch_shapes=[pltpu.VMEM(*buffer) for buffer in buffers.values()]
-        + [dma(dims) for dims in sems.values()],
+        + [dma(dims) for dims in sems.values()]
+        + list(tuples.values()),
         compiler_params=pltpu.CompilerParams(
             collective_id=11, has_side_effects=True, vmem_limit_bytes=63 * 1024 * 1024
         ),
         name="backward",
     )(*[value for value, spec in ins.values()])
-    return dict(zip(outs, results))
+    return SimpleNamespace(**dict(zip(outs, results)))
 
 
 def rope_table(length):
@@ -3240,13 +3232,13 @@
             down_weight,
             post_gain,
         )
-        group_x, wq, wo, proj, inv = [o[f"o_{k}"] for k in ("xg", "wq", "wo", "proj", "inv")]
-        wga, wgb, wgc, wd = [o[f"o_{k}"] for k in ("wga", "wgb", "wgc", "wd")]
-        att, lse, bound, attn = [o[f"o_{k}"] for k in ("att", "lse", "bound", "attn")]
-        branch, resid, group_resid = [o[f"o_{k}"] for k in ("branch", "resid", "group")]
-        gate, up, hidden = [o[f"o_{k}"] for k in ("gate", "up", "hidden")]
+        group_x, wq, wo, proj, inv = o.o_xg, o.o_wq, o.o_wo, o.o_proj, o.o_inv
+        wga, wgb, wgc, wd = o.o_wga, o.o_wgb, o.o_wgc, o.o_wd
+        att, lse, bound, attn = o.o_att, o.o_lse, o.o_bound, o.o_attn
+        branch, resid, group_resid = o.o_branch, o.o_resid, o.o_group
+        gate, up, hidden = o.o_gate, o.o_up, o.o_hidden
         attn = attn.reshape(group_x.shape[0], -1)
-        seen = (o["o_every"],)
+        seen = (o.o_every,)
     else:
         group_x, wq, wo, wga, proj, qkv, inv, zero = project(
             n, x, qkv_weight, table, qk_gain, segment_ids, out_weight, gate_up
@@ -3268,40 +3260,38 @@
     if spread_heads(qkv_weight.shape[2]):
         o = backward(
             n,
-            {
-                "dgu": (dgu, HB),
-                "dgu_s": (dgu_s, HB),
-                "wga": (wga, HB),
-                "wgb": (wgb, HB),
-                "wgc": (wgc, HB),
-                "cot": (cot, VM),
-                "branch": (branch, HB),
-                "post": (post_gain, VM),
-                "gain": (qk_gain, VM),
-                "wo": (wo, HB),
-                "hidden": (hidden, HB),
-                "hidden_s": (hidden_s, HB),
-                "dmlp": (group_dmlp, HB),
-                "dmlp_s": (dmlp_s, HB),
-                "resid": (group_resid, HB),
-                "resid_s": (resid_s, HB),
-                "every": (seen[0], HB),
-                "att": (att, HB),
-                "lse": (lse, VM),
-                "bound": (bound, VM),
-                "attn": (attn, HB),
-                "proj": (proj, HB),
-                "inv": (inv, VM),
-                "table": (table, HB),
-                "wq": (wq, HB),
-                "xg": (group_x, HB),
-                "gmlp": (gain_mlp, VM),
-            },
+            dict(
+                dgu=(dgu, HB),
+                dgu_s=(dgu_s, HB),
+                wga=(wga, HB),
+                wgb=(wgb, HB),
+                wgc=(wgc, HB),
+                cot=(cot, VM),
+                branch=(branch, HB),
+                post=(post_gain, VM),
+                gain=(qk_gain, VM),
+                wo=(wo, HB),
+                hidden=(hidden, HB),
+                hidden_s=(hidden_s, HB),
+                dmlp=(group_dmlp, HB),
+                dmlp_s=(dmlp_s, HB),
+                resid=(group_resid, HB),
+                resid_s=(resid_s, HB),
+                every=(seen[0], HB),
+                att=(att, HB),
+                lse=(lse, VM),
+                bound=(bound, VM),
+                attn=(attn, HB),
+                proj=(proj, HB),
+                inv=(inv, VM),
+                table=(table, HB),
+                wq=(wq, HB),
+                xg=(group_x, HB),
+                gmlp=(gain_mlp, VM),
+            ),
         )
-        input_grad, gain_part = o["o_input"], o["o_gain"]
-        qkv_grads, out_grads, gate_grads, down_grads = [
-            [o[f"o_{k}{i}"] for i in range(3)] for k in ("qkv", "out", "gate", "down")
-        ]
+        input_grad, gain_part = o.o_input, o.o_gain
+        qkv_grads, out_grads, gate_grads, down_grads = o.o_qkv, o.o_out, o.o_gate, o.o_down
     else:
         d_resid, group_dbranch, d_attn, gain_attn, *grads = mlp_back(
             n,

time: 475 us -> 475 us (level)
  no operation moved by 1% of the time
where the time goes in v6:
time: 475 us; the launch traced here: 470 us
  Pallas kernels  455 us (96%)
  other arithmetic  10.2 us (2%)
    pallas_call x1, Pallas kernels, backward(): pl.pallas_call(functools.partial(backward_kernel, n, names), out_shape=li...  192 us
    pallas_call x1, Pallas kernels, forward(): pl.pallas_call(functools.partial(forward_kernel, n, names), out_shape=[sh...  185 us
    pallas_call x1, Pallas kernels, mlp_out(): pl.pallas_call(functools.partial(mlp_out_kernel, n), out_shape=(shape((ro...  77.8 us
    add x4, other arithmetic, total(): return parts[0].astype(F32) + parts[1].astype(F32) + parts[2].astype(F32)  10.2 us

profile of v6, /device:TPU:0, one launch (start us, length us, event | category | flops | bytes accessed | tf_op | source)
XLA Modules:
  0.0 469.7 jit_solution(9847941602455523217)
XLA Ops:
  0.6 185.4 %forward.1 = (bf16[512,2048]{1,0:T(8,128)(2,1)}, bf16[3,2048,512]{2,1,0:T(8,128)(2,1)}, bf16[8,512,256]{2,1,0:T(8,128)(2,1)}, bf16[8,128,2048]{2,1,0:T(8,128)(2,...) custom-call(bf16[128,2048]{1,0:T(8,128)(2,1)} %bitcast.28, ...), custom_call_target="tpu_custom_call" | custom-call | tf_op jit(solution)/shard_map/forward/pallas_call | solution.py:1656
  186.0 77.8 %mlp_out.1 = (bf16[128,2048]{1,0:T(8,128)(2,1)}, bf16[4,128,2048]{2,1,0:T(8,128)(2,1)}, bf16[2,4,128,2048]{3,2,1,0:T(8,128)(2,1)}, f32[1,2048]{1,0:T(1,128)}, bf...) custom-call(bf16[4,128,2048]{2,1,0:T(8,128)(2,1)} %get-tuple-element, ...), custom_call_target="tpu_custom_call" | custom-call | tf_op jit(solution)/shard_map/mlp_out/pallas_call | solution.py:2022
  263.8 191.7 %backward.1 = (bf16[128,2048]{1,0:T(8,128)(2,1)}, f32[4,256]{1,0:T(4,128)}, bf16[2048,256]{1,0:T(8,128)(2,1)}, bf16[2048,256]{1,0:T(8,128)(2,1)}, bf16[2048,256]...) custom-call(bf16[2,512,2048]{2,1,0:T(8,128)(2,1)} %bitcast.16, ...), custom_call_target="tpu_custom_call" | custom-call | tf_op jit(solution)/shard_map/backward/pallas_call | solution.py:3181
  455.5 0.0 copy-start.4
  455.5 0.0 copy-start.5
  455.5 2.1 convert_add_fusion.3
  457.6 0.0 copy-start.3
  457.6 3.2 convert_add_fusion.2
  460.9 0.0 copy-done.4
  460.9 0.0 copy-done.5
  460.9 0.0 copy-done.3
  460.9 0.0 copy-start
  460.9 0.0 copy-start.1
  460.9 1.7 convert_add_fusion.1
  462.6 0.0 copy-done.2
  462.6 0.5 copy-done
  463.1 0.7 copy-done.1
  463.9 3.2 convert_add_fusion
  467.1 0.0 copy-done.6
  467.1 0.8 copy.20
  467.9 0.0 copy-done.7
  467.9 0.8 copy.21
  468.7 0.0 copy-done.8
  468.7 0.6 copy.22
  (4 shorter events, 0.0 us)
Async XLA Ops:
  455.5 5.4 %copy-start.4 = (bf16[2048,256]{1,0:T(8,128)(2,1)S(1)}, bf16[2048,256]{1,0:T(8,128)(2,1)}, u32[]{:S(2)}) copy-start(bf16[2048,256]{1,0:T(8,128)(2,1)} %get-tuple-element.88) | copy-start | bytes 3145732
  455.5 5.4 %copy-start.5 = (bf16[2048,256]{1,0:T(8,128)(2,1)S(1)}, bf16[2048,256]{1,0:T(8,128)(2,1)}, u32[]{:S(2)}) copy-start(bf16[2048,256]{1,0:T(8,128)(2,1)} %get-tuple-element.89) | copy-start | bytes 3145732
  457.6 3.2 copy-start.3
  457.6 4.9 %copy-start.2 = (bf16[2,256,2048]{2,1,0:T(8,128)(2,1)S(1)}, bf16[2,256,2048]{2,1,0:T(8,128)(2,1)}, u32[]{:S(2)}) copy-start(bf16[2,256,2048]{2,1,0:T(8,128)(2,1)} %get-tuple-element.86) | copy-start | bytes 6291460
  460.9 2.2 copy-start
  460.9 3.0 copy-start.1
  463.9 3.2 copy-start.6
  463.9 4.0 copy-start.7
  467.1 1.6 copy-start.8

commit v7 on v6

--- a/solution.py
+++ b/solution.py
@@ -434,8 +434,6 @@
         copies = [
             self.copy(piece, 0, blocks.at[bd, lo], self.got.at[piece, lo], self.xn),
             self.copy(piece, 1, blocks.at[bd, hi], self.got.at[piece, hi], self.yn),
-            self.copy(piece, 2, blocks.at[bx, lo], self.place(out_x, piece, 0), self.xn),
-            self.copy(piece, 3, blocks.at[by, hi], self.place(out_y, piece, 1), self.yn),
         ]
         for copy in copies:
             copy.start()
@@ -462,6 +460,13 @@
         blocks = self.ring.at[slot]
         own_out, out_x, out_y = self.outs
         bx, by, bd = c ^ 1, c ^ 2, c ^ 3
+        whole = [
+            self.copy(piece, 2, blocks.at[bx, lo], self.place(out_x, piece, 0), self.xn),
+            self.copy(piece, 3, blocks.at[by, hi], self.place(out_y, piece, 1), self.yn),
+        ]
+        for copy in whole:
+            copy.start()
+        self.open[piece][0].extend(whole)
         self.copy(piece, 0, blocks.at[bd, lo], self.got.at[piece, lo], self.xn).wait_recv()
         self.add(slot, by, 0, piece)
         first = self.copy(piece, 4, blocks.at[by, lo], self.place(out_y, piece, 0), self.yn)

time: 475 us -> 473 us (level)
  no operation moved by 1% of the time
where the time goes in v7:
time: 473 us; the launch traced here: 466 us
  Pallas kernels  451 us (95%)
  other arithmetic  10.2 us (2%)
    pallas_call x1, Pallas kernels, backward(): pl.pallas_call(functools.partial(backward_kernel, n, names), out_shape=li...  188 us
    pallas_call x1, Pallas kernels, forward(): pl.pallas_call(functools.partial(forward_kernel, n, names), out_shape=[sh...  185 us
    pallas_call x1, Pallas kernels, mlp_out(): pl.pallas_call(functools.partial(mlp_out_kernel, n), out_shape=(shape((ro...  77.8 us
    add x4, other arithmetic, total(): return parts[0].astype(F32) + parts[1].astype(F32) + parts[2].astype(F32)  10.2 us

profile of v7, /device:TPU:0, one launch (start us, length us, event | category | flops | bytes accessed | tf_op | source)
XLA Modules:
  0.0 465.7 jit_solution(10018001960936535714)
XLA Ops:
  0.6 185.4 %forward.1 = (bf16[512,2048]{1,0:T(8,128)(2,1)}, bf16[3,2048,512]{2,1,0:T(8,128)(2,1)}, bf16[8,512,256]{2,1,0:T(8,128)(2,1)}, bf16[8,128,2048]{2,1,0:T(8,128)(2,...) custom-call(bf16[128,2048]{1,0:T(8,128)(2,1)} %bitcast.28, ...), custom_call_target="tpu_custom_call" | custom-call | tf_op jit(solution)/shard_map/forward/pallas_call | solution.py:1661
  186.0 77.8 %mlp_out.1 = (bf16[128,2048]{1,0:T(8,128)(2,1)}, bf16[4,128,2048]{2,1,0:T(8,128)(2,1)}, bf16[2,4,128,2048]{3,2,1,0:T(8,128)(2,1)}, f32[1,2048]{1,0:T(1,128)}, bf...) custom-call(bf16[4,128,2048]{2,1,0:T(8,128)(2,1)} %get-tuple-element, ...), custom_call_target="tpu_custom_call" | custom-call | tf_op jit(solution)/shard_map/mlp_out/pallas_call | solution.py:2027
  263.8 187.7 %backward.1 = (bf16[128,2048]{1,0:T(8,128)(2,1)}, f32[4,256]{1,0:T(4,128)}, bf16[2048,256]{1,0:T(8,128)(2,1)}, bf16[2048,256]{1,0:T(8,128)(2,1)}, bf16[2048,256]...) custom-call(bf16[2,512,2048]{2,1,0:T(8,128)(2,1)} %bitcast.16, ...), custom_call_target="tpu_custom_call" | custom-call | tf_op jit(solution)/shard_map/backward/pallas_call | solution.py:3186
  451.5 0.0 copy-start.4
  451.5 0.0 copy-start.5
  451.5 2.1 convert_add_fusion.3
  453.6 0.0 copy-start.3
  453.6 3.2 convert_add_fusion.2
  456.8 0.0 copy-done.4
  456.8 0.0 copy-done.5
  456.8 0.0 copy-done.3
  456.9 0.0 copy-start
  456.9 0.0 copy-start.1
  456.9 1.7 convert_add_fusion.1
  458.5 0.0 copy-done.2
  458.5 0.5 copy-done
  459.1 0.7 copy-done.1
  459.8 3.2 convert_add_fusion
  463.1 0.0 copy-done.6
  463.1 0.8 copy.20
  463.9 0.0 copy-done.7
  463.9 0.8 copy.21
  464.7 0.0 copy-done.8
  464.7 0.6 copy.22
  (4 shorter events, 0.0 us)
Async XLA Ops:
  451.5 5.4 %copy-start.4 = (bf16[2048,256]{1,0:T(8,128)(2,1)S(1)}, bf16[2048,256]{1,0:T(8,128)(2,1)}, u32[]{:S(2)}) copy-start(bf16[2048,256]{1,0:T(8,128)(2,1)} %get-tuple-element.88) | copy-start | bytes 3145732
  451.5 5.4 %copy-start.5 = (bf16[2048,256]{1,0:T(8,128)(2,1)S(1)}, bf16[2048,256]{1,0:T(8,128)(2,1)}, u32[]{:S(2)}) copy-start(bf16[2048,256]{1,0:T(8,128)(2,1)} %get-tuple-element.89) | copy-start | bytes 3145732
  453.6 3.2 copy-start.3
  453.6 4.9 %copy-start.2 = (bf16[2,256,2048]{2,1,0:T(8,128)(2,1)S(1)}, bf16[2,256,2048]{2,1,0:T(8,128)(2,1)}, u32[]{:S(2)}) copy-start(bf16[2,256,2048]{2,1,0:T(8,128)(2,1)} %get-tuple-element.86) | copy-start | bytes 6291460
  456.9 2.2 copy-start
  456.9 3.0 copy-start.1
  459.8 3.2 copy-start.6
  459.8 4.0 copy-start.7
  463.1 1.6 copy-start.8
